TPU v7x, 256 devices: a whole 4x4x8 slice. The times are simulated.
256 devices in a mesh: outer: 32 (over x_lo, z, core), inner: 8 (over y, x_hi).
Axes of the slice: x: 4 (x_hi: 2, x_lo: 2; x = x_hi * 2 + x_lo), y: 4, z: 8, core: 2. Of those that a mesh axis runs over, the one named last changes fastest.
Arguments:
- query_rows: bfloat16 [65536, 1024], P(('outer', 'inner')), may hold values from -6 to 6
- key_rows: bfloat16 [65536, 1024], P(('outer', 'inner')), may hold values from -6 to 6
- value_rows: bfloat16 [65536, 1024], P(('outer', 'inner')), may hold values from -6 to 6
- layer_output: bfloat16 [65536, 1024], P(('outer', 'inner')), may hold values from -1.5 to 1.5
- output_grad: bfloat16 [65536, 1024], P(('outer', 'inner')), may hold values from -192 to 192
- log_norms: float32 [16, 65536], P(None, ('outer', 'inner')), as said below
Outputs:
- query_grad: bfloat16 [65536, 1024], P(('outer', 'inner'))
- key_grad: bfloat16 [65536, 1024], P(('outer', 'inner'))
- value_grad: bfloat16 [65536, 1024], P(('outer', 'inner'))
Inputs may be any that keep to these rules, and one draw needn't show every extreme that they name: `log_norms`: every entry lies within 1 of log(1280) + 0.5.
All inputs are finite; a program needn't handle non-finite values.
Results may differ from a plain program's by a relative error of at most 0.0057.
Values may be sent and summed in bfloat16 or wider, within the bound.
No kernel may reach another device: no remote copies, remote signals or barrier semaphores. Data moves between devices by JAX's collectives and lax.ppermute only.
A program may use at most 128 MiB of HBM per device.

v0:
```python
import math

import jax
import jax.numpy as jnp
from jax import lax
from jax.sharding import PartitionSpec as P

REACH = 2


def shifted(shard, axis, by):
    devices = lax.axis_size(axis)
    return lax.ppermute(shard, axis, [(i, (i + by) % devices) for i in range(devices)])


def as_sent(shard):

    def short(part):
        return part.astype(jnp.bfloat16) if part.dtype == jnp.float32 else part

    return jax.tree.map(short, shard)


def tile_terms(
    query_block, key_block, value_block, grad_block, norm_block, delta_block, present, scale
):
    row_count = query_block.shape[0]
    head_count = norm_block.shape[0]
    model_width = query_block.shape[1]
    head_size = model_width // head_count
    group_size = math.gcd(head_count, 4)
    group_count = head_count // group_size

    def split_heads(matrix):
        return matrix.reshape(row_count, group_count, group_size, head_size).transpose(1, 0, 2, 3)

    def join_heads(stacked):
        return stacked.transpose(1, 0, 2, 3).reshape(row_count, model_width)

    def one_group(items):
        query_part, key_part, value_part, grad_part, norm_part, delta_part = items
        scores = (
            jnp.einsum("qhe,khe->hqk", query_part, key_part, preferred_element_type=jnp.float32)
            * scale
        )
        probs = jnp.exp(scores - norm_part[:, :, None]) * present
        grad_prob = jnp.einsum(
            "qhe,khe->hqk", grad_part, value_part, preferred_element_type=jnp.float32
        )
        grad_score = (probs * (grad_prob - delta_part[:, :, None])).astype(jnp.bfloat16)
        results = []
        results.append(
            jnp.einsum("hqk,khe->qhe", grad_score, key_part, preferred_element_type=jnp.float32)
        )
        weights = probs.astype(jnp.bfloat16)
        results.append(
            jnp.einsum("hqk,qhe->khe", grad_score, query_part, preferred_element_type=jnp.float32)
        )
        results.append(
            jnp.einsum("hqk,qhe->khe", weights, grad_part, preferred_element_type=jnp.float32)
        )
        return tuple(results)

    stacked = lax.map(
        one_group,
        (
            split_heads(query_block),
            split_heads(key_block),
            split_heads(value_block),
            split_heads(grad_block),
            norm_block.reshape(group_count, group_size, row_count),
            delta_block.reshape(group_count, group_size, row_count),
        ),
    )
    joined = [join_heads(item) for item in stacked]
    grad_query = joined.pop(0)
    grad_key = joined[0]
    grad_value = joined[1]
    return (grad_query, grad_key, grad_value)


def per_device(query_rows, key_rows, value_rows, layer_output, output_grad, log_norms):
    row_count, model_width = query_rows.shape
    head_count = log_norms.shape[0]
    head_size = model_width // head_count
    scale = head_size ** (-0.5)
    flat_index = lax.axis_index("outer") * lax.axis_size("inner") + lax.axis_index("inner")
    device_count = lax.axis_size("outer") * lax.axis_size("inner")
    products = layer_output.astype(jnp.float32) * output_grad.astype(jnp.float32)
    row_delta = products.reshape(row_count, head_count, head_size).sum(-1).T
    zero_rows = jnp.zeros((row_count, model_width), jnp.float32)
    visits = 2 * REACH + 1
    moving_keys, moving_values = shifted((key_rows, value_rows), ("outer", "inner"), REACH)
    query_acc = zero_rows
    key_acc, value_acc = (zero_rows, zero_rows)
    for visit in range(visits):
        block_index = flat_index - REACH + visit
        present = ((block_index >= 0) & (block_index < device_count)).astype(jnp.float32)
        grad_query, grad_key, grad_value = tile_terms(
            query_rows,
            moving_keys,
            moving_values,
            output_grad,
            log_norms,
            row_delta,
            present,
            scale,
        )
        query_acc = query_acc + grad_query
        key_acc = key_acc + grad_key
        value_acc = value_acc + grad_value
        if visit + 1 < visits:
            moving_keys, moving_values = shifted(
                (moving_keys, moving_values), ("outer", "inner"), -1
            )
            key_acc, value_acc = shifted((key_acc, value_acc), ("outer", "inner"), -1)
    key_acc, value_acc = (
        shifted(as_sent(key_acc), ("outer", "inner"), REACH).astype(key_acc.dtype),
        shifted(as_sent(value_acc), ("outer", "inner"), REACH).astype(value_acc.dtype),
    )
    query_grad = (query_acc * scale).astype(jnp.bfloat16)
    key_grad = (key_acc * scale).astype(jnp.bfloat16)
    value_grad = value_acc.astype(jnp.bfloat16)
    return (query_grad, key_grad, value_grad)


def solution(mesh):
    placed = (
        P(("outer", "inner"), None),
        P(("outer", "inner"), None),
        P(("outer", "inner"), None),
        P(("outer", "inner"), None),
        P(("outer", "inner"), None),
        P(None, ("outer", "inner")),
    )
    return jax.shard_map(
        per_device,
        mesh=mesh,
        in_specs=placed,
        out_specs=(
            P(("outer", "inner"), None),
            P(("outer", "inner"), None),
            P(("outer", "inner"), None),
        ),
        check_vma=False,
    )
```

profile of v0, /device:TPU:24, one launch (start us, length us, event | category | flops | bytes accessed | tf_op | source)
XLA Modules:
  0.0 321.6 jit_solution(7736001397597507030)
XLA Ops:
  1.7 1.3 copy.34
  5.0 10.9 %collective-permute-done = bf16[256,1024]{1,0:T(8,128)(2,1)} collective-permute-done((bf16[256,1024]{1,0:T(8,128)(2,1)}, bf16[256,1024]{1,0:T(8,128)(2,1)}, u32[]{:S(2)}, u32[]{:S(2)}) %collective-permute-start) | collective-permute-done | bytes 524320 | tf_op jit(solution)/shard_map/ppermute | solution.py:13
  15.8 3.2 collective-permute-start.2
  19.0 1.3 copy.32
  20.3 5.6 %collective-permute-done.1 = bf16[256,1024]{1,0:T(8,128)(2,1)} collective-permute-done((bf16[256,1024]{1,0:T(8,128)(2,1)}, bf16[256,1024]{1,0:T(8,128)(2,1)}, u32[]{:S(2)}, u32[]{:S(2)}) %collective-permute-start.1) | collective-permute-done | bytes 524320 | tf_op jit(solution)/shard_map/ppermute | solution.py:13
  25.9 3.2 collective-permute-start.3
  29.1 1.3 copy.35
  30.4 1.1 broadcast.21.clone.10
  31.5 1.1 broadcast.21.clone.11
  32.7 11.6 %while.70 = (s32[]{:T(128)}, f32[4,256,4,64]{1,3,2,0:T(8,128)S(1)}, f32[4,256,4,64]{1,3,2,0:T(8,128)}, f32[4,256,4,64]{1,3,2,0:T(8,128)}, bf16[4,256,4,64]{1,3,2...) while((s32[]{:T(128)}, f32[4,256,4,64]{1,3,2,0:T(8,128)S(1)}, ...), condition=%wide.region_2.3_spmd, body=%wide.region_1.2_spmd.sunk | while | flops 169607168 | bytes 6452857 | solution.py:64
  44.8 2.9 collective-permute-start.10
  47.7 1.2 copy.38
  49.0 1.2 copy.39
  50.2 1.1 broadcast.21.clone.12
  51.4 1.1 broadcast.21.clone.14
  52.6 11.6 %while.71 = (s32[]{:T(128)}, f32[4,256,4,64]{1,3,2,0:T(8,128)}, f32[4,256,4,64]{1,3,2,0:T(8,128)S(1)}, f32[4,256,4,64]{1,3,2,0:T(8,128)}, bf16[4,256,4,64]{1,3,2...) while((s32[]{:T(128)}, f32[4,256,4,64]{1,3,2,0:T(8,128)}, ...), condition=%wide.region_4.5_spmd, body=%wide.region_3.4_spmd.sunk | while | flops 169607168 | bytes 6452857 | solution.py:64
  62.3 1.0 fusion.254
  64.7 2.0 collective-permute-start.5
  66.7 5.5 %collective-permute-done.15 = f32[256,1024]{0,1:T(8,128)} collective-permute-done((f32[256,1024]{0,1:T(8,128)}, f32[256,1024]{0,1:T(8,128)}, u32[]{:S(2)}, u32[]{:S(2)}) %collective-permute-start.15) | collective-permute-done | bytes 1048608 | tf_op jit(solution)/shard_map/ppermute | solution.py:13
  72.2 2.6 bitcast_add_fusion.3
  74.8 1.4 collective-permute-start.16
  76.3 18.4 %collective-permute-done.10 = f32[256,1024]{0,1:T(8,128)} collective-permute-done((f32[256,1024]{0,1:T(8,128)}, f32[256,1024]{0,1:T(8,128)}, u32[]{:S(2)}, u32[]{:S(2)}) %collective-permute-start.10) | collective-permute-done | bytes 1048608 | tf_op jit(solution)/shard_map/ppermute | solution.py:13
  94.7 2.3 bitcast_add_fusion.7
  97.0 1.4 collective-permute-start.11
  98.4 7.5 %collective-permute-done.4 = bf16[256,1024]{1,0:T(8,128)(2,1)} collective-permute-done((bf16[256,1024]{1,0:T(8,128)(2,1)}, bf16[256,1024]{1,0:T(8,128)(2,1)}, u32[]{:S(2)}, u32[]{:S(2)}) %collective-permute-start.4) | collective-permute-done | bytes 524320 | tf_op jit(solution)/shard_map/ppermute | solution.py:13
  105.9 1.2 copy.40
  107.2 1.5 collective-permute-start.6
  108.6 8.5 %collective-permute-done.5 = bf16[256,1024]{1,0:T(8,128)(2,1)} collective-permute-done((bf16[256,1024]{1,0:T(8,128)(2,1)}, bf16[256,1024]{1,0:T(8,128)(2,1)}, u32[]{:S(2)}, u32[]{:S(2)}) %collective-permute-start.5) | collective-permute-done | bytes 524320 | tf_op jit(solution)/shard_map/ppermute | solution.py:13
  117.1 1.2 copy.41
  118.4 1.5 collective-permute-start.7
  119.9 1.1 broadcast.21.clone.6
  121.1 1.1 broadcast.21.clone.8
  122.2 11.6 %while.72 = (s32[]{:T(128)}, f32[4,256,4,64]{1,3,2,0:T(8,128)}, f32[4,256,4,64]{1,3,2,0:T(8,128)S(1)}, f32[4,256,4,64]{1,3,2,0:T(8,128)}, bf16[4,256,4,64]{1,3,2...) while((s32[]{:T(128)}, f32[4,256,4,64]{1,3,2,0:T(8,128)}, ...), condition=%wide.region_6.7_spmd, body=%wide.region_5.6_spmd.sunk | while | flops 169607168 | bytes 6452857 | solution.py:64
  133.7 48.4 %collective-permute-done.6 = bf16[256,1024]{1,0:T(8,128)(2,1)} collective-permute-done((bf16[256,1024]{1,0:T(8,128)(2,1)}, bf16[256,1024]{1,0:T(8,128)(2,1)}, u32[]{:S(2)}, u32[]{:S(2)}) %collective-permute-start.6) | collective-permute-done | bytes 524320 | tf_op jit(solution)/shard_map/ppermute | solution.py:13
  182.1 1.2 copy.42
  183.4 9.9 %collective-permute-done.7 = bf16[256,1024]{1,0:T(8,128)(2,1)} collective-permute-done((bf16[256,1024]{1,0:T(8,128)(2,1)}, bf16[256,1024]{1,0:T(8,128)(2,1)}, u32[]{:S(2)}, u32[]{:S(2)}) %collective-permute-start.7) | collective-permute-done | bytes 524320 | tf_op jit(solution)/shard_map/ppermute | solution.py:13
  193.3 1.2 copy.43
  194.7 2.6 bitcast_add_fusion.2
  197.3 2.3 bitcast_add_fusion.6
  199.7 1.1 broadcast.21.clone.3
  200.9 1.1 broadcast.21.clone.5
  202.0 11.6 %while.73 = (s32[]{:T(128)}, f32[4,256,4,64]{1,3,2,0:T(8,128)}, f32[4,256,4,64]{1,3,2,0:T(8,128)S(1)}, f32[4,256,4,64]{1,3,2,0:T(8,128)}, bf16[4,256,4,64]{1,3,2...) while((s32[]{:T(128)}, f32[4,256,4,64]{1,3,2,0:T(8,128)}, ...), condition=%wide.region_8.9_spmd, body=%wide.region_7.8_spmd.sunk | while | flops 169607168 | bytes 6452857 | solution.py:64
  202.9 1.0 fusion.284
  205.9 1.0 fusion.284
  213.6 1.2 copy.44
  214.8 17.7 %collective-permute-done.9 = bf16[256,1024]{1,0:T(8,128)(2,1)} collective-permute-done((bf16[256,1024]{1,0:T(8,128)(2,1)}, bf16[256,1024]{1,0:T(8,128)(2,1)}, u32[]{:S(2)}, u32[]{:S(2)}) %collective-permute-start.9) | collective-permute-done | bytes 524320 | tf_op jit(solution)/shard_map/ppermute | solution.py:13
  232.5 1.2 copy.45
  233.8 21.2 %collective-permute-done.17 = f32[256,1024]{0,1:T(8,128)} collective-permute-done((f32[256,1024]{0,1:T(8,128)}, f32[256,1024]{0,1:T(8,128)}, u32[]{:S(2)}, u32[]{:S(2)}) %collective-permute-start.17) | collective-permute-done | bytes 1048608 | tf_op jit(solution)/shard_map/ppermute | solution.py:13
  255.0 2.6 bitcast_add_fusion.1
  257.6 15.9 %collective-permute-done.12 = f32[256,1024]{0,1:T(8,128)} collective-permute-done((f32[256,1024]{0,1:T(8,128)}, f32[256,1024]{0,1:T(8,128)}, u32[]{:S(2)}, u32[]{:S(2)}) %collective-permute-start.12) | collective-permute-done | bytes 1048608 | tf_op jit(solution)/shard_map/ppermute | solution.py:13
  273.6 2.3 bitcast_add_fusion.5
  275.9 1.1 broadcast.21.clone
  277.1 1.2 broadcast.21.clone.2
  278.3 11.7 %while.74 = (s32[]{:T(128)}, f32[4,256,4,64]{1,3,2,0:T(8,128)}, f32[4,256,4,64]{1,3,2,0:T(8,128)S(1)}, f32[4,256,4,64]{1,3,2,0:T(8,128)}, bf16[4,256,4,64]{1,3,2...) while((s32[]{:T(128)}, f32[4,256,4,64]{1,3,2,0:T(8,128)}, ...), condition=%wide.region_10.11_spmd, body=%wide.region_9.10_spmd.sunk | while | flops 169607168 | bytes 6452857 | solution.py:64
  282.1 1.0 fusion.299
  285.1 1.0 fusion.299
  289.9 11.7 %collective-permute-done.13 = f32[256,1024]{0,1:T(8,128)} collective-permute-done((f32[256,1024]{0,1:T(8,128)}, f32[256,1024]{0,1:T(8,128)}, u32[]{:S(2)}, u32[]{:S(2)}) %collective-permute-start.13) | collective-permute-done | bytes 1048608 | tf_op jit(solution)/shard_map/ppermute | solution.py:13
  301.7 1.5 fusion.141
  303.3 1.8 fusion.140
  306.2 1.0 copy.46
  307.2 6.7 %collective-permute-done.14 = bf16[256,1024]{0,1:T(8,128)(2,1)S(1)} collective-permute-done((bf16[256,1024]{0,1:T(8,128)(2,1)S(1)}, bf16[256,1024]{0,1:T(8,128)(2,1)S(1)}, u32[]{:S(2)}, u32[]{:S(2)}) %collective-permute-start.14) | collective-permute-done | bytes 524320 | tf_op jit(solution)/shard_map/ppermute | solution.py:13
  314.0 1.0 copy.47
  315.0 4.5 %collective-permute-done.19 = bf16[256,1024]{0,1:T(8,128)(2,1)} collective-permute-done((bf16[256,1024]{0,1:T(8,128)(2,1)S(1)}, bf16[256,1024]{0,1:T(8,128)(2,1)}, u32[]{:S(2)}, u32[]{:S(2)}) %collective-permute-start.19) | collective-permute-done | bytes 524320 | tf_op jit(solution)/shard_map/ppermute | solution.py:13
  319.5 2.0 copy.48
  (163 shorter events, 58.5 us)
Async XLA Ops:
  0.6 15.2 %collective-permute-start = (bf16[256,1024]{1,0:T(8,128)(2,1)}, bf16[256,1024]{1,0:T(8,128)(2,1)}, u32[]{:S(2)}, u32[]{:S(2)}) collective-permute-start(bf16[256,1024]{1,0:T(8,128)(2,1)} %param.17), channel_id=1, source_target_pairs={{0,2},{1,3},{2,4},{3,5},{4,6},{5,7},{6,8},{7,9},{8,10},{9,11},{10,... | collective-permute-start | bytes 1572872 | tf_op jit(solution)/shard_map/ppermute | solution.py:13
  0.7 25.2 %collective-permute-start.1 = (bf16[256,1024]{1,0:T(8,128)(2,1)}, bf16[256,1024]{1,0:T(8,128)(2,1)}, u32[]{:S(2)}, u32[]{:S(2)}) collective-permute-start(bf16[256,1024]{1,0:T(8,128)(2,1)} %param.18), channel_id=1, source_target_pairs={{0,2},{1,3},{2,4},{3,5},{4,6},{5,7},{6,8},{7,9},{8,10},{9,11},{10,... | collective-permute-start | bytes 1572872 | tf_op jit(solution)/shard_map/ppermute | solution.py:13
  1.7 1.3 copy-start.6
  3.2 1.0 copy-start.7
  4.2 0.7 copy-start.8
  15.8 31.9 %collective-permute-start.2 = (bf16[256,1024]{1,0:T(8,128)(2,1)}, bf16[256,1024]{1,0:T(8,128)(2,1)}, u32[]{:S(2)}, u32[]{:S(2)}) collective-permute-start(bf16[256,1024]{1,0:T(8,128)(2,1)} %collective-permute-done), channel_id=1, source_target_pairs={{0,255},{1,0},{2,1},{3,2},{4,3},{5,4},{6,5},{7,6},{8,7},{9,8},{10,... | collective-permute-start | bytes 1572872 | tf_op jit(solution)/shard_map/ppermute | solution.py:13
  25.9 23.0 %collective-permute-start.3 = (bf16[256,1024]{1,0:T(8,128)(2,1)}, bf16[256,1024]{1,0:T(8,128)(2,1)}, u32[]{:S(2)}, u32[]{:S(2)}) collective-permute-start(bf16[256,1024]{1,0:T(8,128)(2,1)} %collective-permute-done.1), channel_id=1, source_target_pairs={{0,255},{1,0},{2,1},{3,2},{4,3},{5,4},{6,5},{7,6},{8,7},{9,8},{10,... | collective-permute-start | bytes 1572872 | tf_op jit(solution)/shard_map/ppermute | solution.py:13
  44.3 3.4 %copy-start.1 = (f32[4,256,4,64]{1,3,2,0:T(8,128)}, f32[4,256,4,64]{1,3,2,0:T(8,128)S(1)}, u32[]{:S(2)}) copy-start(f32[4,256,4,64]{1,3,2,0:T(8,128)S(1)} %get-tuple-element.298) | copy-start | bytes 3145732
  44.3 27.9 %collective-permute-start.15 = (f32[256,1024]{0,1:T(8,128)}, f32[256,1024]{0,1:T(8,128)}, u32[]{:S(2)}, u32[]{:S(2)}) collective-permute-start(f32[256,1024]{0,1:T(8,128)} %bitcast.101), channel_id=1, source_target_pairs={{0,255},{1,0},{2,1},{3,2},{4,3},{5,4},{6,5},{7,6},{8,7},{9,8},{10,... | collective-permute-start | bytes 3145736 | tf_op jit(solution)/shard_map/ppermute | solution.py:13
  44.8 49.9 %collective-permute-start.10 = (f32[256,1024]{0,1:T(8,128)}, f32[256,1024]{0,1:T(8,128)}, u32[]{:S(2)}, u32[]{:S(2)}) collective-permute-start(f32[256,1024]{0,1:T(8,128)} %bitcast.437), channel_id=1, source_target_pairs={{0,255},{1,0},{2,1},{3,2},{4,3},{5,4},{6,5},{7,6},{8,7},{9,8},{10,... | collective-permute-start | bytes 3145736 | tf_op jit(solution)/shard_map/ppermute | solution.py:13
  64.2 41.7 %collective-permute-start.4 = (bf16[256,1024]{1,0:T(8,128)(2,1)}, bf16[256,1024]{1,0:T(8,128)(2,1)}, u32[]{:S(2)}, u32[]{:S(2)}) collective-permute-start(bf16[256,1024]{1,0:T(8,128)(2,1)} %collective-permute-done.2), channel_id=1, source_target_pairs={{0,255},{1,0},{2,1},{3,2},{4,3},{5,4},{6,5},{7,6},{8,7},{9,8},{10,... | collective-permute-start | bytes 1572872 | tf_op jit(solution)/shard_map/ppermute | solution.py:13
  64.7 52.4 %collective-permute-start.5 = (bf16[256,1024]{1,0:T(8,128)(2,1)}, bf16[256,1024]{1,0:T(8,128)(2,1)}, u32[]{:S(2)}, u32[]{:S(2)}) collective-permute-start(bf16[256,1024]{1,0:T(8,128)(2,1)} %collective-permute-done.3), channel_id=1, source_target_pairs={{0,255},{1,0},{2,1},{3,2},{4,3},{5,4},{6,5},{7,6},{8,7},{9,8},{10,... | collective-permute-start | bytes 1572872 | tf_op jit(solution)/shard_map/ppermute | solution.py:13
  74.8 119.8 %collective-permute-start.16 = (f32[256,1024]{0,1:T(8,128)}, f32[256,1024]{0,1:T(8,128)}, u32[]{:S(2)}, u32[]{:S(2)}) collective-permute-start(f32[256,1024]{0,1:T(8,128)} %bitcast_add_fusion.3), channel_id=1, source_target_pairs={{0,255},{1,0},{2,1},{3,2},{4,3},{5,4},{6,5},{7,6},{8,7},{9,8},{10,... | collective-permute-start | bytes 3145736 | tf_op jit(solution)/shard_map/ppermute | solution.py:13
  97.0 100.4 %collective-permute-start.11 = (f32[256,1024]{0,1:T(8,128)}, f32[256,1024]{0,1:T(8,128)}, u32[]{:S(2)}, u32[]{:S(2)}) collective-permute-start(f32[256,1024]{0,1:T(8,128)} %bitcast_add_fusion.7), channel_id=1, source_target_pairs={{0,255},{1,0},{2,1},{3,2},{4,3},{5,4},{6,5},{7,6},{8,7},{9,8},{10,... | collective-permute-start | bytes 3145736 | tf_op jit(solution)/shard_map/ppermute | solution.py:13
  107.2 75.0 %collective-permute-start.6 = (bf16[256,1024]{1,0:T(8,128)(2,1)}, bf16[256,1024]{1,0:T(8,128)(2,1)}, u32[]{:S(2)}, u32[]{:S(2)}) collective-permute-start(bf16[256,1024]{1,0:T(8,128)(2,1)} %collective-permute-done.4), channel_id=1, source_target_pairs={{0,255},{1,0},{2,1},{3,2},{4,3},{5,4},{6,5},{7,6},{8,7},{9,8},{10,... | collective-permute-start | bytes 1572872 | tf_op jit(solution)/shard_map/ppermute | solution.py:13
  118.4 75.0 %collective-permute-start.7 = (bf16[256,1024]{1,0:T(8,128)(2,1)}, bf16[256,1024]{1,0:T(8,128)(2,1)}, u32[]{:S(2)}, u32[]{:S(2)}) collective-permute-start(bf16[256,1024]{1,0:T(8,128)(2,1)} %collective-permute-done.5), channel_id=1, source_target_pairs={{0,255},{1,0},{2,1},{3,2},{4,3},{5,4},{6,5},{7,6},{8,7},{9,8},{10,... | collective-permute-start | bytes 1572872 | tf_op jit(solution)/shard_map/ppermute | solution.py:13
  183.4 30.2 %collective-permute-start.8 = (bf16[256,1024]{1,0:T(8,128)(2,1)}, bf16[256,1024]{1,0:T(8,128)(2,1)}, u32[]{:S(2)}, u32[]{:S(2)}) collective-permute-start(bf16[256,1024]{1,0:T(8,128)(2,1)} %collective-permute-done.6), channel_id=1, source_target_pairs={{0,255},{1,0},{2,1},{3,2},{4,3},{5,4},{6,5},{7,6},{8,7},{9,8},{10,... | collective-permute-start | bytes 1572872 | tf_op jit(solution)/shard_map/ppermute | solution.py:13
  194.6 37.9 %collective-permute-start.9 = (bf16[256,1024]{1,0:T(8,128)(2,1)}, bf16[256,1024]{1,0:T(8,128)(2,1)}, u32[]{:S(2)}, u32[]{:S(2)}) collective-permute-start(bf16[256,1024]{1,0:T(8,128)(2,1)} %collective-permute-done.7), channel_id=1, source_target_pairs={{0,255},{1,0},{2,1},{3,2},{4,3},{5,4},{6,5},{7,6},{8,7},{9,8},{10,... | collective-permute-start | bytes 1572872 | tf_op jit(solution)/shard_map/ppermute | solution.py:13
  197.3 57.6 %collective-permute-start.17 = (f32[256,1024]{0,1:T(8,128)}, f32[256,1024]{0,1:T(8,128)}, u32[]{:S(2)}, u32[]{:S(2)}) collective-permute-start(f32[256,1024]{0,1:T(8,128)} %bitcast_add_fusion.2), channel_id=1, source_target_pairs={{0,255},{1,0},{2,1},{3,2},{4,3},{5,4},{6,5},{7,6},{8,7},{9,8},{10,... | collective-permute-start | bytes 3145736 | tf_op jit(solution)/shard_map/ppermute | solution.py:13
  199.7 73.9 %collective-permute-start.12 = (f32[256,1024]{0,1:T(8,128)}, f32[256,1024]{0,1:T(8,128)}, u32[]{:S(2)}, u32[]{:S(2)}) collective-permute-start(f32[256,1024]{0,1:T(8,128)} %bitcast_add_fusion.6), channel_id=1, source_target_pairs={{0,255},{1,0},{2,1},{3,2},{4,3},{5,4},{6,5},{7,6},{8,7},{9,8},{10,... | collective-permute-start | bytes 3145736 | tf_op jit(solution)/shard_map/ppermute | solution.py:13
  257.6 45.6 %collective-permute-start.18 = (f32[256,1024]{0,1:T(8,128)}, f32[256,1024]{0,1:T(8,128)}, u32[]{:S(2)}, u32[]{:S(2)}) collective-permute-start(f32[256,1024]{0,1:T(8,128)} %bitcast_add_fusion.1), channel_id=1, source_target_pairs={{0,255},{1,0},{2,1},{3,2},{4,3},{5,4},{6,5},{7,6},{8,7},{9,8},{10,... | collective-permute-start | bytes 3145736 | tf_op jit(solution)/shard_map/ppermute | solution.py:13
  275.9 25.8 %collective-permute-start.13 = (f32[256,1024]{0,1:T(8,128)}, f32[256,1024]{0,1:T(8,128)}, u32[]{:S(2)}, u32[]{:S(2)}) collective-permute-start(f32[256,1024]{0,1:T(8,128)} %bitcast_add_fusion.5), channel_id=1, source_target_pairs={{0,255},{1,0},{2,1},{3,2},{4,3},{5,4},{6,5},{7,6},{8,7},{9,8},{10,... | collective-permute-start | bytes 3145736 | tf_op jit(solution)/shard_map/ppermute | solution.py:13
  301.7 3.5 %copy-start.3 = (f32[4,256,4,64]{1,3,2,0:T(8,128)S(1)}, f32[4,256,4,64]{1,3,2,0:T(8,128)}, u32[]{:S(2)}) copy-start(f32[4,256,4,64]{1,3,2,0:T(8,128)} %get-tuple-element.299) | copy-start | bytes 3145732
  301.7 3.6 %copy-start.4 = (f32[4,256,4,64]{1,3,2,0:T(8,128)S(1)}, f32[4,256,4,64]{1,3,2,0:T(8,128)}, u32[]{:S(2)}) copy-start(f32[4,256,4,64]{1,3,2,0:T(8,128)} %get-tuple-element.300) | copy-start | bytes 3145732
  301.7 3.6 %copy-start.5 = (f32[4,256,4,64]{1,3,2,0:T(8,128)S(1)}, f32[4,256,4,64]{1,3,2,0:T(8,128)}, u32[]{:S(2)}) copy-start(f32[4,256,4,64]{1,3,2,0:T(8,128)} %get-tuple-element.301) | copy-start | bytes 3145732
  303.2 10.7 %collective-permute-start.14 = (bf16[256,1024]{0,1:T(8,128)(2,1)S(1)}, bf16[256,1024]{0,1:T(8,128)(2,1)S(1)}, u32[]{:S(2)}, u32[]{:S(2)}) collective-permute-start(bf16[256,1024]{0,1:T(8,128)(2,1)S(1)} %fusion.141), channel_id=1, source_target_pairs={{0,2},{1,3},{2,4},{3,5},{4,6},{5,7},{6,8},{7,9},{8,10},{9,11},{10,... | collective-permute-start | bytes 1572872 | tf_op jit(solution)/shard_map/ppermute | solution.py:13
  303.3 2.0 copy-start
  303.3 2.3 copy-start.2
  305.1 14.4 %collective-permute-start.19 = (bf16[256,1024]{0,1:T(8,128)(2,1)S(1)}, bf16[256,1024]{0,1:T(8,128)(2,1)}, u32[]{:S(2)}, u32[]{:S(2)}) collective-permute-start(bf16[256,1024]{0,1:T(8,128)(2,1)S(1)} %fusion.140), channel_id=1, source_target_pairs={{0,2},{1,3},{2,4},{3,5},{4,6},{5,7},{6,8},{7,9},{8,10},{9,11},{10,... | collective-permute-start | bytes 1572872 | tf_op jit(solution)/shard_map/ppermute | solution.py:13
where the time goes:
time: 327 us; the launch traced here: 322 us
  waiting for transfers between devices  192 us (59%)
  matrix products  57.6 us (18%)
  local copies, waits for them, and re-layouts  31.6 us (10%)
  starting transfers between devices  19.5 us (6%)
  other arithmetic  19.1 us (6%)
    ppermute x20, waiting for transfers between devices, shifted(): lax.ppermute(shard, axis, [(i, (i + by) % devices) for i in range(devices)])  192 us
    ppermute x20, starting transfers between devices, shifted(): lax.ppermute(shard, axis, [(i, (i + by) % devices) for i in range(devices)])  19.5 us
    dot_general x20, matrix products, one_group(): jnp.einsum('hqk,qhe->khe', weights, grad_part, preferred_element_type=jnp...  18.4 us
    dot_general x20, matrix products, one_group(): jnp.einsum('hqk,khe->qhe', grad_score, key_part, preferred_element_type=j...  17 us
    ppermute x10, local copies, waits for them, and re-layouts, shifted(): lax.ppermute(shard, axis, [(i, (i + by) % devices) for i in range(devices)])  12.5 us
    another operation x15, local copies, waits for them, and re-layouts  11.5 us
    dot_general x20, matrix products, one_group(): jnp.einsum('qhe,khe->hqk', query_part, key_part, preferred_element_type=j...  8.01 us
    add x3, other arithmetic, per_device(): value_acc = value_acc + grad_value  7.95 us
  transfers between devices with their start and end apart: 20, of which 14 were waited for; matrix products, arithmetic and copies ran while one was open for 32% of the time, Pallas kernels for 0%

commit v1 on v0

v1 whole, which is shorter than its diff:
```python
import functools

import jax
import jax.numpy as jnp
from jax import lax
from jax.experimental import pallas as pl
from jax.experimental.pallas import tpu as pltpu
from jax.sharding import PartitionSpec as P

AXES = ("outer", "inner")
LANES = 128
LOG2E = 1.4426950408889634
VMEM_LIMIT = 48 * 1024 * 1024


def params():
    return pltpu.CompilerParams(
        dimension_semantics=("arbitrary",), vmem_limit_bytes=VMEM_LIMIT
    )


def dot_nt(a, b):
    return lax.dot_general(a, b, (((1,), (1,)), ((), ())), preferred_element_type=jnp.float32)


def dot_nn(a, b):
    return lax.dot_general(a, b, (((1,), (0,)), ((), ())), preferred_element_type=jnp.float32)


def head_masks(dtype):
    lane = lax.broadcasted_iota(jnp.int32, (1, LANES), 1)
    first = jnp.where(lane < LANES // 2, 1.0, 0.0)
    return first.astype(dtype), (1.0 - first).astype(dtype)


def pack_kernel(x_ref, *refs):
    rows = refs[0].shape[0]
    norm_ref = refs[10]
    step = pl.program_id(0)
    for side in range(2):
        q, k, v, o, g = refs[5 * side : 5 * side + 5]
        msg, kv = refs[11 + 2 * side : 13 + 2 * side]
        half = x_ref[0] if side == 0 else 1 - x_ref[0]
        pair = half * pl.num_programs(0) + step
        grad = g[...]
        msg[0:rows] = q[...]
        msg[rows : 2 * rows] = grad
        kv[0:rows] = k[...]
        kv[rows : 2 * rows] = v[...]
        product = o[...].astype(jnp.float32) * grad.astype(jnp.float32)
        high = product.astype(jnp.bfloat16)
        low = (product - high.astype(jnp.float32)).astype(jnp.bfloat16)
        row = lax.broadcasted_iota(jnp.int32, (8, LANES), 0)
        lane = lax.broadcasted_iota(jnp.int32, (8, LANES), 1)
        pick = jnp.where(row == lane // (LANES // 2), 1.0, 0.0).astype(jnp.bfloat16)
        delta = dot_nt(pick, high) + dot_nt(pick, low)
        norms = [norm_ref[pl.ds(2 * pair + h, 1), :] for h in range(2)]
        terms = jnp.concatenate([*norms, delta[0:2]], axis=0)
        terms_high = terms.astype(jnp.bfloat16).astype(jnp.float32)
        both = jnp.concatenate([terms_high, terms - terms_high], axis=0)
        msg[2 * rows : 2 * rows + 16] = jnp.concatenate(
            [both[:, :LANES], both[:, LANES:]], axis=0
        ).astype(jnp.bfloat16)


def pack(x, q, k, v, o, g, norms):
    rows, width = q.shape
    pairs = width // LANES // 2
    own = pl.BlockSpec((rows, LANES), lambda i, x: (0, x[0] * pairs + i))
    other = pl.BlockSpec((rows, LANES), lambda i, x: (0, (1 - x[0]) * pairs + i))
    msg_spec = pl.BlockSpec((2 * rows + 16, LANES), lambda i, x: (0, i))
    kv_spec = pl.BlockSpec((2 * rows, LANES), lambda i, x: (0, i))
    msg = jax.ShapeDtypeStruct((2 * rows + 16, width // 2), jnp.bfloat16)
    kv = jax.ShapeDtypeStruct((2 * rows, width // 2), jnp.bfloat16)
    return pl.pallas_call(
        pack_kernel,
        grid_spec=pltpu.PrefetchScalarGridSpec(
            num_scalar_prefetch=1,
            grid=(pairs,),
            in_specs=[own] * 5
            + [other] * 5
            + [pl.BlockSpec(norms.shape, lambda i, x: (0, 0))],
            out_specs=[msg_spec, kv_spec, msg_spec, kv_spec],
        ),
        out_shape=[msg, kv, msg, kv],
        compiler_params=params(),
        name="pack",
    )(x, q, k, v, o, g, q, k, v, o, g, norms)


def tiles_kernel(*refs, keys, queries, pairs, dq_in, dkv_in, dq_out, scale):
    refs = list(refs)
    kv_refs = {u: refs.pop(0) for u in keys}
    msg_refs = {t: refs.pop(0) for t in queries}
    dq = {t: refs.pop(0)[...] for t in dq_in}
    dkv_refs = {u: refs.pop(0) for u in dkv_in}
    dq_refs = {t: refs.pop(0) for t in dq_out}
    dkv_out = {u: refs.pop(0) for u in keys}
    rows = next(iter(kv_refs.values())).shape[0] // 2
    masks = head_masks(jnp.bfloat16)
    loaded = {}
    for t in queries:
        msg = msg_refs[t]
        q, g = msg[0:rows], msg[rows : 2 * rows]
        info = msg[2 * rows : 2 * rows + 16].astype(jnp.float32)
        both = jnp.concatenate([info[0:8], info[8:16]], axis=1)
        terms = both[0:4] + both[4:8]
        loaded[t] = ([q * m for m in masks], [g * m for m in masks], terms[0:2] * LOG2E, terms[2:4])
    acc = {t: [None, None] for t in queries}
    for u in keys:
        k, v = kv_refs[u][0:rows], kv_refs[u][rows : 2 * rows]
        kt = k.T
        half = LANES // 2
        heads_t = [kt[0:half], kt[half:LANES]]
        dk = dkv_refs[u][0:rows] if u in dkv_refs else None
        dv = dkv_refs[u][rows : 2 * rows] if u in dkv_refs else None
        for t in queries:
            if (u, t) not in pairs:
                continue
            qs, gs, norms, deltas = loaded[t]
            for h in range(2):
                scores = dot_nt(k, qs[h])
                probs = jnp.exp2(scores * (scale * LOG2E) - norms[h : h + 1])
                grad_prob = dot_nt(v, gs[h])
                grad_score = (probs * (grad_prob - deltas[h : h + 1])).astype(jnp.bfloat16)
                weights = probs.astype(jnp.bfloat16)
                part = dot_nn(weights, gs[h])
                dv = part if dv is None else dv + part
                part = dot_nn(grad_score, qs[h])
                dk = part if dk is None else dk + part
                part = dot_nn(heads_t[h], grad_score)
                acc[t][h] = part if acc[t][h] is None else acc[t][h] + part
        final = dkv_out[u].dtype == jnp.bfloat16
        dkv_out[u][0:rows] = (dk * scale if final else dk).astype(dkv_out[u].dtype)
        dkv_out[u][rows : 2 * rows] = dv.astype(dkv_out[u].dtype)
    for t in queries:
        total = jnp.concatenate(acc[t], axis=0).T
        if t in dq:
            total = total + dq[t]
        final = dq_refs[t].dtype == jnp.bfloat16
        dq_refs[t][...] = (total * scale if final else total).astype(dq_refs[t].dtype)


def tiles(kvs, msgs, pairs, dq_in, dkv_in, dq_types, dkv_types, scale, name):
    first = next(iter(kvs.values()))
    rows, width = first.shape[0] // 2, first.shape[1]

    def spec(height):
        return pl.BlockSpec((height, LANES), lambda i: (0, i))

    operands = [*kvs.values(), *msgs.values(), *dq_in.values(), *dkv_in.values()]
    outs = [jax.ShapeDtypeStruct((rows, width), dq_types[t]) for t in msgs]
    outs += [jax.ShapeDtypeStruct((2 * rows, width), dkv_types[u]) for u in kvs]
    results = pl.pallas_call(
        functools.partial(
            tiles_kernel,
            keys=tuple(kvs),
            queries=tuple(msgs),
            pairs=frozenset(pairs),
            dq_in=tuple(dq_in),
            dkv_in=tuple(dkv_in),
            dq_out=tuple(msgs),
            scale=scale,
        ),
        grid=(width // LANES,),
        in_specs=[spec(a.shape[0]) for a in operands],
        out_specs=[spec(a.shape[0]) for a in outs],
        out_shape=outs,
        compiler_params=params(),
        name=name,
    )(*operands)
    count = len(msgs)
    return dict(zip(msgs, results[:count])), dict(zip(kvs, results[count:]))


def finish_kernel(x_ref, dq_own, ret_a, ret_b, dkv_own, dq_other, dkv_other, dq, dk, dv, *, scale):
    rows = dq.shape[0]
    own = pl.program_id(0) < pl.num_programs(0) // 2

    @pl.when(own)
    def _():
        total = dq_own[...] * scale + ret_a[...].astype(jnp.float32) + ret_b[...].astype(jnp.float32)
        dq[...] = total.astype(jnp.bfloat16)
        dk[...] = dkv_own[0:rows]
        dv[...] = dkv_own[rows : 2 * rows]

    @pl.when(jnp.logical_not(own))
    def _():
        dq[...] = dq_other[...]
        dk[...] = dkv_other[0:rows]
        dv[...] = dkv_other[rows : 2 * rows]


def finish(x, dq_own, ret_a, ret_b, dkv_own, dq_other, dkv_other, scale):
    rows, width = dq_own.shape
    pairs = width // LANES

    def own_spec(height):
        return pl.BlockSpec((height, LANES), lambda i, x: (0, jnp.minimum(i, pairs - 1)))

    def other_spec(height):
        return pl.BlockSpec((height, LANES), lambda i, x: (0, jnp.maximum(i - pairs, 0)))

    out = pl.BlockSpec((rows, LANES), lambda i, x: (0, (x[0] * pairs + i) % (2 * pairs)))
    return pl.pallas_call(
        functools.partial(finish_kernel, scale=scale),
        grid_spec=pltpu.PrefetchScalarGridSpec(
            num_scalar_prefetch=1,
            grid=(2 * pairs,),
            in_specs=[own_spec(rows)] * 3
            + [own_spec(2 * rows), other_spec(rows), other_spec(2 * rows)],
            out_specs=[out] * 3,
        ),
        out_shape=[jax.ShapeDtypeStruct((rows, 2 * width), jnp.bfloat16)] * 3,
        compiler_params=params(),
        name="finish",
    )(x, dq_own, ret_a, ret_b, dkv_own, dq_other, dkv_other)


def per_device(query_rows, key_rows, value_rows, layer_output, output_grad, log_norms):
    count = lax.axis_size("outer") * lax.axis_size("inner")
    index = lax.axis_index("outer") * lax.axis_size("inner") + lax.axis_index("inner")
    x = (index % 2).astype(jnp.int32).reshape(1)
    head_size = query_rows.shape[1] // log_norms.shape[0]
    scale = head_size ** (-0.5)

    swap = [(i, i ^ 1) for i in range(count)]
    step_a = [(i, i + 2 if i % 2 == 0 else i - 2) for i in range(count)]
    step_a = [(i, j) for i, j in step_a if 0 <= j < count]
    step_b = [(j, i) for i, j in step_a]

    def send(a, perm):
        return lax.ppermute(a, AXES, perm)

    own, kv_own, to_other, kv_to_other = pack(
        x, query_rows, key_rows, value_rows, layer_output, output_grad, log_norms
    )
    other = send(to_other, swap)
    near_a, near_b = send(own, step_a), send(own, step_b)
    kv_to_other, other = lax.optimization_barrier((kv_to_other, other))
    far_a, far_b = send(other, step_a), send(other, step_b)
    kv_other = send(kv_to_other, swap)

    f32, b16 = jnp.float32, jnp.bfloat16
    dq1, dkv1 = tiles(
        {"own": kv_own},
        {"own": own, "other": other, "near_a": near_a, "near_b": near_b},
        [("own", t) for t in ("own", "other", "near_a", "near_b")],
        {},
        {},
        {"own": f32, "other": f32, "near_a": b16, "near_b": f32},
        {"own": f32},
        scale,
        "tiles_near",
    )
    dq2, dkv2 = tiles(
        {"other": kv_other, "own": kv_own},
        {"own": own, "other": other, "near_b": near_b, "far_a": far_a, "far_b": far_b},
        [("other", t) for t in ("own", "other", "near_b", "far_a", "far_b")] + [("own", "far_a")],
        {t: dq1[t] for t in ("own", "other", "near_b")},
        {"own": dkv1["own"]},
        {"own": f32, "other": f32, "near_b": b16, "far_a": b16, "far_b": b16},
        {"other": b16, "own": b16},
        scale,
        "tiles_far",
    )
    back_far_a, back_far_b = send(dq2["far_a"], step_b), send(dq2["far_b"], step_a)
    dkv_other = send(dkv2["other"], swap)
    back_near_a, back_near_b = send(dq1["near_a"], step_b), send(dq2["near_b"], step_a)
    dq_other = (
        dq2["other"] * scale + back_far_a.astype(jnp.float32) + back_far_b.astype(jnp.float32)
    ).astype(jnp.bfloat16)
    dq_other = send(dq_other, swap)
    return tuple(
        finish(x, dq2["own"], back_near_a, back_near_b, dkv2["own"], dq_other, dkv_other, scale)
    )


def solution(mesh):
    rows = P(AXES, None)
    return jax.shard_map(
        per_device,
        mesh=mesh,
        in_specs=(rows, rows, rows, rows, rows, P(None, AXES)),
        out_specs=(rows, rows, rows),
        check_vma=False,
    )
```

time: 327 us -> 106 us (0.32); the launches traced: 322 us -> 105 us
  waiting for transfers between devices: 192 us -> 29.4 us
  matrix products: 57.6 us -> 0 us
  Pallas kernels: 0 us -> 30 us
  local copies, waits for them, and re-layouts: 31.6 us -> 7.89 us
  other arithmetic: 19.1 us -> 0.11 us
  starting transfers between devices: 19.5 us -> 36.4 us
    ppermute x20 -> x12, waiting for transfers between devices: 192 us -> 29.4 us  [send(): return lax.ppermute(a, AXES, perm)]
    dot_general x100 -> x0, matrix products: 57.6 us -> none  [the longest x20 18.4 us: one_group(): jnp.einsum('hqk,qhe->khe', weights, grad_part, preferred_element_type=jnp...]
    pallas_call x0 -> x4, Pallas kernels: none -> 30 us  [the longest x2 24.2 us: tiles(): pl.pallas_call(functools.partial(tiles_kernel, keys=tuple(kvs), queries=t...]
    ppermute x20 -> x12, starting transfers between devices: 19.5 us -> 36.4 us  [send(): return lax.ppermute(a, AXES, perm)]
    add x6 -> x0, other arithmetic: 14.9 us -> none  [the longest x3 7.95 us: per_device(): value_acc = value_acc + grad_value]
    ppermute x10 -> x0, local copies, waits for them, and re-layouts: 12.5 us -> none  [shifted(): lax.ppermute(shard, axis, [(i, (i + by) % devices) for i in range(devices)])]
    another operation x15 -> x0, local copies, waits for them, and re-layouts: 11.5 us -> none
    convert_element_type x4 -> x1, other arithmetic: 4.02 us -> 0.11 us  [per_device(): dq_other = (dq2['other'] * scale + back_far_a.astype(jnp.float32) + back_...]
  transfers between devices with their start and end apart: 20 -> 12, of which waited for: 14 -> 5; matrix products, arithmetic and copies ran while one was open for 32% -> 0% of each run, Pallas kernels for 0% -> 9%
where the time goes in v1:
time: 106 us; the launch traced here: 105 us
  starting transfers between devices  36.4 us (34%)
  Pallas kernels  30 us (28%)
  waiting for transfers between devices  29.4 us (28%)
  local copies, waits for them, and re-layouts  7.89 us (7%)
    ppermute x12, starting transfers between devices, send(): return lax.ppermute(a, AXES, perm)  36.4 us
    ppermute x12, waiting for transfers between devices, send(): return lax.ppermute(a, AXES, perm)  29.4 us
    pallas_call x2, Pallas kernels, tiles(): pl.pallas_call(functools.partial(tiles_kernel, keys=tuple(kvs), queries=t...  24.2 us
    unnamed x22, local copies, waits for them, and re-layouts  7.89 us
    pallas_call x1, Pallas kernels, finish(): pl.pallas_call(functools.partial(finish_kernel, scale=scale), grid_spec=p...  3.33 us
    pallas_call x1, Pallas kernels, pack(): pl.pallas_call(pack_kernel, grid_spec=pltpu.PrefetchScalarGridSpec(num_sc...  2.48 us
  transfers between devices with their start and end apart: 12, of which 5 were waited for; matrix products, arithmetic and copies ran while one was open for 0% of the time, Pallas kernels for 9%

profile of v1, /device:TPU:24, one launch (start us, length us, event | category | flops | bytes accessed | tf_op | source)
XLA Modules:
  0.0 104.6 jit_solution(11086111103199825750)
XLA Ops:
  0.6 0.0 copy-start.8
  0.7 0.7 copy-done.8
  1.4 0.0 copy-start.2
  1.4 1.0 copy-done.2
  2.4 0.0 copy-start.3
  2.4 1.0 copy-done.3
  3.4 0.0 copy-start.4
  3.4 1.0 copy-done.4
  4.5 0.0 copy-start.5
  4.5 1.0 copy-done.5
  5.5 0.0 copy-start.6
  5.5 1.0 copy-done.6
  6.6 2.5 %pack.1 = (bf16[528,512]{1,0:T(8,128)(2,1)S(1)}, bf16[512,512]{1,0:T(8,128)(2,1)S(1)}, bf16[528,512]{1,0:T(8,128)(2,1)S(1)}, bf16[512,512]{1,0:T(8,128)(2,1)S(1)}) custom-call(s32[1]{0:T(128)} %bitcast.x_ref, bf16[256,1024]{1,0:T(8,128)(2,1)S(1)} %copy-done.2, bf16[256,1024]{1,0:T(8,128)(2,1)S(1)} %copy-done.3, bf16[256,1024]{1,0:T(8,128)(2,1)S(1)} %copy-done.4, ...), custom_call_target="tpu_custom_call" | custom-call | tf_op jit(solution)/shard_map/pack/pallas_call | solution.py:75
  9.1 3.1 %collective-permute-start = (bf16[528,512]{1,0:T(8,128)(2,1)S(1)}, bf16[528,512]{1,0:T(8,128)(2,1)S(1)}, u32[]{:S(2)}, u32[]{:S(2)}) collective-permute-start(bf16[528,512]{1,0:T(8,128)(2,1)S(1)} %get-tuple-element.22), channel_id=1, source_target_pairs={{0,1},{1,0},{2,3},{3,2},{4,5},{5,4},{6,7},{7,6},{8,9},{9,8},{10,11... | collective-permute-start | bytes 1622024 | tf_op jit(solution)/shard_map/ppermute | solution.py:233
  12.2 1.9 %collective-permute-start.5 = (bf16[528,512]{1,0:T(8,128)(2,1)S(1)}, bf16[528,512]{1,0:T(8,128)(2,1)S(1)}, u32[]{:S(2)}, u32[]{:S(2)}) collective-permute-start(bf16[528,512]{1,0:T(8,128)(2,1)S(1)} %get-tuple-element.25.refs_1_.refs_2_), channel_id=1, source_target_pairs={{0,2},{2,4},{3,1},{4,6},{5,3},{6,8},{7,5},{8,10},{9,7},{10,12},{11... | collective-permute-start | bytes 1622024 | tf_op jit(solution)/shard_map/ppermute | solution.py:233
  14.1 3.9 %collective-permute-start.2 = (bf16[528,512]{1,0:T(8,128)(2,1)S(1)}, bf16[528,512]{1,0:T(8,128)(2,1)S(1)}, u32[]{:S(2)}, u32[]{:S(2)}) collective-permute-start(bf16[528,512]{1,0:T(8,128)(2,1)S(1)} %get-tuple-element.25.refs_1_.refs_2_), channel_id=1, source_target_pairs={{2,0},{4,2},{1,3},{6,4},{3,5},{8,6},{5,7},{10,8},{7,9},{12,10},{9,... | collective-permute-start | bytes 1622024 | tf_op jit(solution)/shard_map/ppermute | solution.py:233
  18.0 11.5 %collective-permute-done.refs_2_.refs_3_ = bf16[528,512]{1,0:T(8,128)(2,1)S(1)} collective-permute-done((bf16[528,512]{1,0:T(8,128)(2,1)S(1)}, bf16[528,512]{1,0:T(8,128)(2,1)S(1)}, u32[]{:S(2)}, u32[]{:S(2)}) %collective-permute-start) | collective-permute-done | bytes 540704 | tf_op jit(solution)/shard_map/ppermute | solution.py:233
  29.5 0.0 copy-start
  29.5 1.9 %collective-permute-start.4 = (bf16[528,512]{1,0:T(8,128)(2,1)S(1)}, bf16[528,512]{1,0:T(8,128)(2,1)S(1)}, u32[]{:S(2)}, u32[]{:S(2)}) collective-permute-start(bf16[528,512]{1,0:T(8,128)(2,1)S(1)} %collective-permute-done.refs_2_.refs_3_), channel_id=1, source_target_pairs={{2,0},{4,2},{1,3},{6,4},{3,5},{8,6},{5,7},{10,8},{7,9},{12,10},{9,... | collective-permute-start | bytes 1622024 | tf_op jit(solution)/shard_map/ppermute | solution.py:233
  31.4 4.9 %collective-permute-start.3 = (bf16[528,512]{1,0:T(8,128)(2,1)S(1)}, bf16[528,512]{1,0:T(8,128)(2,1)S(1)}, u32[]{:S(2)}, u32[]{:S(2)}) collective-permute-start(bf16[528,512]{1,0:T(8,128)(2,1)S(1)} %collective-permute-done.refs_2_.refs_3_), channel_id=1, source_target_pairs={{0,2},{2,4},{3,1},{4,6},{5,3},{6,8},{7,5},{8,10},{9,7},{10,12},{11... | collective-permute-start | bytes 1622024 | tf_op jit(solution)/shard_map/ppermute | solution.py:233
  36.3 3.1 %collective-permute-start.1 = (bf16[512,512]{1,0:T(8,128)(2,1)S(1)}, bf16[512,512]{1,0:T(8,128)(2,1)S(1)}, u32[]{:S(2)}, u32[]{:S(2)}) collective-permute-start(bf16[512,512]{1,0:T(8,128)(2,1)S(1)} %get-tuple-element.23), channel_id=1, source_target_pairs={{0,1},{1,0},{2,3},{3,2},{4,5},{5,4},{6,7},{7,6},{8,9},{9,8},{10,11... | collective-permute-start | bytes 1572872 | tf_op jit(solution)/shard_map/ppermute | solution.py:233
  39.4 0.0 collective-permute-done.5.refs_3_
  39.4 0.0 collective-permute-done.2.refs_4_
  39.4 0.0 copy-start.1
  39.4 9.5 %tiles_near.1 = (f32[256,512]{1,0:T(8,128)S(1)}, f32[256,512]{1,0:T(8,128)S(1)}, bf16[256,512]{1,0:T(8,128)(2,1)S(1)}, f32[256,512]{1,0:T(8,128)S(1)}, f32[512,512]{1,0:T(8,128)S(1)}) custom-call(bf16[512,512]{1,0:T(8,128)(2,1)S(1)} %get-tuple-element.24.refs_0_.refs_1_, bf16[528,512]{1,0:T(8,128)(2,1)S(1)} %get-tuple-element.25.refs_1_.refs_2_, ...), custom_call_target="tpu_custom_call" | custom-call | tf_op jit(solution)/shard_map/tiles_near/pallas_call | solution.py:154
  48.9 0.0 copy-done
  48.9 0.0 copy-done.1
  49.0 0.0 copy-start.7
  49.0 1.0 copy-done.7
  50.0 5.0 %collective-permute-done.1.refs_0_ = bf16[512,512]{1,0:T(8,128)(2,1)S(1)} collective-permute-done((bf16[512,512]{1,0:T(8,128)(2,1)S(1)}, bf16[512,512]{1,0:T(8,128)(2,1)S(1)}, u32[]{:S(2)}, u32[]{:S(2)}) %collective-permute-start.1) | collective-permute-done | bytes 524320 | tf_op jit(solution)/shard_map/ppermute | solution.py:233
  55.0 0.0 collective-permute-done.4.refs_6_
  55.0 0.0 copy-start.9
  55.0 0.0 collective-permute-done.3.refs_5_
  55.0 0.0 copy-start.10
  55.0 0.8 copy-done.9
  55.8 0.2 copy-done.10
  55.9 14.7 %tiles_far.1 = (f32[256,512]{1,0:T(8,128)S(1)}, f32[256,512]{1,0:T(8,128)S(1)}, bf16[256,512]{1,0:T(8,128)(2,1)S(1)}, bf16[256,512]{1,0:T(8,128)(2,1)S(1)}, bf16...) custom-call(bf16[512,512]{1,0:T(8,128)(2,1)S(1)} %collective-permute-done.1.refs_0_, ...), custom_call_target="tpu_custom_call" | custom-call | tf_op jit(solution)/shard_map/tiles_far/pallas_call | solution.py:154
  70.6 1.9 %collective-permute-start.8 = (bf16[256,512]{1,0:T(8,128)(2,1)S(1)}, bf16[256,512]{1,0:T(8,128)(2,1)S(1)}, u32[]{:S(2)}, u32[]{:S(2)}) collective-permute-start(bf16[256,512]{1,0:T(8,128)(2,1)S(1)} %get-tuple-element.36), channel_id=1, source_target_pairs={{2,0},{4,2},{1,3},{6,4},{3,5},{8,6},{5,7},{10,8},{7,9},{12,10},{9,... | collective-permute-start | bytes 786440 | tf_op jit(solution)/shard_map/ppermute | solution.py:233
  72.6 4.9 %collective-permute-start.9 = (bf16[256,512]{1,0:T(8,128)(2,1)S(1)}, bf16[256,512]{1,0:T(8,128)(2,1)S(1)}, u32[]{:S(2)}, u32[]{:S(2)}) collective-permute-start(bf16[256,512]{1,0:T(8,128)(2,1)S(1)} %get-tuple-element.37), channel_id=1, source_target_pairs={{0,2},{2,4},{3,1},{4,6},{5,3},{6,8},{7,5},{8,10},{9,7},{10,12},{11... | collective-permute-start | bytes 786440 | tf_op jit(solution)/shard_map/ppermute | solution.py:233
  77.4 3.2 %collective-permute-start.11 = (bf16[512,512]{1,0:T(8,128)(2,1)S(1)}, bf16[512,512]{1,0:T(8,128)(2,1)S(1)}, u32[]{:S(2)}, u32[]{:S(2)}) collective-permute-start(bf16[512,512]{1,0:T(8,128)(2,1)S(1)} %get-tuple-element.38), channel_id=1, source_target_pairs={{0,1},{1,0},{2,3},{3,2},{4,5},{5,4},{6,7},{7,6},{8,9},{9,8},{10,11... | collective-permute-start | bytes 1572872 | tf_op jit(solution)/shard_map/ppermute | solution.py:233
  80.6 1.9 %collective-permute-start.6 = (bf16[256,512]{1,0:T(8,128)(2,1)S(1)}, bf16[256,512]{1,0:T(8,128)(2,1)S(1)}, u32[]{:S(2)}, u32[]{:S(2)}) collective-permute-start(bf16[256,512]{1,0:T(8,128)(2,1)S(1)} %get-tuple-element.32), channel_id=1, source_target_pairs={{2,0},{4,2},{1,3},{6,4},{3,5},{8,6},{5,7},{10,8},{7,9},{12,10},{9,... | collective-permute-start | bytes 786440 | tf_op jit(solution)/shard_map/ppermute | solution.py:233
  82.5 4.9 %collective-permute-start.7 = (bf16[256,512]{1,0:T(8,128)(2,1)S(1)}, bf16[256,512]{1,0:T(8,128)(2,1)S(1)}, u32[]{:S(2)}, u32[]{:S(2)}) collective-permute-start(bf16[256,512]{1,0:T(8,128)(2,1)S(1)} %get-tuple-element.33), channel_id=1, source_target_pairs={{0,2},{2,4},{3,1},{4,6},{5,3},{6,8},{7,5},{8,10},{9,7},{10,12},{11... | collective-permute-start | bytes 786440 | tf_op jit(solution)/shard_map/ppermute | solution.py:233
  87.4 0.0 collective-permute-done.8
  87.4 0.0 collective-permute-done.9
  87.4 0.1 add_convert_fusion
  87.5 0.9 collective-permute-start.10
  88.4 3.0 %collective-permute-done.6.ret_a = bf16[256,512]{1,0:T(8,128)(2,1)S(1)} collective-permute-done((bf16[256,512]{1,0:T(8,128)(2,1)S(1)}, bf16[256,512]{1,0:T(8,128)(2,1)S(1)}, u32[]{:S(2)}, u32[]{:S(2)}) %collective-permute-start.6) | collective-permute-done | bytes 262176 | tf_op jit(solution)/shard_map/ppermute | solution.py:233
  91.3 0.0 collective-permute-done.7.ret_b
  91.3 5.3 %collective-permute-done.11.dkv_other = bf16[512,512]{1,0:T(8,128)(2,1)S(1)} collective-permute-done((bf16[512,512]{1,0:T(8,128)(2,1)S(1)}, bf16[512,512]{1,0:T(8,128)(2,1)S(1)}, u32[]{:S(2)}, u32[]{:S(2)}) %collective-permute-start.11) | collective-permute-done | bytes 524320 | tf_op jit(solution)/shard_map/ppermute | solution.py:233
  96.7 4.6 %collective-permute-done.10.dq_other = bf16[256,512]{1,0:T(8,128)(2,1)S(1)} collective-permute-done((bf16[256,512]{1,0:T(8,128)(2,1)S(1)}, bf16[256,512]{1,0:T(8,128)(2,1)S(1)}, u32[]{:S(2)}, u32[]{:S(2)}) %collective-permute-start.10) | collective-permute-done | bytes 262176 | tf_op jit(solution)/shard_map/ppermute | solution.py:233
  101.3 3.3 %finish.1 = (bf16[256,1024]{1,0:T(8,128)(2,1)}, bf16[256,1024]{1,0:T(8,128)(2,1)}, bf16[256,1024]{1,0:T(8,128)(2,1)}) custom-call(s32[1]{0:T(128)} %bitcast.x_ref, f32[256,512]{1,0:T(8,128)S(1)} %get-tuple-element.31.dq_own, bf16[256,512]{1,0:T(8,128)(2,1)S(1)} %collective-permute-done.6.ret_a, bf16[256,512]{1,0:T(8,128)(2,1)S(1)} %collective-permute-done.7.ret_b, ...), custom_call_target="tpu_custom_call" | custom-call | tf_op jit(solution)/shard_map/finish/pallas_call | solution.py:205
Async XLA Ops:
  0.6 0.7 copy-start.8
  1.4 1.0 copy-start.2
  2.4 1.0 copy-start.3
  3.4 1.0 copy-start.4
  4.5 1.0 copy-start.5
  5.5 1.0 copy-start.6
  9.1 20.4 %collective-permute-start = (bf16[528,512]{1,0:T(8,128)(2,1)S(1)}, bf16[528,512]{1,0:T(8,128)(2,1)S(1)}, u32[]{:S(2)}, u32[]{:S(2)}) collective-permute-start(bf16[528,512]{1,0:T(8,128)(2,1)S(1)} %get-tuple-element.22), channel_id=1, source_target_pairs={{0,1},{1,0},{2,3},{3,2},{4,5},{5,4},{6,7},{7,6},{8,9},{9,8},{10,11... | collective-permute-start | bytes 1622024 | tf_op jit(solution)/shard_map/ppermute | solution.py:233
  12.2 27.3 %collective-permute-start.5 = (bf16[528,512]{1,0:T(8,128)(2,1)S(1)}, bf16[528,512]{1,0:T(8,128)(2,1)S(1)}, u32[]{:S(2)}, u32[]{:S(2)}) collective-permute-start(bf16[528,512]{1,0:T(8,128)(2,1)S(1)} %get-tuple-element.25.refs_1_.refs_2_), channel_id=1, source_target_pairs={{0,2},{2,4},{3,1},{4,6},{5,3},{6,8},{7,5},{8,10},{9,7},{10,12},{11... | collective-permute-start | bytes 1622024 | tf_op jit(solution)/shard_map/ppermute | solution.py:233
  14.1 25.3 %collective-permute-start.2 = (bf16[528,512]{1,0:T(8,128)(2,1)S(1)}, bf16[528,512]{1,0:T(8,128)(2,1)S(1)}, u32[]{:S(2)}, u32[]{:S(2)}) collective-permute-start(bf16[528,512]{1,0:T(8,128)(2,1)S(1)} %get-tuple-element.25.refs_1_.refs_2_), channel_id=1, source_target_pairs={{2,0},{4,2},{1,3},{6,4},{3,5},{8,6},{5,7},{10,8},{7,9},{12,10},{9,... | collective-permute-start | bytes 1622024 | tf_op jit(solution)/shard_map/ppermute | solution.py:233
  29.5 19.4 %copy-start = (bf16[528,512]{1,0:T(8,128)(2,1)}, bf16[528,512]{1,0:T(8,128)(2,1)S(1)}, u32[]{:S(2)}) copy-start(bf16[528,512]{1,0:T(8,128)(2,1)S(1)} %collective-permute-done.refs_2_.refs_3_) | copy-start | bytes 1622020
  29.5 25.5 %collective-permute-start.4 = (bf16[528,512]{1,0:T(8,128)(2,1)S(1)}, bf16[528,512]{1,0:T(8,128)(2,1)S(1)}, u32[]{:S(2)}, u32[]{:S(2)}) collective-permute-start(bf16[528,512]{1,0:T(8,128)(2,1)S(1)} %collective-permute-done.refs_2_.refs_3_), channel_id=1, source_target_pairs={{2,0},{4,2},{1,3},{6,4},{3,5},{8,6},{5,7},{10,8},{7,9},{12,10},{9,... | collective-permute-start | bytes 1622024 | tf_op jit(solution)/shard_map/ppermute | solution.py:233
  31.4 23.6 %collective-permute-start.3 = (bf16[528,512]{1,0:T(8,128)(2,1)S(1)}, bf16[528,512]{1,0:T(8,128)(2,1)S(1)}, u32[]{:S(2)}, u32[]{:S(2)}) collective-permute-start(bf16[528,512]{1,0:T(8,128)(2,1)S(1)} %collective-permute-done.refs_2_.refs_3_), channel_id=1, source_target_pairs={{0,2},{2,4},{3,1},{4,6},{5,3},{6,8},{7,5},{8,10},{9,7},{10,12},{11... | collective-permute-start | bytes 1622024 | tf_op jit(solution)/shard_map/ppermute | solution.py:233
  36.3 18.7 %collective-permute-start.1 = (bf16[512,512]{1,0:T(8,128)(2,1)S(1)}, bf16[512,512]{1,0:T(8,128)(2,1)S(1)}, u32[]{:S(2)}, u32[]{:S(2)}) collective-permute-start(bf16[512,512]{1,0:T(8,128)(2,1)S(1)} %get-tuple-element.23), channel_id=1, source_target_pairs={{0,1},{1,0},{2,3},{3,2},{4,5},{5,4},{6,7},{7,6},{8,9},{9,8},{10,11... | collective-permute-start | bytes 1572872 | tf_op jit(solution)/shard_map/ppermute | solution.py:233
  39.4 9.5 %copy-start.1 = (bf16[528,512]{1,0:T(8,128)(2,1)}, bf16[528,512]{1,0:T(8,128)(2,1)S(1)}, u32[]{:S(2)}) copy-start(bf16[528,512]{1,0:T(8,128)(2,1)S(1)} %collective-permute-done.2.refs_4_) | copy-start | bytes 1622020
  49.0 1.0 copy-start.7
  55.0 0.8 copy-start.9
  55.0 1.0 copy-start.10
  70.6 16.7 %collective-permute-start.8 = (bf16[256,512]{1,0:T(8,128)(2,1)S(1)}, bf16[256,512]{1,0:T(8,128)(2,1)S(1)}, u32[]{:S(2)}, u32[]{:S(2)}) collective-permute-start(bf16[256,512]{1,0:T(8,128)(2,1)S(1)} %get-tuple-element.36), channel_id=1, source_target_pairs={{2,0},{4,2},{1,3},{6,4},{3,5},{8,6},{5,7},{10,8},{7,9},{12,10},{9,... | collective-permute-start | bytes 786440 | tf_op jit(solution)/shard_map/ppermute | solution.py:233
  72.6 14.8 %collective-permute-start.9 = (bf16[256,512]{1,0:T(8,128)(2,1)S(1)}, bf16[256,512]{1,0:T(8,128)(2,1)S(1)}, u32[]{:S(2)}, u32[]{:S(2)}) collective-permute-start(bf16[256,512]{1,0:T(8,128)(2,1)S(1)} %get-tuple-element.37), channel_id=1, source_target_pairs={{0,2},{2,4},{3,1},{4,6},{5,3},{6,8},{7,5},{8,10},{9,7},{10,12},{11... | collective-permute-start | bytes 786440 | tf_op jit(solution)/shard_map/ppermute | solution.py:233
  77.4 19.2 %collective-permute-start.11 = (bf16[512,512]{1,0:T(8,128)(2,1)S(1)}, bf16[512,512]{1,0:T(8,128)(2,1)S(1)}, u32[]{:S(2)}, u32[]{:S(2)}) collective-permute-start(bf16[512,512]{1,0:T(8,128)(2,1)S(1)} %get-tuple-element.38), channel_id=1, source_target_pairs={{0,1},{1,0},{2,3},{3,2},{4,5},{5,4},{6,7},{7,6},{8,9},{9,8},{10,11... | collective-permute-start | bytes 1572872 | tf_op jit(solution)/shard_map/ppermute | solution.py:233
  80.6 10.7 %collective-permute-start.6 = (bf16[256,512]{1,0:T(8,128)(2,1)S(1)}, bf16[256,512]{1,0:T(8,128)(2,1)S(1)}, u32[]{:S(2)}, u32[]{:S(2)}) collective-permute-start(bf16[256,512]{1,0:T(8,128)(2,1)S(1)} %get-tuple-element.32), channel_id=1, source_target_pairs={{2,0},{4,2},{1,3},{6,4},{3,5},{8,6},{5,7},{10,8},{7,9},{12,10},{9,... | collective-permute-start | bytes 786440 | tf_op jit(solution)/shard_map/ppermute | solution.py:233
  82.5 8.8 %collective-permute-start.7 = (bf16[256,512]{1,0:T(8,128)(2,1)S(1)}, bf16[256,512]{1,0:T(8,128)(2,1)S(1)}, u32[]{:S(2)}, u32[]{:S(2)}) collective-permute-start(bf16[256,512]{1,0:T(8,128)(2,1)S(1)} %get-tuple-element.33), channel_id=1, source_target_pairs={{0,2},{2,4},{3,1},{4,6},{5,3},{6,8},{7,5},{8,10},{9,7},{10,12},{11... | collective-permute-start | bytes 786440 | tf_op jit(solution)/shard_map/ppermute | solution.py:233
  87.5 13.8 %collective-permute-start.10 = (bf16[256,512]{1,0:T(8,128)(2,1)S(1)}, bf16[256,512]{1,0:T(8,128)(2,1)S(1)}, u32[]{:S(2)}, u32[]{:S(2)}) collective-permute-start(bf16[256,512]{1,0:T(8,128)(2,1)S(1)} %add_convert_fusion), channel_id=1, source_target_pairs={{0,1},{1,0},{2,3},{3,2},{4,5},{5,4},{6,7},{7,6},{8,9},{9,8},{10,11... | collective-permute-start | bytes 786440 | tf_op jit(solution)/shard_map/ppermute | solution.py:233

commit v2 on v0

v2 whole, which is shorter than its diff:
```python
import functools

import jax
import jax.numpy as jnp
from jax import lax
from jax.experimental import pallas as pl
from jax.experimental.pallas import tpu as pltpu
from jax.sharding import PartitionSpec as P

AXES = ("outer", "inner")
LANES = 128
LOG2E = 1.4426950408889634
WHOLE = pl.BlockSpec(memory_space=pltpu.VMEM)
IN_HBM = pl.BlockSpec(memory_space=pltpu.HBM)
PARAMS = pltpu.CompilerParams(vmem_limit_bytes=16 * 1024 * 1024)


def dot_nt(a, b):
    return lax.dot_general(a, b, (((1,), (1,)), ((), ())), preferred_element_type=jnp.float32)


def dot_nn(a, b):
    return lax.dot_general(a, b, (((1,), (0,)), ((), ())), preferred_element_type=jnp.float32)


def head_masks(dtype):
    lane = lax.broadcasted_iota(jnp.int32, (1, LANES), 1)
    first = jnp.where(lane < LANES // 2, 1.0, 0.0)
    return first.astype(dtype), (1.0 - first).astype(dtype)


def pack_kernel(x_ref, q, k, v, o, g, norms, msg, kv, msg_other, kv_other, outs, norm_buf, sems, norm_sem):
    rows, width = q.shape
    half = width // 2
    sides = ((1 - x_ref[0], msg_other, kv_other), (x_ref[0], msg, kv))
    norm_copy = pltpu.make_async_copy(norms, norm_buf, norm_sem)
    norm_copy.start()
    copies = []
    for at, (side, to, _) in enumerate(sides):
        columns = pl.ds(pl.multiple_of(side * half, LANES), half)
        moves = ((g, to.at[rows : 2 * rows]), (o, outs.at[at]), (q, to.at[0:rows]))
        copies.append([pltpu.make_async_copy(a.at[:, columns], b, sems.at[at, n]) for n, (a, b) in enumerate(moves)])
    later = []
    for at, (side, _, to) in enumerate(sides):
        columns = pl.ds(pl.multiple_of(side * half, LANES), half)
        moves = ((k, to.at[0:rows]), (v, to.at[rows : 2 * rows]))
        later += [pltpu.make_async_copy(a.at[:, columns], b, sems.at[at, 3 + n]) for n, (a, b) in enumerate(moves)]
    for copy in copies[0] + copies[1] + later:
        copy.start()
    norm_copy.wait()
    row = lax.broadcasted_iota(jnp.int32, (8, LANES), 0)
    lane = lax.broadcasted_iota(jnp.int32, (8, LANES), 1)
    pick = jnp.where(row == lane // (LANES // 2), 1.0, 0.0).astype(jnp.bfloat16)
    for at, (side, to, _) in enumerate(sides):
        copies[at][0].wait()
        copies[at][1].wait()
        for pair in range(half // LANES):
            span = slice(pair * LANES, (pair + 1) * LANES)
            product = outs[at, :, span].astype(jnp.float32) * to[rows : 2 * rows, span].astype(jnp.float32)
            high = product.astype(jnp.bfloat16)
            low = (product - high.astype(jnp.float32)).astype(jnp.bfloat16)
            delta = dot_nt(pick, high) + dot_nt(pick, low)
            first = 2 * (side * (half // LANES) + pair)
            terms = jnp.concatenate(
                [norm_buf[pl.ds(first, 1), :], norm_buf[pl.ds(first + 1, 1), :], delta[0:2]], axis=0
            )
            terms_high = terms.astype(jnp.bfloat16).astype(jnp.float32)
            both = jnp.concatenate([terms_high, terms - terms_high], axis=0)
            to[2 * rows : 2 * rows + 16, span] = jnp.concatenate(
                [both[:, :LANES], both[:, LANES:]], axis=0
            ).astype(jnp.bfloat16)
        copies[at][2].wait()
    for copy in later:
        copy.wait()


def pack(x, q, k, v, o, g, norms):
    rows, width = q.shape
    msg = jax.ShapeDtypeStruct((2 * rows + 16, width // 2), jnp.bfloat16)
    kv = jax.ShapeDtypeStruct((2 * rows, width // 2), jnp.bfloat16)
    return pl.pallas_call(
        pack_kernel,
        in_specs=[pl.BlockSpec(memory_space=pltpu.SMEM)] + [IN_HBM] * 6,
        out_specs=[WHOLE] * 4,
        out_shape=[msg, kv, msg, kv],
        scratch_shapes=[
            pltpu.VMEM((2, rows, width // 2), jnp.bfloat16),
            pltpu.VMEM(norms.shape, jnp.float32),
            pltpu.SemaphoreType.DMA((2, 5)),
            pltpu.SemaphoreType.DMA,
        ],
        compiler_params=PARAMS,
        name="pack",
    )(x, *(pltpu.with_memory_space_constraint(a, pltpu.HBM) for a in (q, k, v, o, g, norms)))


def run_tiles(kv_refs, msg_refs, pairs, dq_in, dkv_in, dq_out, dkv_out, scale):
    rows, width = next(iter(kv_refs.values())).shape
    rows //= 2
    half = LANES // 2
    masks = head_masks(jnp.bfloat16)
    key_side, query_side = {}, {}

    def span(group):
        return slice(group * LANES, (group + 1) * LANES)

    def keys_of(u, group):
        if (u, group) not in key_side:
            k, v = kv_refs[u][0:rows, span(group)], kv_refs[u][rows : 2 * rows, span(group)]
            kt = k.T
            sums = [None, None]
            if u in dkv_in:
                sums = [dkv_in[u][0:rows, span(group)], dkv_in[u][rows : 2 * rows, span(group)]]
            key_side[u, group] = (k, v, [kt[0:half], kt[half:LANES]], sums)
        return key_side[u, group]

    def queries_of(t, group):
        if (t, group) not in query_side:
            msg = msg_refs[t]
            q, g = msg[0:rows, span(group)], msg[rows : 2 * rows, span(group)]
            info = msg[2 * rows : 2 * rows + 16, span(group)].astype(jnp.float32)
            both = jnp.concatenate([info[0:8], info[8:16]], axis=1)
            terms = both[0:4] + both[4:8]
            query_side[t, group] = (
                [q * m for m in masks],
                [g * m for m in masks],
                terms[0:2] * LOG2E,
                terms[2:4],
                [None, None],
            )
        return query_side[t, group]

    def plus(a, b):
        return b if a is None else a + b

    items = [(group, u, t, h) for group in range(width // LANES) for u, t in pairs for h in range(2)]
    last_of = {}
    for group, u, t, h in items:
        last_of["key", u, group] = last_of["query", t, group] = (group, u, t, h)

    def products(item):
        group, u, t, h = item
        k, v, _, _ = keys_of(u, group)
        qs, gs = queries_of(t, group)[:2]
        return dot_nt(k, qs[h]), dot_nt(v, gs[h])

    def weigh(item, scores, grad_prob):
        group, u, t, h = item
        _, _, norms, deltas, _ = queries_of(t, group)
        probs = jnp.exp2(scores * (scale * LOG2E) - norms[h : h + 1])
        grad_score = probs * (grad_prob - deltas[h : h + 1])
        return probs.astype(jnp.bfloat16), grad_score.astype(jnp.bfloat16)

    def add_up(item, weights, grad_score):
        group, u, t, h = item
        _, _, kt, sums = keys_of(u, group)
        qs, gs, _, _, dq = queries_of(t, group)
        sums[1] = plus(sums[1], dot_nn(weights, gs[h]))
        sums[0] = plus(sums[0], dot_nn(grad_score, qs[h]))
        dq[h] = plus(dq[h], dot_nn(kt[h], grad_score))
        if last_of["query", t, group] == item:
            total = jnp.concatenate(dq, axis=0).T
            if t in dq_in:
                total = total + dq_in[t][:, span(group)]
            ref = dq_out[t]
            final = ref.dtype == jnp.bfloat16
            ref[:, span(group)] = (total * scale if final else total).astype(ref.dtype)
        if last_of["key", u, group] == item:
            ref = dkv_out[u]
            final = ref.dtype == jnp.bfloat16
            ref[0:rows, span(group)] = (sums[0] * scale if final else sums[0]).astype(ref.dtype)
            ref[rows : 2 * rows, span(group)] = sums[1].astype(ref.dtype)

    made, weighed = {}, {}
    for step in range(len(items) + 2):
        if step < len(items):
            made[step] = products(items[step])
        if 0 <= step - 1 < len(items):
            weighed[step - 1] = weigh(items[step - 1], *made.pop(step - 1))
        if 0 <= step - 2:
            add_up(items[step - 2], *weighed.pop(step - 2))


def near_kernel(kv, own, other, near_1, near_2, dq_own, dq_other, dq_1, dq_2, dkv, *, scale):
    run_tiles(
        {"own": kv},
        {"own": own, "other": other, "1": near_1, "2": near_2},
        [("own", t) for t in ("own", "1", "2", "other")],
        {},
        {},
        {"own": dq_own, "other": dq_other, "1": dq_1, "2": dq_2},
        {"own": dkv},
        scale,
    )


def near_tiles(kv, own, other, near_1, near_2, scale):
    rows, width = kv.shape[0] // 2, kv.shape[1]
    part = jax.ShapeDtypeStruct((rows, width), jnp.float32)
    return pl.pallas_call(
        functools.partial(near_kernel, scale=scale),
        in_specs=[WHOLE] * 5,
        out_specs=[WHOLE] * 5,
        out_shape=[part] * 4 + [jax.ShapeDtypeStruct(kv.shape, jnp.float32)],
        compiler_params=PARAMS,
        name="near_tiles",
    )(kv, own, other, near_1, near_2)


def far_kernel(
    place_ref, kv, kv_other, own, other, near_1, near_2, far_1, far_2, dq_own, dq_other, dq_1, dq_2, dkv,
    out_own, out_other, back_1, back_2, dkv_own, dkv_other, near_b, far_a, far_b, dq_b, back_a, back_b, *, scale
):
    rows = dq_1.shape[0]

    def sort(sides):
        (near_a_in, far_a_in, dq_a_in), (near_b_in, far_b_in, dq_b_in) = sides
        near_b[...] = near_b_in[...]
        far_a[...] = far_a_in[...]
        far_b[...] = far_b_in[...]
        dq_b[...] = dq_b_in[...]
        back_a[0:rows] = (dq_a_in[...] * scale).astype(back_a.dtype)

    first, second = (near_1, far_1, dq_1), (near_2, far_2, dq_2)
    pl.when(place_ref[1] == 1)(lambda: sort((first, second)))
    pl.when(place_ref[1] != 1)(lambda: sort((second, first)))
    run_tiles(
        {"own": kv, "other": kv_other},
        {"own": own, "other": other, "near_b": near_b, "far_a": far_a, "far_b": far_b},
        [("other", "near_b"), ("other", "far_b"), ("other", "far_a"), ("own", "far_a"), ("other", "own"), ("other", "other")],
        {"own": dq_own, "other": dq_other, "near_b": dq_b},
        {"own": dkv},
        {
            "own": out_own,
            "other": out_other,
            "near_b": back_b.at[0:rows],
            "far_a": back_a.at[rows : 2 * rows],
            "far_b": back_b.at[rows : 2 * rows],
        },
        {"own": dkv_own, "other": dkv_other},
        scale,
    )

    def unsort(out_a, out_b):
        out_a[...] = back_a[...]
        out_b[...] = back_b[...]

    pl.when(place_ref[1] == 1)(lambda: unsort(back_1, back_2))
    pl.when(place_ref[1] != 1)(lambda: unsort(back_2, back_1))


def far_tiles(x, *operands, scale):
    kv, msg = operands[0], operands[2]
    rows, width = kv.shape[0] // 2, kv.shape[1]
    part = jax.ShapeDtypeStruct((rows, width), jnp.float32)
    done = jax.ShapeDtypeStruct(kv.shape, jnp.bfloat16)
    return pl.pallas_call(
        functools.partial(far_kernel, scale=scale),
        in_specs=[pl.BlockSpec(memory_space=pltpu.SMEM)] + [WHOLE] * len(operands),
        out_specs=[WHOLE] * 6,
        out_shape=[part, part] + [done] * 4,
        scratch_shapes=[pltpu.VMEM(msg.shape, msg.dtype)] * 3
        + [pltpu.VMEM(part.shape, part.dtype)]
        + [pltpu.VMEM(done.shape, done.dtype)] * 2,
        compiler_params=PARAMS,
        name="far_tiles",
    )(x, *operands)


def sum_other_kernel(dq, back_a, back_b, out, *, scale):
    rows = dq.shape[0]
    total = dq[...] * scale + back_a[rows:].astype(jnp.float32) + back_b[rows:].astype(jnp.float32)
    out[...] = total.astype(jnp.bfloat16)


def sum_other(dq, back_a, back_b, scale):
    return pl.pallas_call(
        functools.partial(sum_other_kernel, scale=scale),
        in_specs=[WHOLE] * 3,
        out_specs=WHOLE,
        out_shape=jax.ShapeDtypeStruct(dq.shape, jnp.bfloat16),
        compiler_params=PARAMS,
        name="sum_other",
    )(dq, back_a, back_b)


def finish_kernel(x_ref, dq_own, back_a, back_b, dkv_own, dkv_other, dq, dk, dv, buffer, sems, *, scale):
    rows, half = buffer.shape
    at_own = pl.ds(pl.multiple_of(x_ref[0] * half, LANES), half)
    at_other = pl.ds(pl.multiple_of((1 - x_ref[0]) * half, LANES), half)
    moves = (
        (dkv_own.at[0:rows], dk.at[:, at_own]),
        (dkv_own.at[rows : 2 * rows], dv.at[:, at_own]),
        (dkv_other.at[0:rows], dk.at[:, at_other]),
        (dkv_other.at[rows : 2 * rows], dv.at[:, at_other]),
    )
    copies = [pltpu.make_async_copy(a, b, sems.at[n]) for n, (a, b) in enumerate(moves)]
    for copy in copies:
        copy.start()
    total = (
        dq_own[...] * scale + back_a[0:rows].astype(jnp.float32) + back_b[0:rows].astype(jnp.float32)
    )
    buffer[...] = total.astype(jnp.bfloat16)
    copies.append(pltpu.make_async_copy(buffer, dq.at[:, at_own], sems.at[4]))
    copies[-1].start()
    for copy in copies:
        copy.wait()


def finish(x, dq_own, back_a, back_b, dkv_own, dkv_other, scale):
    rows, half = dq_own.shape
    return pl.pallas_call(
        functools.partial(finish_kernel, scale=scale),
        in_specs=[pl.BlockSpec(memory_space=pltpu.SMEM)] + [WHOLE] * 5,
        out_specs=[IN_HBM] * 3,
        out_shape=[jax.ShapeDtypeStruct((rows, 2 * half), jnp.bfloat16)] * 3,
        scratch_shapes=[pltpu.VMEM((rows, half), jnp.bfloat16), pltpu.SemaphoreType.DMA((5,))],
        compiler_params=PARAMS,
        name="finish",
    )(x, dq_own, back_a, back_b, dkv_own, dkv_other)


def place_kernel(x_ref, part, _, whole, sem):
    half = part.shape[1]
    at_other = pl.ds(pl.multiple_of((1 - x_ref[0]) * half, LANES), half)
    copy = pltpu.make_async_copy(part, whole.at[:, at_other], sem)
    copy.start()
    copy.wait()


def place(x, part, whole):
    return pl.pallas_call(
        place_kernel,
        in_specs=[pl.BlockSpec(memory_space=pltpu.SMEM), WHOLE, IN_HBM],
        out_specs=IN_HBM,
        out_shape=jax.ShapeDtypeStruct(whole.shape, whole.dtype),
        scratch_shapes=[pltpu.SemaphoreType.DMA],
        input_output_aliases={2: 0},
        compiler_params=PARAMS,
        name="place",
    )(x, part, whole)


def per_device(query_rows, key_rows, value_rows, layer_output, output_grad, log_norms):
    count = lax.axis_size("outer") * lax.axis_size("inner")
    index = lax.axis_index("outer") * lax.axis_size("inner") + lax.axis_index("inner")
    column, row = index % 2, index // 2 % 2
    x = jnp.stack([column, column ^ row]).astype(jnp.int32)
    head_size = query_rows.shape[1] // log_norms.shape[0]
    scale = head_size ** (-0.5)

    swap = [(i, i ^ 1) for i in range(count)]
    step_1 = [(i, i ^ 2) for i in range(count)]
    step_2 = [(i, ((i + 2) ^ 2) - 2) for i in range(count)]
    step_2 = [(i, j) for i, j in step_2 if 0 <= j < count]

    def send(a, perm):
        return lax.ppermute(a, AXES, perm)

    own, kv_own, to_other, kv_to_other = pack(
        x, query_rows, key_rows, value_rows, layer_output, output_grad, log_norms
    )
    other = send(to_other, swap)
    near_1, near_2 = send(own, step_1), send(own, step_2)
    kv_to_other, other = lax.optimization_barrier((kv_to_other, other))
    kv_other = send(kv_to_other, swap)
    far_1, far_2 = send(other, step_1), send(other, step_2)
    dq_own, dq_other, dq_1, dq_2, dkv = near_tiles(kv_own, own, other, near_1, near_2, scale)
    dq_own, dq_other, to_1, to_2, dkv_own, dkv_to_other = far_tiles(
        x, kv_own, kv_other, own, other, near_1, near_2, far_1, far_2,
        dq_own, dq_other, dq_1, dq_2, dkv, scale=scale,
    )
    dkv_other = send(dkv_to_other, swap)
    back_1, back_2 = send(to_1, step_1), send(to_2, step_2)
    dq_from_other = send(sum_other(dq_other, back_1, back_2, scale), swap)
    dq, dk, dv = finish(x, dq_own, back_1, back_2, dkv_own, dkv_other, scale)
    return place(x, dq_from_other, dq), dk, dv


def solution(mesh):
    rows = P(AXES, None)
    return jax.shard_map(
        per_device,
        mesh=mesh,
        in_specs=(rows, rows, rows, rows, rows, P(None, AXES)),
        out_specs=(rows, rows, rows),
        check_vma=False,
    )
```

time: 327 us -> 83.3 us (0.25); the launches traced: 322 us -> 83.1 us
  waiting for transfers between devices: 192 us -> 47.3 us
  matrix products: 57.6 us -> 0 us
  local copies, waits for them, and re-layouts: 31.6 us -> 0 us
  Pallas kernels: 0 us -> 20.1 us
  other arithmetic: 19.1 us -> 0.08 us
  starting transfers between devices: 19.5 us -> 14.7 us
    ppermute x20 -> x10, waiting for transfers between devices: 192 us -> 47.3 us  [send(): return lax.ppermute(a, AXES, perm)]
    dot_general x100 -> x0, matrix products: 57.6 us -> none  [the longest x20 18.4 us: one_group(): jnp.einsum('hqk,qhe->khe', weights, grad_part, preferred_element_type=jnp...]
    pallas_call x0 -> x6, Pallas kernels: none -> 20.1 us  [the longest x1 9 us: far_tiles(): pl.pallas_call(functools.partial(far_kernel, scale=scale), in_specs=[pl.B...]
    add x6 -> x0, other arithmetic: 14.9 us -> none  [the longest x3 7.95 us: per_device(): value_acc = value_acc + grad_value]
    ppermute x10 -> x0, local copies, waits for them, and re-layouts: 12.5 us -> none  [shifted(): lax.ppermute(shard, axis, [(i, (i + by) % devices) for i in range(devices)])]
    another operation x15 -> x0, local copies, waits for them, and re-layouts: 11.5 us -> none
    unnamed x24 -> x0, local copies, waits for them, and re-layouts: 7.49 us -> none
    ppermute x20 -> x10, starting transfers between devices: 19.5 us -> 14.7 us  [send(): return lax.ppermute(a, AXES, perm)]
  transfers between devices with their start and end apart: 20 -> 10, of which waited for: 14 -> 6; matrix products, arithmetic and copies ran while one was open for 32% -> 0% of each run, Pallas kernels for 0% -> 9%
where the time goes in v2:
time: 83.3 us; the launch traced here: 83.1 us
  waiting for transfers between devices  47.3 us (57%)
  Pallas kernels  20.1 us (24%)
  starting transfers between devices  14.7 us (18%)
  between operations  0.91 us (1%)
    ppermute x10, waiting for transfers between devices, send(): return lax.ppermute(a, AXES, perm)  47.3 us
    ppermute x10, starting transfers between devices, send(): return lax.ppermute(a, AXES, perm)  14.7 us
    pallas_call x1, Pallas kernels, far_tiles(): pl.pallas_call(functools.partial(far_kernel, scale=scale), in_specs=[pl.B...  9 us
    pallas_call x1, Pallas kernels, near_tiles(): pl.pallas_call(functools.partial(near_kernel, scale=scale), in_specs=[WHO...  5.41 us
    pallas_call x1, Pallas kernels, pack(): pl.pallas_call(pack_kernel, in_specs=[pl.BlockSpec(memory_space=pltpu.SME...  2.69 us
  transfers between devices with their start and end apart: 10, of which 6 were waited for; matrix products, arithmetic and copies ran while one was open for 0% of the time, Pallas kernels for 9%

profile of v2, /device:TPU:24, one launch (start us, length us, event | category | flops | bytes accessed | tf_op | source)
XLA Modules:
  0.0 83.1 jit_solution(6260659556198986750)
XLA Ops:
  0.7 0.1 pad_add_fusion.x_ref.place_ref
  0.7 2.7 %pack.1 = (bf16[528,512]{1,0:T(8,128)(2,1)S(1)}, bf16[512,512]{1,0:T(8,128)(2,1)S(1)}, bf16[528,512]{1,0:T(8,128)(2,1)S(1)}, bf16[512,512]{1,0:T(8,128)(2,1)S(1)}) custom-call(s32[2]{0:T(128)S(1)} %pad_add_fusion.x_ref.place_ref, bf16[256,1024]{1,0:T(8,128)(2,1)} %q.1, bf16[256,1024]{1,0:T(8,128)(2,1)} %k.1, bf16[256,1024]{1,0:T(8,128)(2,1)} %v.1, ...), custom_call_target="tpu_custom_call" | custom-call | tf_op jit(solution)/shard_map/pack/pallas_call | solution.py:81
  3.4 3.1 %collective-permute-start = (bf16[528,512]{1,0:T(8,128)(2,1)S(1)}, bf16[528,512]{1,0:T(8,128)(2,1)S(1)}, u32[]{:S(2)}, u32[]{:S(2)}) collective-permute-start(bf16[528,512]{1,0:T(8,128)(2,1)S(1)} %get-tuple-element.25), channel_id=1, source_target_pairs={{0,1},{1,0},{2,3},{3,2},{4,5},{5,4},{6,7},{7,6},{8,9},{9,8},{10,11... | collective-permute-start | bytes 1622024 | tf_op jit(solution)/shard_map/ppermute | solution.py:358
  6.5 1.9 %collective-permute-start.3 = (bf16[528,512]{1,0:T(8,128)(2,1)S(1)}, bf16[528,512]{1,0:T(8,128)(2,1)S(1)}, u32[]{:S(2)}, u32[]{:S(2)}) collective-permute-start(bf16[528,512]{1,0:T(8,128)(2,1)S(1)} %get-tuple-element.27.own), channel_id=1, source_target_pairs={{2,4},{3,5},{4,2},{5,3},{6,8},{7,9},{8,6},{9,7},{10,12},{11,13},{1... | collective-permute-start | bytes 1622024 | tf_op jit(solution)/shard_map/ppermute | solution.py:358
  8.5 1.3 %collective-permute-start.2 = (bf16[528,512]{1,0:T(8,128)(2,1)S(1)}, bf16[528,512]{1,0:T(8,128)(2,1)S(1)}, u32[]{:S(2)}, u32[]{:S(2)}) collective-permute-start(bf16[528,512]{1,0:T(8,128)(2,1)S(1)} %get-tuple-element.27.own), channel_id=1, source_target_pairs={{0,2},{1,3},{2,0},{3,1},{4,6},{5,7},{6,4},{7,5},{8,10},{9,11},{10,... | collective-permute-start | bytes 1622024 | tf_op jit(solution)/shard_map/ppermute | solution.py:358
  9.7 15.1 %collective-permute-done.other = bf16[528,512]{1,0:T(8,128)(2,1)S(1)} collective-permute-done((bf16[528,512]{1,0:T(8,128)(2,1)S(1)}, bf16[528,512]{1,0:T(8,128)(2,1)S(1)}, u32[]{:S(2)}, u32[]{:S(2)}) %collective-permute-start) | collective-permute-done | bytes 540704 | tf_op jit(solution)/shard_map/ppermute | solution.py:358
  24.8 1.9 %collective-permute-start.5 = (bf16[528,512]{1,0:T(8,128)(2,1)S(1)}, bf16[528,512]{1,0:T(8,128)(2,1)S(1)}, u32[]{:S(2)}, u32[]{:S(2)}) collective-permute-start(bf16[528,512]{1,0:T(8,128)(2,1)S(1)} %collective-permute-done.other), channel_id=1, source_target_pairs={{2,4},{3,5},{4,2},{5,3},{6,8},{7,9},{8,6},{9,7},{10,12},{11,13},{1... | collective-permute-start | bytes 1622024 | tf_op jit(solution)/shard_map/ppermute | solution.py:358
  26.8 0.1 collective-permute-start.4
  26.9 3.1 %collective-permute-start.1 = (bf16[512,512]{1,0:T(8,128)(2,1)S(1)}, bf16[512,512]{1,0:T(8,128)(2,1)S(1)}, u32[]{:S(2)}, u32[]{:S(2)}) collective-permute-start(bf16[512,512]{1,0:T(8,128)(2,1)S(1)} %get-tuple-element.26), channel_id=1, source_target_pairs={{0,1},{1,0},{2,3},{3,2},{4,5},{5,4},{6,7},{7,6},{8,9},{9,8},{10,11... | collective-permute-start | bytes 1572872 | tf_op jit(solution)/shard_map/ppermute | solution.py:358
  30.0 0.0 collective-permute-done.3.near_2
  30.0 0.0 collective-permute-done.2.near_1
  30.0 5.4 %near_tiles.1 = (f32[256,512]{1,0:T(8,128)S(1)}, f32[256,512]{1,0:T(8,128)S(1)}, f32[256,512]{1,0:T(8,128)S(1)}, f32[256,512]{1,0:T(8,128)S(1)}, f32[512,512]{1,0:T(8,128)S(1)}) custom-call(bf16[512,512]{1,0:T(8,128)(2,1)S(1)} %get-tuple-element.23.kv, bf16[528,512]{1,0:T(8,128)(2,1)S(1)} %get-tuple-element.27.own, ...), custom_call_target="tpu_custom_call" | custom-call | tf_op jit(solution)/shard_map/near_tiles/pallas_call | solution.py:200
  35.4 10.7 %collective-permute-done.1.kv_other = bf16[512,512]{1,0:T(8,128)(2,1)S(1)} collective-permute-done((bf16[512,512]{1,0:T(8,128)(2,1)S(1)}, bf16[512,512]{1,0:T(8,128)(2,1)S(1)}, u32[]{:S(2)}, u32[]{:S(2)}) %collective-permute-start.1) | collective-permute-done | bytes 524320 | tf_op jit(solution)/shard_map/ppermute | solution.py:358
  46.1 0.0 collective-permute-done.5.far_2
  46.1 0.0 collective-permute-done.4.far_1
  46.1 9.0 %far_tiles.1 = (f32[256,512]{1,0:T(8,128)S(1)}, f32[256,512]{1,0:T(8,128)S(1)}, bf16[512,512]{1,0:T(8,128)(2,1)S(1)}, bf16[512,512]{1,0:T(8,128)(2,1)S(1)}, bf16...) custom-call(s32[2]{0:T(128)S(1)} %pad_add_fusion.x_ref.place_ref, bf16[512,512]{1,0:T(8,128)(2,1)S(1)} %get-tuple-element.23.kv, ...), custom_call_target="tpu_custom_call" | custom-call | tf_op jit(solution)/shard_map/far_tiles/pallas_call | solution.py:257
  55.1 0.1 collective-permute-start.6
  55.2 1.9 %collective-permute-start.7 = (bf16[512,512]{1,0:T(8,128)(2,1)S(1)}, bf16[512,512]{1,0:T(8,128)(2,1)S(1)}, u32[]{:S(2)}, u32[]{:S(2)}) collective-permute-start(bf16[512,512]{1,0:T(8,128)(2,1)S(1)} %get-tuple-element.36), channel_id=1, source_target_pairs={{2,4},{3,5},{4,2},{5,3},{6,8},{7,9},{8,6},{9,7},{10,12},{11,13},{1... | collective-permute-start | bytes 1572872 | tf_op jit(solution)/shard_map/ppermute | solution.py:358
  57.1 0.7 collective-permute-start.9
  57.8 11.2 %collective-permute-done.6.back_a = bf16[512,512]{1,0:T(8,128)(2,1)S(1)} collective-permute-done((bf16[512,512]{1,0:T(8,128)(2,1)S(1)}, bf16[512,512]{1,0:T(8,128)(2,1)S(1)}, u32[]{:S(2)}, u32[]{:S(2)}) %collective-permute-start.6) | collective-permute-done | bytes 524320 | tf_op jit(solution)/shard_map/ppermute | solution.py:358
  69.0 3.5 %collective-permute-done.7.back_b = bf16[512,512]{1,0:T(8,128)(2,1)S(1)} collective-permute-done((bf16[512,512]{1,0:T(8,128)(2,1)S(1)}, bf16[512,512]{1,0:T(8,128)(2,1)S(1)}, u32[]{:S(2)}, u32[]{:S(2)}) %collective-permute-start.7) | collective-permute-done | bytes 524320 | tf_op jit(solution)/shard_map/ppermute | solution.py:358
  72.5 0.1 sum_other.1
  72.6 0.7 collective-permute-start.8
  73.3 2.9 %collective-permute-done.9.dkv_other = bf16[512,512]{1,0:T(8,128)(2,1)S(1)} collective-permute-done((bf16[512,512]{1,0:T(8,128)(2,1)S(1)}, bf16[512,512]{1,0:T(8,128)(2,1)S(1)}, u32[]{:S(2)}, u32[]{:S(2)}) %collective-permute-start.9) | collective-permute-done | bytes 524320 | tf_op jit(solution)/shard_map/ppermute | solution.py:358
  76.2 1.6 %finish.1 = (bf16[256,1024]{1,0:T(8,128)(2,1)}, bf16[256,1024]{1,0:T(8,128)(2,1)}, bf16[256,1024]{1,0:T(8,128)(2,1)}) custom-call(s32[2]{0:T(128)S(1)} %pad_add_fusion.x_ref.place_ref, f32[256,512]{1,0:T(8,128)S(1)} %get-tuple-element.37.dq_own, bf16[512,512]{1,0:T(8,128)(2,1)S(1)} %collective-permute-done.6.back_a, ...), custom_call_target="tpu_custom_call" | custom-call | tf_op jit(solution)/shard_map/finish/pallas_call | solution.py:312
  77.8 3.9 %collective-permute-done.8.part = bf16[256,512]{1,0:T(8,128)(2,1)S(1)} collective-permute-done((bf16[256,512]{1,0:T(8,128)(2,1)S(1)}, bf16[256,512]{1,0:T(8,128)(2,1)S(1)}, u32[]{:S(2)}, u32[]{:S(2)}) %collective-permute-start.8) | collective-permute-done | bytes 262176 | tf_op jit(solution)/shard_map/ppermute | solution.py:358
  81.7 1.3 %place.1 = bf16[256,1024]{1,0:T(8,128)(2,1)} custom-call(s32[2]{0:T(128)S(1)} %pad_add_fusion.x_ref.place_ref, bf16[256,512]{1,0:T(8,128)(2,1)S(1)} %collective-permute-done.8.part, bf16[256,1024]{1,0:T(8,128)(2,1)} %get-tuple-element.40._), custom_call_target="tpu_custom_call", output_to_operand_aliasing={{}: (2, {})} | custom-call | tf_op jit(solution)/shard_map/place/pallas_call | solution.py:332
Async XLA Ops:
  3.4 21.4 %collective-permute-start = (bf16[528,512]{1,0:T(8,128)(2,1)S(1)}, bf16[528,512]{1,0:T(8,128)(2,1)S(1)}, u32[]{:S(2)}, u32[]{:S(2)}) collective-permute-start(bf16[528,512]{1,0:T(8,128)(2,1)S(1)} %get-tuple-element.25), channel_id=1, source_target_pairs={{0,1},{1,0},{2,3},{3,2},{4,5},{5,4},{6,7},{7,6},{8,9},{9,8},{10,11... | collective-permute-start | bytes 1622024 | tf_op jit(solution)/shard_map/ppermute | solution.py:358
  6.5 23.4 %collective-permute-start.3 = (bf16[528,512]{1,0:T(8,128)(2,1)S(1)}, bf16[528,512]{1,0:T(8,128)(2,1)S(1)}, u32[]{:S(2)}, u32[]{:S(2)}) collective-permute-start(bf16[528,512]{1,0:T(8,128)(2,1)S(1)} %get-tuple-element.27.own), channel_id=1, source_target_pairs={{2,4},{3,5},{4,2},{5,3},{6,8},{7,9},{8,6},{9,7},{10,12},{11,13},{1... | collective-permute-start | bytes 1622024 | tf_op jit(solution)/shard_map/ppermute | solution.py:358
  8.5 21.5 %collective-permute-start.2 = (bf16[528,512]{1,0:T(8,128)(2,1)S(1)}, bf16[528,512]{1,0:T(8,128)(2,1)S(1)}, u32[]{:S(2)}, u32[]{:S(2)}) collective-permute-start(bf16[528,512]{1,0:T(8,128)(2,1)S(1)} %get-tuple-element.27.own), channel_id=1, source_target_pairs={{0,2},{1,3},{2,0},{3,1},{4,6},{5,7},{6,4},{7,5},{8,10},{9,11},{10,... | collective-permute-start | bytes 1622024 | tf_op jit(solution)/shard_map/ppermute | solution.py:358
  24.8 21.2 %collective-permute-start.5 = (bf16[528,512]{1,0:T(8,128)(2,1)S(1)}, bf16[528,512]{1,0:T(8,128)(2,1)S(1)}, u32[]{:S(2)}, u32[]{:S(2)}) collective-permute-start(bf16[528,512]{1,0:T(8,128)(2,1)S(1)} %collective-permute-done.other), channel_id=1, source_target_pairs={{2,4},{3,5},{4,2},{5,3},{6,8},{7,9},{8,6},{9,7},{10,12},{11,13},{1... | collective-permute-start | bytes 1622024 | tf_op jit(solution)/shard_map/ppermute | solution.py:358
  26.8 19.3 %collective-permute-start.4 = (bf16[528,512]{1,0:T(8,128)(2,1)S(1)}, bf16[528,512]{1,0:T(8,128)(2,1)S(1)}, u32[]{:S(2)}, u32[]{:S(2)}) collective-permute-start(bf16[528,512]{1,0:T(8,128)(2,1)S(1)} %collective-permute-done.other), channel_id=1, source_target_pairs={{0,2},{1,3},{2,0},{3,1},{4,6},{5,7},{6,4},{7,5},{8,10},{9,11},{10,... | collective-permute-start | bytes 1622024 | tf_op jit(solution)/shard_map/ppermute | solution.py:358
  26.9 19.2 %collective-permute-start.1 = (bf16[512,512]{1,0:T(8,128)(2,1)S(1)}, bf16[512,512]{1,0:T(8,128)(2,1)S(1)}, u32[]{:S(2)}, u32[]{:S(2)}) collective-permute-start(bf16[512,512]{1,0:T(8,128)(2,1)S(1)} %get-tuple-element.26), channel_id=1, source_target_pairs={{0,1},{1,0},{2,3},{3,2},{4,5},{5,4},{6,7},{7,6},{8,9},{9,8},{10,11... | collective-permute-start | bytes 1572872 | tf_op jit(solution)/shard_map/ppermute | solution.py:358
  55.1 13.9 %collective-permute-start.6 = (bf16[512,512]{1,0:T(8,128)(2,1)S(1)}, bf16[512,512]{1,0:T(8,128)(2,1)S(1)}, u32[]{:S(2)}, u32[]{:S(2)}) collective-permute-start(bf16[512,512]{1,0:T(8,128)(2,1)S(1)} %get-tuple-element.35), channel_id=1, source_target_pairs={{0,2},{1,3},{2,0},{3,1},{4,6},{5,7},{6,4},{7,5},{8,10},{9,11},{10,... | collective-permute-start | bytes 1572872 | tf_op jit(solution)/shard_map/ppermute | solution.py:358
  55.2 17.3 %collective-permute-start.7 = (bf16[512,512]{1,0:T(8,128)(2,1)S(1)}, bf16[512,512]{1,0:T(8,128)(2,1)S(1)}, u32[]{:S(2)}, u32[]{:S(2)}) collective-permute-start(bf16[512,512]{1,0:T(8,128)(2,1)S(1)} %get-tuple-element.36), channel_id=1, source_target_pairs={{2,4},{3,5},{4,2},{5,3},{6,8},{7,9},{8,6},{9,7},{10,12},{11,13},{1... | collective-permute-start | bytes 1572872 | tf_op jit(solution)/shard_map/ppermute | solution.py:358
  57.1 19.0 %collective-permute-start.9 = (bf16[512,512]{1,0:T(8,128)(2,1)S(1)}, bf16[512,512]{1,0:T(8,128)(2,1)S(1)}, u32[]{:S(2)}, u32[]{:S(2)}) collective-permute-start(bf16[512,512]{1,0:T(8,128)(2,1)S(1)} %get-tuple-element.39), channel_id=1, source_target_pairs={{0,1},{1,0},{2,3},{3,2},{4,5},{5,4},{6,7},{7,6},{8,9},{9,8},{10,11... | collective-permute-start | bytes 1572872 | tf_op jit(solution)/shard_map/ppermute | solution.py:358
  72.6 9.1 %collective-permute-start.8 = (bf16[256,512]{1,0:T(8,128)(2,1)S(1)}, bf16[256,512]{1,0:T(8,128)(2,1)S(1)}, u32[]{:S(2)}, u32[]{:S(2)}) collective-permute-start(bf16[256,512]{1,0:T(8,128)(2,1)S(1)} %sum_other.1), channel_id=1, source_target_pairs={{0,1},{1,0},{2,3},{3,2},{4,5},{5,4},{6,7},{7,6},{8,9},{9,8},{10,11... | collective-permute-start | bytes 786440 | tf_op jit(solution)/shard_map/ppermute | solution.py:358

commit v3 on v2

--- a/solution.py
+++ b/solution.py
@@ -10,6 +10,7 @@
 AXES = ("outer", "inner")
 LANES = 128
 LOG2E = 1.4426950408889634
+PAD = 16
 WHOLE = pl.BlockSpec(memory_space=pltpu.VMEM)
 IN_HBM = pl.BlockSpec(memory_space=pltpu.HBM)
 PARAMS = pltpu.CompilerParams(vmem_limit_bytes=16 * 1024 * 1024)
@@ -48,6 +49,7 @@
     for copy in copies[0] + copies[1] + later:
         copy.start()
     norm_copy.wait()
+    kv_other[2 * rows :] = jnp.zeros((PAD, half), kv_other.dtype)
     row = lax.broadcasted_iota(jnp.int32, (8, LANES), 0)
     lane = lax.broadcasted_iota(jnp.int32, (8, LANES), 1)
     pick = jnp.where(row == lane // (LANES // 2), 1.0, 0.0).astype(jnp.bfloat16)
@@ -78,11 +80,12 @@
     rows, width = q.shape
     msg = jax.ShapeDtypeStruct((2 * rows + 16, width // 2), jnp.bfloat16)
     kv = jax.ShapeDtypeStruct((2 * rows, width // 2), jnp.bfloat16)
+    kv_sent = jax.ShapeDtypeStruct((2 * rows + PAD, width // 2), jnp.bfloat16)
     return pl.pallas_call(
         pack_kernel,
         in_specs=[pl.BlockSpec(memory_space=pltpu.SMEM)] + [IN_HBM] * 6,
         out_specs=[WHOLE] * 4,
-        out_shape=[msg, kv, msg, kv],
+        out_shape=[msg, kv, msg, kv_sent],
         scratch_shapes=[
             pltpu.VMEM((2, rows, width // 2), jnp.bfloat16),
             pltpu.VMEM(norms.shape, jnp.float32),
@@ -95,8 +98,7 @@
 
 
 def run_tiles(kv_refs, msg_refs, pairs, dq_in, dkv_in, dq_out, dkv_out, scale):
-    rows, width = next(iter(kv_refs.values())).shape
-    rows //= 2
+    rows, width = next(iter(dq_out.values())).shape
     half = LANES // 2
     masks = head_masks(jnp.bfloat16)
     key_side, query_side = {}, {}
@@ -207,64 +209,93 @@
     )(kv, own, other, near_1, near_2)
 
 
+def mid_kernel(
+    sides_ref, kv_other, own, other, near_1, near_2, dq_own, dq_other, dq_1, dq_2,
+    out_own, out_other, back_near_a, back_near_b, dkv_other, near_b, dq_b, *, scale
+):
+    def sort(a, b):
+        near_b[...] = b[0][...]
+        dq_b[...] = b[1][...]
+        back_near_a[...] = (a[1][...] * scale).astype(back_near_a.dtype)
+
+    pl.when(sides_ref[0] == 1)(lambda: sort((near_1, dq_1), (near_2, dq_2)))
+    pl.when(sides_ref[0] != 1)(lambda: sort((near_2, dq_2), (near_1, dq_1)))
+    run_tiles(
+        {"other": kv_other},
+        {"own": own, "other": other, "near_b": near_b},
+        [("other", t) for t in ("own", "other", "near_b")],
+        {"own": dq_own, "other": dq_other, "near_b": dq_b},
+        {},
+        {"own": out_own, "other": out_other, "near_b": back_near_b},
+        {"other": dkv_other},
+        scale,
+    )
+
+
+def mid_tiles(sides, *operands, scale):
+    msg, part_dq = operands[1], operands[5]
+    rows, width = part_dq.shape
+    part = jax.ShapeDtypeStruct((rows, width), jnp.float32)
+    done = jax.ShapeDtypeStruct((rows, width), jnp.bfloat16)
+    return pl.pallas_call(
+        functools.partial(mid_kernel, scale=scale),
+        in_specs=[pl.BlockSpec(memory_space=pltpu.SMEM)] + [WHOLE] * len(operands),
+        out_specs=[WHOLE] * 5,
+        out_shape=[part, part, done, done, jax.ShapeDtypeStruct((2 * rows, width), jnp.float32)],
+        scratch_shapes=[pltpu.VMEM(msg.shape, msg.dtype), pltpu.VMEM(part.shape, part.dtype)],
+        compiler_params=PARAMS,
+        name="mid_tiles",
+    )(sides, *operands)
+
+
 def far_kernel(
-    place_ref, kv, kv_other, own, other, near_1, near_2, far_1, far_2, dq_own, dq_other, dq_1, dq_2, dkv,
-    out_own, out_other, back_1, back_2, dkv_own, dkv_other, near_b, far_a, far_b, dq_b, back_a, back_b, *, scale
+    sides_ref, kv, kv_other, far_1, far_2, back_near_a, back_near_b, dkv, dkv_part,
+    back_1, back_2, dkv_own, dkv_other, far_a, far_b, back_a, back_b, *, scale
 ):
-    rows = dq_1.shape[0]
-
-    def sort(sides):
-        (near_a_in, far_a_in, dq_a_in), (near_b_in, far_b_in, dq_b_in) = sides
-        near_b[...] = near_b_in[...]
-        far_a[...] = far_a_in[...]
-        far_b[...] = far_b_in[...]
-        dq_b[...] = dq_b_in[...]
-        back_a[0:rows] = (dq_a_in[...] * scale).astype(back_a.dtype)
-
-    first, second = (near_1, far_1, dq_1), (near_2, far_2, dq_2)
-    pl.when(place_ref[1] == 1)(lambda: sort((first, second)))
-    pl.when(place_ref[1] != 1)(lambda: sort((second, first)))
+    rows = back_near_a.shape[0]
+
+    def sort(a, b):
+        far_a[...] = a[...]
+        far_b[...] = b[...]
+
+    pl.when(sides_ref[0] == 1)(lambda: sort(far_1, far_2))
+    pl.when(sides_ref[0] != 1)(lambda: sort(far_2, far_1))
     run_tiles(
         {"own": kv, "other": kv_other},
-        {"own": own, "other": other, "near_b": near_b, "far_a": far_a, "far_b": far_b},
-        [("other", "near_b"), ("other", "far_b"), ("other", "far_a"), ("own", "far_a"), ("other", "own"), ("other", "other")],
-        {"own": dq_own, "other": dq_other, "near_b": dq_b},
-        {"own": dkv},
-        {
-            "own": out_own,
-            "other": out_other,
-            "near_b": back_b.at[0:rows],
-            "far_a": back_a.at[rows : 2 * rows],
-            "far_b": back_b.at[rows : 2 * rows],
-        },
+        {"far_a": far_a, "far_b": far_b},
+        [("other", "far_b"), ("other", "far_a"), ("own", "far_a")],
+        {},
+        {"own": dkv, "other": dkv_part},
+        {"far_a": back_a, "far_b": back_b},
         {"own": dkv_own, "other": dkv_other},
         scale,
     )
 
+    dkv_other[2 * rows :] = jnp.zeros((PAD, dkv_other.shape[1]), dkv_other.dtype)
+
     def unsort(out_a, out_b):
-        out_a[...] = back_a[...]
-        out_b[...] = back_b[...]
-
-    pl.when(place_ref[1] == 1)(lambda: unsort(back_1, back_2))
-    pl.when(place_ref[1] != 1)(lambda: unsort(back_2, back_1))
-
-
-def far_tiles(x, *operands, scale):
-    kv, msg = operands[0], operands[2]
-    rows, width = kv.shape[0] // 2, kv.shape[1]
-    part = jax.ShapeDtypeStruct((rows, width), jnp.float32)
+        out_a[0:rows] = back_near_a[...]
+        out_b[0:rows] = back_near_b[...]
+        out_a[rows : 2 * rows] = back_a[...]
+        out_b[rows : 2 * rows] = back_b[...]
+
+    pl.when(sides_ref[0] == 1)(lambda: unsort(back_1, back_2))
+    pl.when(sides_ref[0] != 1)(lambda: unsort(back_2, back_1))
+
+
+def far_tiles(sides, *operands, scale):
+    kv, msg, part = operands[0], operands[2], operands[4]
     done = jax.ShapeDtypeStruct(kv.shape, jnp.bfloat16)
     return pl.pallas_call(
         functools.partial(far_kernel, scale=scale),
         in_specs=[pl.BlockSpec(memory_space=pltpu.SMEM)] + [WHOLE] * len(operands),
-        out_specs=[WHOLE] * 6,
-        out_shape=[part, part] + [done] * 4,
-        scratch_shapes=[pltpu.VMEM(msg.shape, msg.dtype)] * 3
-        + [pltpu.VMEM(part.shape, part.dtype)]
-        + [pltpu.VMEM(done.shape, done.dtype)] * 2,
+        out_specs=[WHOLE] * 4,
+        out_shape=[done] * 3 + [jax.ShapeDtypeStruct((kv.shape[0] + PAD, kv.shape[1]), jnp.bfloat16)],
+        scratch_shapes=[pltpu.VMEM(msg.shape, msg.dtype)] * 2
+        + [pltpu.VMEM(part.shape, part.dtype)] * 2,
         compiler_params=PARAMS,
         name="far_tiles",
-    )(x, *operands)
+    )(sides, *operands)
 
 
 def sum_other_kernel(dq, back_a, back_b, out, *, scale):
@@ -345,7 +376,8 @@
     count = lax.axis_size("outer") * lax.axis_size("inner")
     index = lax.axis_index("outer") * lax.axis_size("inner") + lax.axis_index("inner")
     column, row = index % 2, index // 2 % 2
-    x = jnp.stack([column, column ^ row]).astype(jnp.int32)
+    x = column.astype(jnp.int32).reshape(1)
+    sides = (column ^ row).astype(jnp.int32).reshape(1)
     head_size = query_rows.shape[1] // log_norms.shape[0]
     scale = head_size ** (-0.5)
 
@@ -366,9 +398,11 @@
     kv_other = send(kv_to_other, swap)
     far_1, far_2 = send(other, step_1), send(other, step_2)
     dq_own, dq_other, dq_1, dq_2, dkv = near_tiles(kv_own, own, other, near_1, near_2, scale)
-    dq_own, dq_other, to_1, to_2, dkv_own, dkv_to_other = far_tiles(
-        x, kv_own, kv_other, own, other, near_1, near_2, far_1, far_2,
-        dq_own, dq_other, dq_1, dq_2, dkv, scale=scale,
+    dq_own, dq_other, back_near_a, back_near_b, dkv_part = mid_tiles(
+        sides, kv_other, own, other, near_1, near_2, dq_own, dq_other, dq_1, dq_2, scale=scale
+    )
+    to_1, to_2, dkv_own, dkv_to_other = far_tiles(
+        sides, kv_own, kv_other, far_1, far_2, back_near_a, back_near_b, dkv, dkv_part, scale=scale
     )
     dkv_other = send(dkv_to_other, swap)
     back_1, back_2 = send(to_1, step_1), send(to_2, step_2)

time: 83.3 us -> 81.3 us (0.976)
  waiting for transfers between devices: 47.3 us -> 41 us
  starting transfers between devices: 14.7 us -> 19.1 us
    ppermute x10, waiting for transfers between devices: 47.3 us -> 41 us  [send(): return lax.ppermute(a, AXES, perm)]
    ppermute x10, starting transfers between devices: 14.7 us -> 19.1 us  [send(): return lax.ppermute(a, AXES, perm)]
    pallas_call x0 -> x1, Pallas kernels: none -> 4.3 us  [mid_tiles(): pl.pallas_call(functools.partial(mid_kernel, scale=scale), in_specs=[pl.B...]
    pallas_call x1, Pallas kernels: 9 us -> 5.4 us  [far_tiles(): pl.pallas_call(functools.partial(far_kernel, scale=scale), in_specs=[pl.B...]
  transfers between devices with their start and end apart: 10 -> 10, of which waited for: 6 -> 5; matrix products, arithmetic and copies ran while one was open for 0% -> 0% of each run, Pallas kernels for 9% -> 13%
where the time goes in v3:
time: 81.3 us; the launch traced here: 80.9 us
  waiting for transfers between devices  41 us (50%)
  Pallas kernels  19.8 us (24%)
  starting transfers between devices  19.1 us (23%)
  between operations  0.95 us (1%)
    ppermute x10, waiting for transfers between devices, send(): return lax.ppermute(a, AXES, perm)  41 us
    ppermute x10, starting transfers between devices, send(): return lax.ppermute(a, AXES, perm)  19.1 us
    pallas_call x1, Pallas kernels, far_tiles(): pl.pallas_call(functools.partial(far_kernel, scale=scale), in_specs=[pl.B...  5.4 us
    pallas_call x1, Pallas kernels, near_tiles(): pl.pallas_call(functools.partial(near_kernel, scale=scale), in_specs=[WHO...  5.26 us
    pallas_call x1, Pallas kernels, mid_tiles(): pl.pallas_call(functools.partial(mid_kernel, scale=scale), in_specs=[pl.B...  4.3 us
    pallas_call x1, Pallas kernels, pack(): pl.pallas_call(pack_kernel, in_specs=[pl.BlockSpec(memory_space=pltpu.SME...  2.95 us
  transfers between devices with their start and end apart: 10, of which 5 were waited for; matrix products, arithmetic and copies ran while one was open for 0% of the time, Pallas kernels for 13%

profile of v3, /device:TPU:24, one launch (start us, length us, event | category | flops | bytes accessed | tf_op | source)
XLA Modules:
  0.0 80.9 jit_solution(302343560637570258)
XLA Ops:
  0.6 2.9 %pack.1 = (bf16[528,512]{1,0:T(8,128)(2,1)S(1)}, bf16[512,512]{1,0:T(8,128)(2,1)S(1)}, bf16[528,512]{1,0:T(8,128)(2,1)S(1)}, bf16[528,512]{1,0:T(8,128)(2,1)}) custom-call(s32[1]{0:T(128)} %bitcast.x_ref, bf16[256,1024]{1,0:T(8,128)(2,1)} %q.1, bf16[256,1024]{1,0:T(8,128)(2,1)} %k.1, bf16[256,1024]{1,0:T(8,128)(2,1)} %v.1, bf16[256,1024]{1,0:T(8,128)(2,1)} %o.1, ...), custom_call_target="tpu_custom_call" | custom-call | tf_op jit(solution)/shard_map/pack/pallas_call | solution.py:84
  3.6 3.1 %collective-permute-start = (bf16[528,512]{1,0:T(8,128)(2,1)S(1)}, bf16[528,512]{1,0:T(8,128)(2,1)S(1)}, u32[]{:S(2)}, u32[]{:S(2)}) collective-permute-start(bf16[528,512]{1,0:T(8,128)(2,1)S(1)} %get-tuple-element.27), channel_id=1, source_target_pairs={{0,1},{1,0},{2,3},{3,2},{4,5},{5,4},{6,7},{7,6},{8,9},{9,8},{10,11... | collective-permute-start | bytes 1622024 | tf_op jit(solution)/shard_map/ppermute | solution.py:390
  6.7 0.7 collective-permute-start.2
  7.4 1.9 %collective-permute-start.3 = (bf16[528,512]{1,0:T(8,128)(2,1)S(1)}, bf16[528,512]{1,0:T(8,128)(2,1)S(1)}, u32[]{:S(2)}, u32[]{:S(2)}) collective-permute-start(bf16[528,512]{1,0:T(8,128)(2,1)S(1)} %get-tuple-element.29.own), channel_id=1, source_target_pairs={{2,4},{3,5},{4,2},{5,3},{6,8},{7,9},{8,6},{9,7},{10,12},{11,13},{1... | collective-permute-start | bytes 1622024 | tf_op jit(solution)/shard_map/ppermute | solution.py:390
  9.4 15.6 %collective-permute-done.other = bf16[528,512]{1,0:T(8,128)(2,1)S(1)} collective-permute-done((bf16[528,512]{1,0:T(8,128)(2,1)S(1)}, bf16[528,512]{1,0:T(8,128)(2,1)S(1)}, u32[]{:S(2)}, u32[]{:S(2)}) %collective-permute-start) | collective-permute-done | bytes 540704 | tf_op jit(solution)/shard_map/ppermute | solution.py:390
  25.0 3.0 %collective-permute-start.1 = (bf16[528,512]{1,0:T(8,128)(2,1)}, bf16[528,512]{1,0:T(8,128)(2,1)S(1)}, u32[]{:S(2)}, u32[]{:S(2)}) collective-permute-start(bf16[528,512]{1,0:T(8,128)(2,1)} %get-tuple-element.28), channel_id=1, source_target_pairs={{0,1},{1,0},{2,3},{3,2},{4,5},{5,4},{6,7},{7,6},{8,9},{9,8},{10,11... | collective-permute-start | bytes 1622024 | tf_op jit(solution)/shard_map/ppermute | solution.py:390
  28.0 0.0 collective-permute-start.4
  28.0 1.9 %collective-permute-start.5 = (bf16[528,512]{1,0:T(8,128)(2,1)S(1)}, bf16[528,512]{1,0:T(8,128)(2,1)}, u32[]{:S(2)}, u32[]{:S(2)}) collective-permute-start(bf16[528,512]{1,0:T(8,128)(2,1)S(1)} %collective-permute-done.other), channel_id=1, source_target_pairs={{2,4},{3,5},{4,2},{5,3},{6,8},{7,9},{8,6},{9,7},{10,12},{11,13},{1... | collective-permute-start | bytes 1622024 | tf_op jit(solution)/shard_map/ppermute | solution.py:390
  30.0 0.0 collective-permute-done.2.near_1
  30.0 0.0 collective-permute-done.3.near_2
  30.0 5.3 %near_tiles.1 = (f32[256,512]{1,0:T(8,128)S(1)}, f32[256,512]{1,0:T(8,128)S(1)}, f32[256,512]{1,0:T(8,128)S(1)}, f32[256,512]{1,0:T(8,128)S(1)}, f32[512,512]{1,0:T(8,128)S(1)}) custom-call(bf16[512,512]{1,0:T(8,128)(2,1)S(1)} %get-tuple-element.31.kv, bf16[528,512]{1,0:T(8,128)(2,1)S(1)} %get-tuple-element.29.own, ...), custom_call_target="tpu_custom_call" | custom-call | tf_op jit(solution)/shard_map/near_tiles/pallas_call | solution.py:202
  35.3 10.4 %collective-permute-done.1.kv_other = bf16[528,512]{1,0:T(8,128)(2,1)S(1)} collective-permute-done((bf16[528,512]{1,0:T(8,128)(2,1)}, bf16[528,512]{1,0:T(8,128)(2,1)S(1)}, u32[]{:S(2)}, u32[]{:S(2)}) %collective-permute-start.1) | collective-permute-done | bytes 540704 | tf_op jit(solution)/shard_map/ppermute | solution.py:390
  45.7 4.3 %mid_tiles.1 = (f32[256,512]{1,0:T(8,128)S(1)}, f32[256,512]{1,0:T(8,128)S(1)}, bf16[256,512]{1,0:T(8,128)(2,1)S(1)}, bf16[256,512]{1,0:T(8,128)(2,1)S(1)}, f32[512,512]{1,0:T(8,128)S(1)}) custom-call(s32[1]{0:T(128)} %bitcast.1.sides_ref, bf16[528,512]{1,0:T(8,128)(2,1)S(1)} %collective-permute-done.1.kv_other, bf16[528,512]{1,0:T(8,128)(2,1)S(1)} %get-tuple-element.29.own, ...), custom_call_target="tpu_custom_call" | custom-call | tf_op jit(solution)/shard_map/mid_tiles/pallas_call | solution.py:240
  50.0 0.0 collective-permute-done.4.far_1
  50.0 0.0 collective-permute-done.5.far_2
  50.0 5.4 %far_tiles.1 = (bf16[512,512]{1,0:T(8,128)(2,1)S(1)}, bf16[512,512]{1,0:T(8,128)(2,1)S(1)}, bf16[512,512]{1,0:T(8,128)(2,1)S(1)}, bf16[528,512]{1,0:T(8,128)(2,1)S(1)}) custom-call(s32[1]{0:T(128)} %bitcast.1.sides_ref, bf16[512,512]{1,0:T(8,128)(2,1)S(1)} %get-tuple-element.31.kv, bf16[528,512]{1,0:T(8,128)(2,1)S(1)} %collective-permute-done.1.kv_other, ...), custom_call_target="tpu_custom_call" | custom-call | tf_op jit(solution)/shard_map/far_tiles/pallas_call | solution.py:289
  55.4 0.1 collective-permute-start.6
  55.5 1.9 %collective-permute-start.7 = (bf16[512,512]{1,0:T(8,128)(2,1)S(1)}, bf16[512,512]{1,0:T(8,128)(2,1)S(1)}, u32[]{:S(2)}, u32[]{:S(2)}) collective-permute-start(bf16[512,512]{1,0:T(8,128)(2,1)S(1)} %get-tuple-element.42), channel_id=1, source_target_pairs={{2,4},{3,5},{4,2},{5,3},{6,8},{7,9},{8,6},{9,7},{10,12},{11,13},{1... | collective-permute-start | bytes 1572872 | tf_op jit(solution)/shard_map/ppermute | solution.py:390
  57.4 3.1 %collective-permute-start.9 = (bf16[528,512]{1,0:T(8,128)(2,1)S(1)}, bf16[528,512]{1,0:T(8,128)(2,1)S(1)}, u32[]{:S(2)}, u32[]{:S(2)}) collective-permute-start(bf16[528,512]{1,0:T(8,128)(2,1)S(1)} %get-tuple-element.45), channel_id=1, source_target_pairs={{0,1},{1,0},{2,3},{3,2},{4,5},{5,4},{6,7},{7,6},{8,9},{9,8},{10,11... | collective-permute-start | bytes 1622024 | tf_op jit(solution)/shard_map/ppermute | solution.py:390
  60.5 6.8 %collective-permute-done.6.back_a = bf16[512,512]{1,0:T(8,128)(2,1)S(1)} collective-permute-done((bf16[512,512]{1,0:T(8,128)(2,1)S(1)}, bf16[512,512]{1,0:T(8,128)(2,1)S(1)}, u32[]{:S(2)}, u32[]{:S(2)}) %collective-permute-start.6) | collective-permute-done | bytes 524320 | tf_op jit(solution)/shard_map/ppermute | solution.py:390
  67.3 4.6 %collective-permute-done.7.back_b = bf16[512,512]{1,0:T(8,128)(2,1)S(1)} collective-permute-done((bf16[512,512]{1,0:T(8,128)(2,1)S(1)}, bf16[512,512]{1,0:T(8,128)(2,1)S(1)}, u32[]{:S(2)}, u32[]{:S(2)}) %collective-permute-start.7) | collective-permute-done | bytes 524320 | tf_op jit(solution)/shard_map/ppermute | solution.py:390
  71.9 0.1 sum_other.1
  72.0 3.4 %collective-permute-start.8 = (bf16[256,512]{1,0:T(8,128)(2,1)S(1)}, bf16[256,512]{1,0:T(8,128)(2,1)S(1)}, u32[]{:S(2)}, u32[]{:S(2)}) collective-permute-start(bf16[256,512]{1,0:T(8,128)(2,1)S(1)} %sum_other.1), channel_id=1, source_target_pairs={{0,1},{1,0},{2,3},{3,2},{4,5},{5,4},{6,7},{7,6},{8,9},{9,8},{10,11... | collective-permute-start | bytes 786440 | tf_op jit(solution)/shard_map/ppermute | solution.py:390
  75.4 0.0 collective-permute-done.9.dkv_other
  75.4 1.1 %finish.1 = (bf16[256,1024]{1,0:T(8,128)(2,1)}, bf16[256,1024]{1,0:T(8,128)(2,1)}, bf16[256,1024]{1,0:T(8,128)(2,1)}) custom-call(s32[1]{0:T(128)} %bitcast.x_ref, f32[256,512]{1,0:T(8,128)S(1)} %get-tuple-element.43.dq_own, bf16[512,512]{1,0:T(8,128)(2,1)S(1)} %collective-permute-done.6.back_a, bf16[512,512]{1,0:T(8,128)(2,1)S(1)} %collective-permute-done.7.back_b, ...), custom_call_target="tpu_custom_call" | custom-call | tf_op jit(solution)/shard_map/finish/pallas_call | solution.py:343
  76.5 3.5 %collective-permute-done.8.part = bf16[256,512]{1,0:T(8,128)(2,1)S(1)} collective-permute-done((bf16[256,512]{1,0:T(8,128)(2,1)S(1)}, bf16[256,512]{1,0:T(8,128)(2,1)S(1)}, u32[]{:S(2)}, u32[]{:S(2)}) %collective-permute-start.8) | collective-permute-done | bytes 262176 | tf_op jit(solution)/shard_map/ppermute | solution.py:390
  80.0 0.7 place.1
Async XLA Ops:
  3.6 21.4 %collective-permute-start = (bf16[528,512]{1,0:T(8,128)(2,1)S(1)}, bf16[528,512]{1,0:T(8,128)(2,1)S(1)}, u32[]{:S(2)}, u32[]{:S(2)}) collective-permute-start(bf16[528,512]{1,0:T(8,128)(2,1)S(1)} %get-tuple-element.27), channel_id=1, source_target_pairs={{0,1},{1,0},{2,3},{3,2},{4,5},{5,4},{6,7},{7,6},{8,9},{9,8},{10,11... | collective-permute-start | bytes 1622024 | tf_op jit(solution)/shard_map/ppermute | solution.py:390
  6.7 23.3 %collective-permute-start.2 = (bf16[528,512]{1,0:T(8,128)(2,1)S(1)}, bf16[528,512]{1,0:T(8,128)(2,1)S(1)}, u32[]{:S(2)}, u32[]{:S(2)}) collective-permute-start(bf16[528,512]{1,0:T(8,128)(2,1)S(1)} %get-tuple-element.29.own), channel_id=1, source_target_pairs={{0,2},{1,3},{2,0},{3,1},{4,6},{5,7},{6,4},{7,5},{8,10},{9,11},{10,... | collective-permute-start | bytes 1622024 | tf_op jit(solution)/shard_map/ppermute | solution.py:390
  7.4 22.5 %collective-permute-start.3 = (bf16[528,512]{1,0:T(8,128)(2,1)S(1)}, bf16[528,512]{1,0:T(8,128)(2,1)S(1)}, u32[]{:S(2)}, u32[]{:S(2)}) collective-permute-start(bf16[528,512]{1,0:T(8,128)(2,1)S(1)} %get-tuple-element.29.own), channel_id=1, source_target_pairs={{2,4},{3,5},{4,2},{5,3},{6,8},{7,9},{8,6},{9,7},{10,12},{11,13},{1... | collective-permute-start | bytes 1622024 | tf_op jit(solution)/shard_map/ppermute | solution.py:390
  25.0 20.7 %collective-permute-start.1 = (bf16[528,512]{1,0:T(8,128)(2,1)}, bf16[528,512]{1,0:T(8,128)(2,1)S(1)}, u32[]{:S(2)}, u32[]{:S(2)}) collective-permute-start(bf16[528,512]{1,0:T(8,128)(2,1)} %get-tuple-element.28), channel_id=1, source_target_pairs={{0,1},{1,0},{2,3},{3,2},{4,5},{5,4},{6,7},{7,6},{8,9},{9,8},{10,11... | collective-permute-start | bytes 1622024 | tf_op jit(solution)/shard_map/ppermute | solution.py:390
  28.0 22.0 %collective-permute-start.4 = (bf16[528,512]{1,0:T(8,128)(2,1)S(1)}, bf16[528,512]{1,0:T(8,128)(2,1)}, u32[]{:S(2)}, u32[]{:S(2)}) collective-permute-start(bf16[528,512]{1,0:T(8,128)(2,1)S(1)} %collective-permute-done.other), channel_id=1, source_target_pairs={{0,2},{1,3},{2,0},{3,1},{4,6},{5,7},{6,4},{7,5},{8,10},{9,11},{10,... | collective-permute-start | bytes 1622024 | tf_op jit(solution)/shard_map/ppermute | solution.py:390
  28.0 22.0 %collective-permute-start.5 = (bf16[528,512]{1,0:T(8,128)(2,1)S(1)}, bf16[528,512]{1,0:T(8,128)(2,1)}, u32[]{:S(2)}, u32[]{:S(2)}) collective-permute-start(bf16[528,512]{1,0:T(8,128)(2,1)S(1)} %collective-permute-done.other), channel_id=1, source_target_pairs={{2,4},{3,5},{4,2},{5,3},{6,8},{7,9},{8,6},{9,7},{10,12},{11,13},{1... | collective-permute-start | bytes 1622024 | tf_op jit(solution)/shard_map/ppermute | solution.py:390
  55.4 11.9 %collective-permute-start.6 = (bf16[512,512]{1,0:T(8,128)(2,1)S(1)}, bf16[512,512]{1,0:T(8,128)(2,1)S(1)}, u32[]{:S(2)}, u32[]{:S(2)}) collective-permute-start(bf16[512,512]{1,0:T(8,128)(2,1)S(1)} %get-tuple-element.41), channel_id=1, source_target_pairs={{0,2},{1,3},{2,0},{3,1},{4,6},{5,7},{6,4},{7,5},{8,10},{9,11},{10,... | collective-permute-start | bytes 1572872 | tf_op jit(solution)/shard_map/ppermute | solution.py:390
  55.5 16.4 %collective-permute-start.7 = (bf16[512,512]{1,0:T(8,128)(2,1)S(1)}, bf16[512,512]{1,0:T(8,128)(2,1)S(1)}, u32[]{:S(2)}, u32[]{:S(2)}) collective-permute-start(bf16[512,512]{1,0:T(8,128)(2,1)S(1)} %get-tuple-element.42), channel_id=1, source_target_pairs={{2,4},{3,5},{4,2},{5,3},{6,8},{7,9},{8,6},{9,7},{10,12},{11,13},{1... | collective-permute-start | bytes 1572872 | tf_op jit(solution)/shard_map/ppermute | solution.py:390
  57.4 18.0 %collective-permute-start.9 = (bf16[528,512]{1,0:T(8,128)(2,1)S(1)}, bf16[528,512]{1,0:T(8,128)(2,1)S(1)}, u32[]{:S(2)}, u32[]{:S(2)}) collective-permute-start(bf16[528,512]{1,0:T(8,128)(2,1)S(1)} %get-tuple-element.45), channel_id=1, source_target_pairs={{0,1},{1,0},{2,3},{3,2},{4,5},{5,4},{6,7},{7,6},{8,9},{9,8},{10,11... | collective-permute-start | bytes 1622024 | tf_op jit(solution)/shard_map/ppermute | solution.py:390
  72.0 8.0 %collective-permute-start.8 = (bf16[256,512]{1,0:T(8,128)(2,1)S(1)}, bf16[256,512]{1,0:T(8,128)(2,1)S(1)}, u32[]{:S(2)}, u32[]{:S(2)}) collective-permute-start(bf16[256,512]{1,0:T(8,128)(2,1)S(1)} %sum_other.1), channel_id=1, source_target_pairs={{0,1},{1,0},{2,3},{3,2},{4,5},{5,4},{6,7},{7,6},{8,9},{9,8},{10,11... | collective-permute-start | bytes 786440 | tf_op jit(solution)/shard_map/ppermute | solution.py:390

commit v4 on v3

v4 whole, which is shorter than its diff:
```python
import functools

import jax
import jax.numpy as jnp
from jax import lax
from jax.experimental import pallas as pl
from jax.experimental.pallas import tpu as pltpu
from jax.sharding import PartitionSpec as P

AXES = ("outer", "inner")
LANES = 128
LOG2E = 1.4426950408889634
PAD = 16
WHOLE = pl.BlockSpec(memory_space=pltpu.VMEM)
IN_HBM = pl.BlockSpec(memory_space=pltpu.HBM)
PARAMS = pltpu.CompilerParams(vmem_limit_bytes=16 * 1024 * 1024)


def dot_nt(a, b):
    return lax.dot_general(a, b, (((1,), (1,)), ((), ())), preferred_element_type=jnp.float32)


def dot_nn(a, b):
    return lax.dot_general(a, b, (((1,), (0,)), ((), ())), preferred_element_type=jnp.float32)


def head_masks(dtype):
    lane = lax.broadcasted_iota(jnp.int32, (1, LANES), 1)
    first = jnp.where(lane < LANES // 2, 1.0, 0.0)
    return first.astype(dtype), (1.0 - first).astype(dtype)


def pack_kernel(x_ref, q, o, g, norms, *refs, other):
    if other:
        k, v, msg, kv, outs, norm_buf, sems = refs
    else:
        msg, outs, norm_buf, sems = refs
    rows, width = q.shape
    half = width // 2
    side = 1 - x_ref[0] if other else x_ref[0]
    columns = pl.ds(pl.multiple_of(side * half, LANES), half)
    moves = [(g.at[:, columns], msg.at[rows : 2 * rows]), (o.at[:, columns], outs), (norms, norm_buf)]
    moves.append((q.at[:, columns], msg.at[0:rows]))
    if other:
        moves += [(k.at[:, columns], kv.at[0:rows]), (v.at[:, columns], kv.at[rows : 2 * rows])]
    copies = [pltpu.make_async_copy(a, b, sems.at[n]) for n, (a, b) in enumerate(moves)]
    for copy in copies:
        copy.start()
    if other:
        kv[2 * rows :] = jnp.zeros((PAD, half), kv.dtype)
    row = lax.broadcasted_iota(jnp.int32, (8, LANES), 0)
    lane = lax.broadcasted_iota(jnp.int32, (8, LANES), 1)
    pick = jnp.where(row == lane // (LANES // 2), 1.0, 0.0).astype(jnp.bfloat16)
    for copy in copies[:3]:
        copy.wait()
    for pair in range(half // LANES):
        span = slice(pair * LANES, (pair + 1) * LANES)
        product = outs[:, span].astype(jnp.float32) * msg[rows : 2 * rows, span].astype(jnp.float32)
        high = product.astype(jnp.bfloat16)
        low = (product - high.astype(jnp.float32)).astype(jnp.bfloat16)
        delta = dot_nt(pick, high) + dot_nt(pick, low)
        first = 2 * (side * (half // LANES) + pair)
        terms = jnp.concatenate(
            [norm_buf[pl.ds(first, 1), :], norm_buf[pl.ds(first + 1, 1), :], delta[0:2]], axis=0
        )
        terms_high = terms.astype(jnp.bfloat16).astype(jnp.float32)
        both = jnp.concatenate([terms_high, terms - terms_high], axis=0)
        msg[2 * rows : 2 * rows + 16, span] = jnp.concatenate(
            [both[:, :LANES], both[:, LANES:]], axis=0
        ).astype(jnp.bfloat16)
    for copy in copies[3:]:
        copy.wait()


def pack(x, q, o, g, norms, *kv, name):
    rows, width = q.shape
    shapes = [jax.ShapeDtypeStruct((2 * rows + 16, width // 2), jnp.bfloat16)]
    if kv:
        shapes.append(jax.ShapeDtypeStruct((2 * rows + PAD, width // 2), jnp.bfloat16))
    operands = [pltpu.with_memory_space_constraint(a, pltpu.HBM) for a in (q, o, g, norms, *kv)]
    return pl.pallas_call(
        functools.partial(pack_kernel, other=bool(kv)),
        in_specs=[pl.BlockSpec(memory_space=pltpu.SMEM)] + [IN_HBM] * len(operands),
        out_specs=[WHOLE] * len(shapes),
        out_shape=shapes,
        scratch_shapes=[
            pltpu.VMEM((rows, width // 2), jnp.bfloat16),
            pltpu.VMEM(norms.shape, jnp.float32),
            pltpu.SemaphoreType.DMA((len(operands),)),
        ],
        compiler_params=PARAMS,
        name=name,
    )(x, *operands)


def load(source, rows, columns):
    if not isinstance(source, tuple):
        return source[rows, columns]
    flag, first, second = source
    return jnp.where(flag, first[rows, columns], second[rows, columns])


def run_tiles(kv_refs, msg_refs, pairs, dq_in, dkv_in, dq_out, dkv_out, scale):
    rows, width = next(iter(dq_out.values())).shape
    half = LANES // 2
    masks = head_masks(jnp.bfloat16)
    key_side, query_side = {}, {}

    def span(group):
        return slice(group * LANES, (group + 1) * LANES)

    def keys_of(u, group):
        if (u, group) not in key_side:
            k, v = kv_refs[u][0:rows, span(group)], kv_refs[u][rows : 2 * rows, span(group)]
            kt = k.T
            sums = [None, None]
            if u in dkv_in:
                sums = [dkv_in[u][0:rows, span(group)], dkv_in[u][rows : 2 * rows, span(group)]]
            key_side[u, group] = (k, v, [kt[0:half], kt[half:LANES]], sums)
        return key_side[u, group]

    def queries_of(t, group):
        if (t, group) not in query_side:
            q = load(msg_refs[t], slice(0, rows), span(group))
            g = load(msg_refs[t], slice(rows, 2 * rows), span(group))
            info = load(msg_refs[t], slice(2 * rows, 2 * rows + 16), span(group)).astype(jnp.float32)
            both = jnp.concatenate([info[0:8], info[8:16]], axis=1)
            terms = both[0:4] + both[4:8]
            query_side[t, group] = (
                [q * m for m in masks],
                [g * m for m in masks],
                terms[0:2] * LOG2E,
                terms[2:4],
                [None, None],
            )
        return query_side[t, group]

    def plus(a, b):
        return b if a is None else a + b

    items = [(group, u, t, h) for group in range(width // LANES) for u, t in pairs for h in range(2)]
    last_of = {}
    for group, u, t, h in items:
        last_of["key", u, group] = last_of["query", t, group] = (group, u, t, h)

    def products(item):
        group, u, t, h = item
        k, v, _, _ = keys_of(u, group)
        qs, gs = queries_of(t, group)[:2]
        return dot_nt(k, qs[h]), dot_nt(v, gs[h])

    def weigh(item, scores, grad_prob):
        group, u, t, h = item
        _, _, norms, deltas, _ = queries_of(t, group)
        probs = jnp.exp2(scores * (scale * LOG2E) - norms[h : h + 1])
        grad_score = probs * (grad_prob - deltas[h : h + 1])
        return probs.astype(jnp.bfloat16), grad_score.astype(jnp.bfloat16)

    def add_up(item, weights, grad_score):
        group, u, t, h = item
        _, _, kt, sums = keys_of(u, group)
        qs, gs, _, _, dq = queries_of(t, group)
        sums[1] = plus(sums[1], dot_nn(weights, gs[h]))
        sums[0] = plus(sums[0], dot_nn(grad_score, qs[h]))
        dq[h] = plus(dq[h], dot_nn(kt[h], grad_score))
        if last_of["query", t, group] == item:
            total = jnp.concatenate(dq, axis=0).T
            if t in dq_in:
                total = total + load(dq_in[t], slice(0, rows), span(group))
            ref = dq_out[t]
            final = ref.dtype == jnp.bfloat16
            ref[:, span(group)] = (total * scale if final else total).astype(ref.dtype)
        if last_of["key", u, group] == item:
            ref = dkv_out[u]
            final = ref.dtype == jnp.bfloat16
            ref[0:rows, span(group)] = (sums[0] * scale if final else sums[0]).astype(ref.dtype)
            ref[rows : 2 * rows, span(group)] = sums[1].astype(ref.dtype)

    made, weighed = {}, {}
    for step in range(len(items) + 2):
        if step < len(items):
            made[step] = products(items[step])
        if 0 <= step - 1 < len(items):
            weighed[step - 1] = weigh(items[step - 1], *made.pop(step - 1))
        if 0 <= step - 2:
            add_up(items[step - 2], *weighed.pop(step - 2))


def near_kernel(
    x_ref, k, v, own, other, near_1, near_2,
    dq_own, dq_other, dq_1, dq_2, dkv, kv, sems, *, scale
):
    rows, half = dq_own.shape
    columns = pl.ds(pl.multiple_of(x_ref[0] * half, LANES), half)
    moves = ((k, kv.at[0:rows]), (v, kv.at[rows : 2 * rows]))
    copies = [pltpu.make_async_copy(a.at[:, columns], b, sems.at[n]) for n, (a, b) in enumerate(moves)]
    for copy in copies:
        copy.start()
    for copy in copies:
        copy.wait()
    run_tiles(
        {"own": kv},
        {"own": own, "other": other, "1": near_1, "2": near_2},
        [("own", t) for t in ("own", "other", "1", "2")],
        {},
        {},
        {"own": dq_own, "other": dq_other, "1": dq_1, "2": dq_2},
        {"own": dkv},
        scale,
    )


def near_tiles(x, k, v, *msgs, scale):
    rows, width = k.shape[0], k.shape[1] // 2
    part = jax.ShapeDtypeStruct((rows, width), jnp.float32)
    sums = jax.ShapeDtypeStruct((2 * rows, width), jnp.float32)
    kv = jax.ShapeDtypeStruct((2 * rows, width), jnp.bfloat16)
    return pl.pallas_call(
        functools.partial(near_kernel, scale=scale),
        in_specs=[pl.BlockSpec(memory_space=pltpu.SMEM)] + [IN_HBM] * 2 + [WHOLE] * len(msgs),
        out_specs=[WHOLE] * 6,
        out_shape=[part] * 4 + [sums, kv],
        scratch_shapes=[pltpu.SemaphoreType.DMA((2,))],
        compiler_params=PARAMS,
        name="near_tiles",
    )(x, *(pltpu.with_memory_space_constraint(a, pltpu.HBM) for a in (k, v)), *msgs)


def mid_kernel(
    sides_ref, kv_other, own, other, near_1, near_2, dq_own, dq_other, dq_1, dq_2,
    out_own, out_other, back_near_a, back_near_b, dkv_other, *, scale
):
    first = sides_ref[0] == 1
    every = slice(None)
    back_near_a[...] = (load((first, dq_1, dq_2), every, every) * scale).astype(back_near_a.dtype)
    run_tiles(
        {"other": kv_other},
        {"own": own, "other": other, "near_b": (first, near_2, near_1)},
        [("other", t) for t in ("own", "other", "near_b")],
        {"own": dq_own, "other": dq_other, "near_b": (first, dq_2, dq_1)},
        {},
        {"own": out_own, "other": out_other, "near_b": back_near_b},
        {"other": dkv_other},
        scale,
    )


def mid_tiles(sides, *operands, scale):
    rows, width = operands[5].shape
    part = jax.ShapeDtypeStruct((rows, width), jnp.float32)
    done = jax.ShapeDtypeStruct((rows, width), jnp.bfloat16)
    return pl.pallas_call(
        functools.partial(mid_kernel, scale=scale),
        in_specs=[pl.BlockSpec(memory_space=pltpu.SMEM)] + [WHOLE] * len(operands),
        out_specs=[WHOLE] * 5,
        out_shape=[part, part, done, done, jax.ShapeDtypeStruct((2 * rows, width), jnp.float32)],
        compiler_params=PARAMS,
        name="mid_tiles",
    )(sides, *operands)


def far_kernel(
    sides_ref, relayed_ref, kv, kv_other, far_1, far_2, back_near_a, back_near_b, relayed, dkv_in, dkv_part_in,
    back_near_1, back_near_2, back_far_1, back_far_2, dkv_own, dkv_other, dkv, dkv_part, back_a, back_b, *, scale
):
    first = sides_ref[0] == 1
    every = slice(None)
    back_near_1[...] = load((first, back_near_a, back_near_b), every, every)
    back_near_2[...] = load((first, back_near_b, back_near_a), every, every)
    dkv_other[2 * back_a.shape[0] :] = jnp.zeros((PAD, dkv_other.shape[1]), dkv_other.dtype)

    def relayed_tiles(keys):
        run_tiles(
            {"own": kv, "other": kv_other},
            {"near": relayed},
            [(u, "near") for u in keys],
            {},
            {"own": dkv, "other": dkv_part},
            {"near": back_near_2},
            {"own": dkv, "other": dkv_part},
            scale,
        )

    here = relayed_ref[0] == 1
    pl.when(jnp.logical_and(here, first))(lambda: relayed_tiles(("own", "other")))
    pl.when(jnp.logical_and(here, jnp.logical_not(first)))(lambda: relayed_tiles(("own",)))
    run_tiles(
        {"own": kv, "other": kv_other},
        {"far_a": (first, far_1, far_2), "far_b": (first, far_2, far_1)},
        [("other", "far_b"), ("other", "far_a"), ("own", "far_a")],
        {},
        {"own": dkv, "other": dkv_part},
        {"far_a": back_a, "far_b": back_b},
        {"own": dkv_own, "other": dkv_other},
        scale,
    )
    back_far_1[...] = load((first, back_a, back_b), every, every)
    back_far_2[...] = load((first, back_b, back_a), every, every)


def far_tiles(sides, relayed_here, *operands, scale):
    kv, part, sums = operands[0], operands[4], operands[7]
    part_done = jax.ShapeDtypeStruct(part.shape, jnp.bfloat16)
    done = jax.ShapeDtypeStruct(kv.shape, jnp.bfloat16)
    sent = jax.ShapeDtypeStruct((kv.shape[0] + PAD, kv.shape[1]), jnp.bfloat16)
    results = pl.pallas_call(
        functools.partial(far_kernel, scale=scale),
        in_specs=[pl.BlockSpec(memory_space=pltpu.SMEM)] * 2 + [WHOLE] * len(operands),
        out_specs=[WHOLE] * 8,
        out_shape=[part_done] * 4 + [done, sent] + [jax.ShapeDtypeStruct(sums.shape, sums.dtype)] * 2,
        scratch_shapes=[pltpu.VMEM(part.shape, part.dtype)] * 2,
        input_output_aliases={9: 6, 10: 7},
        compiler_params=PARAMS,
        name="far_tiles",
    )(sides, relayed_here, *operands)
    return results[:6]


def sum_other_kernel(dq, back_a, back_b, out, *, scale):
    total = dq[...] * scale + back_a[...].astype(jnp.float32) + back_b[...].astype(jnp.float32)
    out[...] = total.astype(jnp.bfloat16)


def sum_other(dq, back_a, back_b, scale):
    return pl.pallas_call(
        functools.partial(sum_other_kernel, scale=scale),
        in_specs=[WHOLE] * 3,
        out_specs=WHOLE,
        out_shape=jax.ShapeDtypeStruct(dq.shape, jnp.bfloat16),
        compiler_params=PARAMS,
        name="sum_other",
    )(dq, back_a, back_b)


def finish_kernel(x_ref, dq_own, back_a, back_b, dkv_own, dkv_other, dq, dk, dv, buffer, sems, *, scale):
    rows, half = buffer.shape
    at_own = pl.ds(pl.multiple_of(x_ref[0] * half, LANES), half)
    at_other = pl.ds(pl.multiple_of((1 - x_ref[0]) * half, LANES), half)
    moves = (
        (dkv_own.at[0:rows], dk.at[:, at_own]),
        (dkv_own.at[rows : 2 * rows], dv.at[:, at_own]),
        (dkv_other.at[0:rows], dk.at[:, at_other]),
        (dkv_other.at[rows : 2 * rows], dv.at[:, at_other]),
    )
    copies = [pltpu.make_async_copy(a, b, sems.at[n]) for n, (a, b) in enumerate(moves)]
    for copy in copies:
        copy.start()
    total = (
        dq_own[...] * scale + back_a[...].astype(jnp.float32) + back_b[...].astype(jnp.float32)
    )
    buffer[...] = total.astype(jnp.bfloat16)
    copies.append(pltpu.make_async_copy(buffer, dq.at[:, at_own], sems.at[4]))
    copies[-1].start()
    for copy in copies:
        copy.wait()


def finish(x, dq_own, back_a, back_b, dkv_own, dkv_other, scale):
    rows, half = dq_own.shape
    return pl.pallas_call(
        functools.partial(finish_kernel, scale=scale),
        in_specs=[pl.BlockSpec(memory_space=pltpu.SMEM)] + [WHOLE] * 5,
        out_specs=[IN_HBM] * 3,
        out_shape=[jax.ShapeDtypeStruct((rows, 2 * half), jnp.bfloat16)] * 3,
        scratch_shapes=[pltpu.VMEM((rows, half), jnp.bfloat16), pltpu.SemaphoreType.DMA((5,))],
        compiler_params=PARAMS,
        name="finish",
    )(x, dq_own, back_a, back_b, dkv_own, dkv_other)


def place_kernel(x_ref, part, _, whole, sem):
    half = part.shape[1]
    at_other = pl.ds(pl.multiple_of((1 - x_ref[0]) * half, LANES), half)
    copy = pltpu.make_async_copy(part, whole.at[:, at_other], sem)
    copy.start()
    copy.wait()


def place(x, part, whole):
    return pl.pallas_call(
        place_kernel,
        in_specs=[pl.BlockSpec(memory_space=pltpu.SMEM), WHOLE, IN_HBM],
        out_specs=IN_HBM,
        out_shape=jax.ShapeDtypeStruct(whole.shape, whole.dtype),
        scratch_shapes=[pltpu.SemaphoreType.DMA],
        input_output_aliases={2: 0},
        compiler_params=PARAMS,
        name="place",
    )(x, part, whole)


def per_device(query_rows, key_rows, value_rows, layer_output, output_grad, log_norms):
    count = lax.axis_size("outer") * lax.axis_size("inner")
    index = lax.axis_index("outer") * lax.axis_size("inner") + lax.axis_index("inner")
    column, row = index % 2, index // 2 % 2
    x = column.astype(jnp.int32).reshape(1)
    sides = (column ^ row).astype(jnp.int32).reshape(1)
    head_size = query_rows.shape[1] // log_norms.shape[0]
    scale = head_size ** (-0.5)

    swap = [(i, i ^ 1) for i in range(count)]
    step_1 = [(i, i ^ 2) for i in range(count)]
    step_2 = [(i, ((i + 2) ^ 2) - 2) for i in range(count)]
    step_2 = [(i, j) for i, j in step_2 if 0 <= j < count]
    half = count // 2
    across = [(half - 2 + k, count - 2 + k) for k in range(2)] + [(half + k, k) for k in range(2)]
    onward = [(count - 2 + k, half + k) for k in range(2)] + [(k, half - 2 + k) for k in range(2)]
    step_2_own = [(i, j) for i, j in step_2 if (i < half) == (j < half)]
    relayed_here = ((index >= half - 2) & (index < half + 2)).astype(jnp.int32).reshape(1)

    def send(a, perm):
        return lax.ppermute(a, AXES, perm)

    to_other, kv_to_other = pack(
        x, query_rows, layer_output, output_grad, log_norms, key_rows, value_rows, name="pack_other"
    )
    (own,) = pack(x, query_rows, layer_output, output_grad, log_norms, name="pack_own")
    other = send(to_other, swap)
    near_1, near_2 = send(own, step_1), send(own, step_2_own)
    relayed = send(send(own, across), onward)
    kv_to_other, other = lax.optimization_barrier((kv_to_other, other))
    kv_other = send(kv_to_other, swap)
    far_1, far_2 = send(other, step_1), send(other, step_2)
    dq_own, dq_other, dq_1, dq_2, dkv, kv_own = near_tiles(
        x, key_rows, value_rows, own, other, near_1, near_2, scale=scale
    )
    dq_own, dq_other, back_near_a, back_near_b, dkv_part = mid_tiles(
        sides, kv_other, own, other, near_1, near_2,
        dq_own, dq_other, dq_1, dq_2, scale=scale,
    )
    near_to_1, near_to_2, far_to_1, far_to_2, dkv_own, dkv_to_other = far_tiles(
        sides, relayed_here, kv_own, kv_other, far_1, far_2, back_near_a, back_near_b, relayed,
        dkv, dkv_part, scale=scale,
    )
    dkv_other = send(dkv_to_other, swap)
    far_back_1, far_back_2 = send(far_to_1, step_1), send(far_to_2, step_2)
    back_1, back_2 = send(near_to_1, step_1), send(near_to_2, step_2)
    dq_from_other = send(sum_other(dq_other, far_back_1, far_back_2, scale), swap)
    dq, dk, dv = finish(x, dq_own, back_1, back_2, dkv_own, dkv_other, scale)
    return place(x, dq_from_other, dq), dk, dv


def solution(mesh):
    rows = P(AXES, None)
    return jax.shard_map(
        per_device,
        mesh=mesh,
        in_specs=(rows, rows, rows, rows, rows, P(None, AXES)),
        out_specs=(rows, rows, rows),
        check_vma=False,
    )
```

time: 81.3 us -> 76.1 us (0.936)
  waiting for transfers between devices: 41 us -> 28.4 us
  starting transfers between devices: 19.1 us -> 24.9 us
  Pallas kernels: 19.8 us -> 21.5 us
    ppermute x10 -> x14, waiting for transfers between devices: 41 us -> 28.4 us  [send(): return lax.ppermute(a, AXES, perm)]
    ppermute x10 -> x14, starting transfers between devices: 19.1 us -> 24.9 us  [send(): return lax.ppermute(a, AXES, perm)]
    pallas_call x2 -> x3, Pallas kernels: 8.21 us -> 9.84 us  [the longest x1 6.31 us: near_tiles(): pl.pallas_call(functools.partial(near_kernel, scale=scale), in_specs=[pl....]
  transfers between devices with their start and end apart: 10 -> 14, of which waited for: 5 -> 8; matrix products, arithmetic and copies ran while one was open for 0% -> 0% of each run, Pallas kernels for 13% -> 17%
where the time goes in v4:
time: 76.1 us; the launch traced here: 75.9 us
  waiting for transfers between devices  28.4 us (37%)
  starting transfers between devices  24.9 us (33%)
  Pallas kernels  21.5 us (28%)
  between operations  0.95 us (1%)
    ppermute x14, waiting for transfers between devices, send(): return lax.ppermute(a, AXES, perm)  28.4 us
    ppermute x14, starting transfers between devices, send(): return lax.ppermute(a, AXES, perm)  24.9 us
    pallas_call x1, Pallas kernels, near_tiles(): pl.pallas_call(functools.partial(near_kernel, scale=scale), in_specs=[pl....  6.31 us
    pallas_call x1, Pallas kernels, far_tiles(): pl.pallas_call(functools.partial(far_kernel, scale=scale), in_specs=[pl.B...  5.6 us
    pallas_call x1, Pallas kernels, mid_tiles(): pl.pallas_call(functools.partial(mid_kernel, scale=scale), in_specs=[pl.B...  4.18 us
    pallas_call x2, Pallas kernels, pack(): pl.pallas_call(functools.partial(pack_kernel, other=bool(kv)), in_specs=[...  3.53 us
  transfers between devices with their start and end apart: 14, of which 8 were waited for; matrix products, arithmetic and copies ran while one was open for 0% of the time, Pallas kernels for 17%

profile of v4, /device:TPU:24, one launch (start us, length us, event | category | flops | bytes accessed | tf_op | source)
XLA Modules:
  0.0 75.9 jit_solution(1516035453509540740)
XLA Ops:
  0.6 2.2 %pack_other.1 = (bf16[528,512]{1,0:T(8,128)(2,1)S(1)}, bf16[528,512]{1,0:T(8,128)(2,1)}) custom-call(s32[1]{0:T(128)} %bitcast.x_ref, bf16[256,1024]{1,0:T(8,128)(2,1)} %q.3, bf16[256,1024]{1,0:T(8,128)(2,1)} %o.3, bf16[256,1024]{1,0:T(8,128)(2,1)} %g.3, f32[16,256]{1,0:T(8,128)} %norms.3, bf16[256,1024]{1,0:T(8,128)(2,1)} %k.1, bf16[256,1024]{1,0:T(8,128)(2,1)} %v.1), custom_call_target="tpu_custom_call" | custom-call | tf_op jit(solution)/shard_map/pack_other/pallas_call | solution.py:81
  2.8 3.1 %collective-permute-start = (bf16[528,512]{1,0:T(8,128)(2,1)S(1)}, bf16[528,512]{1,0:T(8,128)(2,1)S(1)}, u32[]{:S(2)}, u32[]{:S(2)}) collective-permute-start(bf16[528,512]{1,0:T(8,128)(2,1)S(1)} %get-tuple-element.28), channel_id=1, source_target_pairs={{0,1},{1,0},{2,3},{3,2},{4,5},{5,4},{6,7},{7,6},{8,9},{9,8},{10,11... | collective-permute-start | bytes 1622024 | tf_op jit(solution)/shard_map/ppermute | solution.py:412
  5.9 1.3 %pack_own.1.own = bf16[528,512]{1,0:T(8,128)(2,1)S(1)} custom-call(s32[1]{0:T(128)} %bitcast.x_ref, bf16[256,1024]{1,0:T(8,128)(2,1)} %q.3, bf16[256,1024]{1,0:T(8,128)(2,1)} %o.3, bf16[256,1024]{1,0:T(8,128)(2,1)} %g.3, f32[16,256]{1,0:T(8,128)} %norms.3), custom_call_target="tpu_custom_call" | custom-call | tf_op jit(solution)/shard_map/pack_own/pallas_call | solution.py:81
  7.3 0.8 %collective-permute-start.2 = (bf16[528,512]{1,0:T(8,128)(2,1)S(1)}, bf16[528,512]{1,0:T(8,128)(2,1)S(1)}, u32[]{:S(2)}, u32[]{:S(2)}) collective-permute-start(bf16[528,512]{1,0:T(8,128)(2,1)S(1)} %pack_own.1.own), channel_id=1, source_target_pairs={{0,2},{1,3},{2,0},{3,1},{4,6},{5,7},{6,4},{7,5},{8,10},{9,11},{10,... | collective-permute-start | bytes 1622024 | tf_op jit(solution)/shard_map/ppermute | solution.py:412
  8.1 1.5 %collective-permute-start.6 = (bf16[528,512]{1,0:T(8,128)(2,1)S(1)}, bf16[528,512]{1,0:T(8,128)(2,1)}, u32[]{:S(2)}, u32[]{:S(2)}) collective-permute-start(bf16[528,512]{1,0:T(8,128)(2,1)S(1)} %pack_own.1.own), channel_id=1, source_target_pairs={{126,254},{127,255},{128,0},{129,1}} | collective-permute-start | bytes 1622024 | tf_op jit(solution)/shard_map/ppermute | solution.py:412
  9.6 1.9 %collective-permute-start.3 = (bf16[528,512]{1,0:T(8,128)(2,1)S(1)}, bf16[528,512]{1,0:T(8,128)(2,1)S(1)}, u32[]{:S(2)}, u32[]{:S(2)}) collective-permute-start(bf16[528,512]{1,0:T(8,128)(2,1)S(1)} %pack_own.1.own), channel_id=1, source_target_pairs={{2,4},{3,5},{4,2},{5,3},{6,8},{7,9},{8,6},{9,7},{10,12},{11,13},{1... | collective-permute-start | bytes 1622024 | tf_op jit(solution)/shard_map/ppermute | solution.py:412
  11.5 6.9 %collective-permute-done.other = bf16[528,512]{1,0:T(8,128)(2,1)S(1)} collective-permute-done((bf16[528,512]{1,0:T(8,128)(2,1)S(1)}, bf16[528,512]{1,0:T(8,128)(2,1)S(1)}, u32[]{:S(2)}, u32[]{:S(2)}) %collective-permute-start) | collective-permute-done | bytes 540704 | tf_op jit(solution)/shard_map/ppermute | solution.py:412
  18.4 3.0 %collective-permute-start.1 = (bf16[528,512]{1,0:T(8,128)(2,1)}, bf16[528,512]{1,0:T(8,128)(2,1)S(1)}, u32[]{:S(2)}, u32[]{:S(2)}) collective-permute-start(bf16[528,512]{1,0:T(8,128)(2,1)} %get-tuple-element.29), channel_id=1, source_target_pairs={{0,1},{1,0},{2,3},{3,2},{4,5},{5,4},{6,7},{7,6},{8,9},{9,8},{10,11... | collective-permute-start | bytes 1622024 | tf_op jit(solution)/shard_map/ppermute | solution.py:412
  21.5 0.7 collective-permute-start.4
  22.2 0.0 collective-permute-done.2.near_1
  22.2 1.9 %collective-permute-start.5 = (bf16[528,512]{1,0:T(8,128)(2,1)S(1)}, bf16[528,512]{1,0:T(8,128)(2,1)}, u32[]{:S(2)}, u32[]{:S(2)}) collective-permute-start(bf16[528,512]{1,0:T(8,128)(2,1)S(1)} %collective-permute-done.other), channel_id=1, source_target_pairs={{2,4},{3,5},{4,2},{5,3},{6,8},{7,9},{8,6},{9,7},{10,12},{11,13},{1... | collective-permute-start | bytes 1622024 | tf_op jit(solution)/shard_map/ppermute | solution.py:412
  24.1 0.0 collective-permute-done.6
  24.1 1.5 %collective-permute-start.7 = (bf16[528,512]{1,0:T(8,128)(2,1)}, bf16[528,512]{1,0:T(8,128)(2,1)}, u32[]{:S(2)}, u32[]{:S(2)}) collective-permute-start(bf16[528,512]{1,0:T(8,128)(2,1)} %collective-permute-done.6), channel_id=1, source_target_pairs={{254,128},{255,129},{0,126},{1,127}} | collective-permute-start | bytes 1622024 | tf_op jit(solution)/shard_map/ppermute | solution.py:412
  25.6 1.6 %collective-permute-done.3.near_2 = bf16[528,512]{1,0:T(8,128)(2,1)S(1)} collective-permute-done((bf16[528,512]{1,0:T(8,128)(2,1)S(1)}, bf16[528,512]{1,0:T(8,128)(2,1)S(1)}, u32[]{:S(2)}, u32[]{:S(2)}) %collective-permute-start.3) | collective-permute-done | bytes 540704 | tf_op jit(solution)/shard_map/ppermute | solution.py:412
  27.3 6.3 %near_tiles.1 = (f32[256,512]{1,0:T(8,128)S(1)}, f32[256,512]{1,0:T(8,128)S(1)}, f32[256,512]{1,0:T(8,128)S(1)}, f32[256,512]{1,0:T(8,128)S(1)}, f32[512,512]{1,0:T(8,128)S(1)}, /*index=5*/bf16[512,512]{1,0:T(8,128)(2,1)S(1)}) custom-call(s32[1]{0:T(128)} %bitcast.x_ref, bf16[256,1024]{1,0:T(8,128)(2,1)} %k.1, bf16[256,1024]{1,0:T(8,128)(2,1)} %v.1, ...), custom_call_target="tpu_custom_call" | custom-call | tf_op jit(solution)/shard_map/near_tiles/pallas_call | solution.py:218
  33.6 5.5 %collective-permute-done.1.kv_other = bf16[528,512]{1,0:T(8,128)(2,1)S(1)} collective-permute-done((bf16[528,512]{1,0:T(8,128)(2,1)}, bf16[528,512]{1,0:T(8,128)(2,1)S(1)}, u32[]{:S(2)}, u32[]{:S(2)}) %collective-permute-start.1) | collective-permute-done | bytes 540704 | tf_op jit(solution)/shard_map/ppermute | solution.py:412
  39.1 4.2 %mid_tiles.1 = (f32[256,512]{1,0:T(8,128)S(1)}, f32[256,512]{1,0:T(8,128)S(1)}, bf16[256,512]{1,0:T(8,128)(2,1)S(1)}, bf16[256,512]{1,0:T(8,128)(2,1)S(1)}, f32[512,512]{1,0:T(8,128)S(1)}) custom-call(s32[1]{0:T(128)} %bitcast.1.sides_ref, bf16[528,512]{1,0:T(8,128)(2,1)S(1)} %collective-permute-done.1.kv_other, bf16[528,512]{1,0:T(8,128)(2,1)S(1)} %pack_own.1.own, ...), custom_call_target="tpu_custom_call" | custom-call | tf_op jit(solution)/shard_map/mid_tiles/pallas_call | solution.py:252
  43.3 0.0 collective-permute-done.4.far_1
  43.3 0.0 collective-permute-done.5.far_2
  43.3 0.0 collective-permute-done.7.relayed
  43.3 5.6 %far_tiles.1 = (bf16[256,512]{1,0:T(8,128)(2,1)S(1)}, bf16[256,512]{1,0:T(8,128)(2,1)S(1)}, bf16[256,512]{1,0:T(8,128)(2,1)S(1)}, bf16[256,512]{1,0:T(8,128)(2,1...) custom-call(s32[1]{0:T(128)} %bitcast.1.sides_ref, ...), custom_call_target="tpu_custom_call", output_to_operand_aliasing={{6}: (9, {}), {7}: (10, {})} | custom-call | tf_op jit(solution)/shard_map/far_tiles/pallas_call | solution.py:306
  48.9 3.1 %collective-permute-start.13 = (bf16[528,512]{1,0:T(8,128)(2,1)S(1)}, bf16[528,512]{1,0:T(8,128)(2,1)S(1)}, u32[]{:S(2)}, u32[]{:S(2)}) collective-permute-start(bf16[528,512]{1,0:T(8,128)(2,1)S(1)} %get-tuple-element.47), channel_id=1, source_target_pairs={{0,1},{1,0},{2,3},{3,2},{4,5},{5,4},{6,7},{7,6},{8,9},{9,8},{10,11... | collective-permute-start | bytes 1622024 | tf_op jit(solution)/shard_map/ppermute | solution.py:412
  52.0 0.0 collective-permute-start.8
  52.0 1.9 %collective-permute-start.9 = (bf16[256,512]{1,0:T(8,128)(2,1)S(1)}, bf16[256,512]{1,0:T(8,128)(2,1)S(1)}, u32[]{:S(2)}, u32[]{:S(2)}) collective-permute-start(bf16[256,512]{1,0:T(8,128)(2,1)S(1)} %get-tuple-element.42), channel_id=1, source_target_pairs={{2,4},{3,5},{4,2},{5,3},{6,8},{7,9},{8,6},{9,7},{10,12},{11,13},{1... | collective-permute-start | bytes 786440 | tf_op jit(solution)/shard_map/ppermute | solution.py:412
  53.9 2.1 %collective-permute-start.11 = (bf16[256,512]{1,0:T(8,128)(2,1)S(1)}, bf16[256,512]{1,0:T(8,128)(2,1)S(1)}, u32[]{:S(2)}, u32[]{:S(2)}) collective-permute-start(bf16[256,512]{1,0:T(8,128)(2,1)S(1)} %get-tuple-element.44), channel_id=1, source_target_pairs={{0,2},{1,3},{2,0},{3,1},{4,6},{5,7},{6,4},{7,5},{8,10},{9,11},{10,... | collective-permute-start | bytes 786440 | tf_op jit(solution)/shard_map/ppermute | solution.py:412
  56.1 2.8 %collective-permute-start.12 = (bf16[256,512]{1,0:T(8,128)(2,1)S(1)}, bf16[256,512]{1,0:T(8,128)(2,1)S(1)}, u32[]{:S(2)}, u32[]{:S(2)}) collective-permute-start(bf16[256,512]{1,0:T(8,128)(2,1)S(1)} %get-tuple-element.45), channel_id=1, source_target_pairs={{2,4},{3,5},{4,2},{5,3},{6,8},{7,9},{8,6},{9,7},{10,12},{11,13},{1... | collective-permute-start | bytes 786440 | tf_op jit(solution)/shard_map/ppermute | solution.py:412
  58.9 2.0 %collective-permute-done.8.back_a = bf16[256,512]{1,0:T(8,128)(2,1)S(1)} collective-permute-done((bf16[256,512]{1,0:T(8,128)(2,1)S(1)}, bf16[256,512]{1,0:T(8,128)(2,1)S(1)}, u32[]{:S(2)}, u32[]{:S(2)}) %collective-permute-start.8) | collective-permute-done | bytes 262176 | tf_op jit(solution)/shard_map/ppermute | solution.py:412
  60.9 4.6 %collective-permute-done.9.back_b = bf16[256,512]{1,0:T(8,128)(2,1)S(1)} collective-permute-done((bf16[256,512]{1,0:T(8,128)(2,1)S(1)}, bf16[256,512]{1,0:T(8,128)(2,1)S(1)}, u32[]{:S(2)}, u32[]{:S(2)}) %collective-permute-start.9) | collective-permute-done | bytes 262176 | tf_op jit(solution)/shard_map/ppermute | solution.py:412
  65.5 0.1 sum_other.1
  65.6 0.5 collective-permute-start.10
  66.1 0.0 collective-permute-done.11.back_a
  66.1 2.2 %collective-permute-done.12.back_b = bf16[256,512]{1,0:T(8,128)(2,1)S(1)} collective-permute-done((bf16[256,512]{1,0:T(8,128)(2,1)S(1)}, bf16[256,512]{1,0:T(8,128)(2,1)S(1)}, u32[]{:S(2)}, u32[]{:S(2)}) %collective-permute-start.12) | collective-permute-done | bytes 262176 | tf_op jit(solution)/shard_map/ppermute | solution.py:412
  68.3 2.0 %collective-permute-done.13.dkv_other = bf16[528,512]{1,0:T(8,128)(2,1)S(1)} collective-permute-done((bf16[528,512]{1,0:T(8,128)(2,1)S(1)}, bf16[528,512]{1,0:T(8,128)(2,1)S(1)}, u32[]{:S(2)}, u32[]{:S(2)}) %collective-permute-start.13) | collective-permute-done | bytes 540704 | tf_op jit(solution)/shard_map/ppermute | solution.py:412
  70.3 1.1 %finish.1 = (bf16[256,1024]{1,0:T(8,128)(2,1)}, bf16[256,1024]{1,0:T(8,128)(2,1)}, bf16[256,1024]{1,0:T(8,128)(2,1)}) custom-call(s32[1]{0:T(128)} %bitcast.x_ref, f32[256,512]{1,0:T(8,128)S(1)} %get-tuple-element.43.dq_own, bf16[256,512]{1,0:T(8,128)(2,1)S(1)} %collective-permute-done.11.back_a, bf16[256,512]{1,0:T(8,128)(2,1)S(1)} %collective-permute-done.12.back_b, ...), custom_call_target="tpu_custom_call" | custom-call | tf_op jit(solution)/shard_map/finish/pallas_call | solution.py:360
  71.4 3.6 %collective-permute-done.10.part = bf16[256,512]{1,0:T(8,128)(2,1)S(1)} collective-permute-done((bf16[256,512]{1,0:T(8,128)(2,1)S(1)}, bf16[256,512]{1,0:T(8,128)(2,1)S(1)}, u32[]{:S(2)}, u32[]{:S(2)}) %collective-permute-start.10) | collective-permute-done | bytes 262176 | tf_op jit(solution)/shard_map/ppermute | solution.py:412
  75.0 0.7 place.1
Async XLA Ops:
  2.8 15.6 %collective-permute-start = (bf16[528,512]{1,0:T(8,128)(2,1)S(1)}, bf16[528,512]{1,0:T(8,128)(2,1)S(1)}, u32[]{:S(2)}, u32[]{:S(2)}) collective-permute-start(bf16[528,512]{1,0:T(8,128)(2,1)S(1)} %get-tuple-element.28), channel_id=1, source_target_pairs={{0,1},{1,0},{2,3},{3,2},{4,5},{5,4},{6,7},{7,6},{8,9},{9,8},{10,11... | collective-permute-start | bytes 1622024 | tf_op jit(solution)/shard_map/ppermute | solution.py:412
  7.3 14.9 %collective-permute-start.2 = (bf16[528,512]{1,0:T(8,128)(2,1)S(1)}, bf16[528,512]{1,0:T(8,128)(2,1)S(1)}, u32[]{:S(2)}, u32[]{:S(2)}) collective-permute-start(bf16[528,512]{1,0:T(8,128)(2,1)S(1)} %pack_own.1.own), channel_id=1, source_target_pairs={{0,2},{1,3},{2,0},{3,1},{4,6},{5,7},{6,4},{7,5},{8,10},{9,11},{10,... | collective-permute-start | bytes 1622024 | tf_op jit(solution)/shard_map/ppermute | solution.py:412
  8.1 16.0 %collective-permute-start.6 = (bf16[528,512]{1,0:T(8,128)(2,1)S(1)}, bf16[528,512]{1,0:T(8,128)(2,1)}, u32[]{:S(2)}, u32[]{:S(2)}) collective-permute-start(bf16[528,512]{1,0:T(8,128)(2,1)S(1)} %pack_own.1.own), channel_id=1, source_target_pairs={{126,254},{127,255},{128,0},{129,1}} | collective-permute-start | bytes 1622024 | tf_op jit(solution)/shard_map/ppermute | solution.py:412
  9.6 17.7 %collective-permute-start.3 = (bf16[528,512]{1,0:T(8,128)(2,1)S(1)}, bf16[528,512]{1,0:T(8,128)(2,1)S(1)}, u32[]{:S(2)}, u32[]{:S(2)}) collective-permute-start(bf16[528,512]{1,0:T(8,128)(2,1)S(1)} %pack_own.1.own), channel_id=1, source_target_pairs={{2,4},{3,5},{4,2},{5,3},{6,8},{7,9},{8,6},{9,7},{10,12},{11,13},{1... | collective-permute-start | bytes 1622024 | tf_op jit(solution)/shard_map/ppermute | solution.py:412
  18.4 20.7 %collective-permute-start.1 = (bf16[528,512]{1,0:T(8,128)(2,1)}, bf16[528,512]{1,0:T(8,128)(2,1)S(1)}, u32[]{:S(2)}, u32[]{:S(2)}) collective-permute-start(bf16[528,512]{1,0:T(8,128)(2,1)} %get-tuple-element.29), channel_id=1, source_target_pairs={{0,1},{1,0},{2,3},{3,2},{4,5},{5,4},{6,7},{7,6},{8,9},{9,8},{10,11... | collective-permute-start | bytes 1622024 | tf_op jit(solution)/shard_map/ppermute | solution.py:412
  21.5 21.8 %collective-permute-start.4 = (bf16[528,512]{1,0:T(8,128)(2,1)S(1)}, bf16[528,512]{1,0:T(8,128)(2,1)S(1)}, u32[]{:S(2)}, u32[]{:S(2)}) collective-permute-start(bf16[528,512]{1,0:T(8,128)(2,1)S(1)} %collective-permute-done.other), channel_id=1, source_target_pairs={{0,2},{1,3},{2,0},{3,1},{4,6},{5,7},{6,4},{7,5},{8,10},{9,11},{10,... | collective-permute-start | bytes 1622024 | tf_op jit(solution)/shard_map/ppermute | solution.py:412
  22.2 21.1 %collective-permute-start.5 = (bf16[528,512]{1,0:T(8,128)(2,1)S(1)}, bf16[528,512]{1,0:T(8,128)(2,1)}, u32[]{:S(2)}, u32[]{:S(2)}) collective-permute-start(bf16[528,512]{1,0:T(8,128)(2,1)S(1)} %collective-permute-done.other), channel_id=1, source_target_pairs={{2,4},{3,5},{4,2},{5,3},{6,8},{7,9},{8,6},{9,7},{10,12},{11,13},{1... | collective-permute-start | bytes 1622024 | tf_op jit(solution)/shard_map/ppermute | solution.py:412
  24.1 19.2 %collective-permute-start.7 = (bf16[528,512]{1,0:T(8,128)(2,1)}, bf16[528,512]{1,0:T(8,128)(2,1)}, u32[]{:S(2)}, u32[]{:S(2)}) collective-permute-start(bf16[528,512]{1,0:T(8,128)(2,1)} %collective-permute-done.6), channel_id=1, source_target_pairs={{254,128},{255,129},{0,126},{1,127}} | collective-permute-start | bytes 1622024 | tf_op jit(solution)/shard_map/ppermute | solution.py:412
  48.9 21.4 %collective-permute-start.13 = (bf16[528,512]{1,0:T(8,128)(2,1)S(1)}, bf16[528,512]{1,0:T(8,128)(2,1)S(1)}, u32[]{:S(2)}, u32[]{:S(2)}) collective-permute-start(bf16[528,512]{1,0:T(8,128)(2,1)S(1)} %get-tuple-element.47), channel_id=1, source_target_pairs={{0,1},{1,0},{2,3},{3,2},{4,5},{5,4},{6,7},{7,6},{8,9},{9,8},{10,11... | collective-permute-start | bytes 1622024 | tf_op jit(solution)/shard_map/ppermute | solution.py:412
  52.0 8.9 %collective-permute-start.8 = (bf16[256,512]{1,0:T(8,128)(2,1)S(1)}, bf16[256,512]{1,0:T(8,128)(2,1)S(1)}, u32[]{:S(2)}, u32[]{:S(2)}) collective-permute-start(bf16[256,512]{1,0:T(8,128)(2,1)S(1)} %get-tuple-element.41), channel_id=1, source_target_pairs={{0,2},{1,3},{2,0},{3,1},{4,6},{5,7},{6,4},{7,5},{8,10},{9,11},{10,... | collective-permute-start | bytes 786440 | tf_op jit(solution)/shard_map/ppermute | solution.py:412
  52.0 13.5 %collective-permute-start.9 = (bf16[256,512]{1,0:T(8,128)(2,1)S(1)}, bf16[256,512]{1,0:T(8,128)(2,1)S(1)}, u32[]{:S(2)}, u32[]{:S(2)}) collective-permute-start(bf16[256,512]{1,0:T(8,128)(2,1)S(1)} %get-tuple-element.42), channel_id=1, source_target_pairs={{2,4},{3,5},{4,2},{5,3},{6,8},{7,9},{8,6},{9,7},{10,12},{11,13},{1... | collective-permute-start | bytes 786440 | tf_op jit(solution)/shard_map/ppermute | solution.py:412
  53.9 12.1 %collective-permute-start.11 = (bf16[256,512]{1,0:T(8,128)(2,1)S(1)}, bf16[256,512]{1,0:T(8,128)(2,1)S(1)}, u32[]{:S(2)}, u32[]{:S(2)}) collective-permute-start(bf16[256,512]{1,0:T(8,128)(2,1)S(1)} %get-tuple-element.44), channel_id=1, source_target_pairs={{0,2},{1,3},{2,0},{3,1},{4,6},{5,7},{6,4},{7,5},{8,10},{9,11},{10,... | collective-permute-start | bytes 786440 | tf_op jit(solution)/shard_map/ppermute | solution.py:412
  56.1 12.2 %collective-permute-start.12 = (bf16[256,512]{1,0:T(8,128)(2,1)S(1)}, bf16[256,512]{1,0:T(8,128)(2,1)S(1)}, u32[]{:S(2)}, u32[]{:S(2)}) collective-permute-start(bf16[256,512]{1,0:T(8,128)(2,1)S(1)} %get-tuple-element.45), channel_id=1, source_target_pairs={{2,4},{3,5},{4,2},{5,3},{6,8},{7,9},{8,6},{9,7},{10,12},{11,13},{1... | collective-permute-start | bytes 786440 | tf_op jit(solution)/shard_map/ppermute | solution.py:412
  65.6 9.4 %collective-permute-start.10 = (bf16[256,512]{1,0:T(8,128)(2,1)S(1)}, bf16[256,512]{1,0:T(8,128)(2,1)S(1)}, u32[]{:S(2)}, u32[]{:S(2)}) collective-permute-start(bf16[256,512]{1,0:T(8,128)(2,1)S(1)} %sum_other.1), channel_id=1, source_target_pairs={{0,1},{1,0},{2,3},{3,2},{4,5},{5,4},{6,7},{7,6},{8,9},{9,8},{10,11... | collective-permute-start | bytes 786440 | tf_op jit(solution)/shard_map/ppermute | solution.py:412

commit v5 on v4

--- a/solution.py
+++ b/solution.py
@@ -32,21 +32,22 @@
 
 def pack_kernel(x_ref, q, o, g, norms, *refs, other):
     if other:
+        msg, outs, norm_buf, sems = refs
+    else:
         k, v, msg, kv, outs, norm_buf, sems = refs
-    else:
-        msg, outs, norm_buf, sems = refs
     rows, width = q.shape
     half = width // 2
     side = 1 - x_ref[0] if other else x_ref[0]
     columns = pl.ds(pl.multiple_of(side * half, LANES), half)
     moves = [(g.at[:, columns], msg.at[rows : 2 * rows]), (o.at[:, columns], outs), (norms, norm_buf)]
     moves.append((q.at[:, columns], msg.at[0:rows]))
-    if other:
-        moves += [(k.at[:, columns], kv.at[0:rows]), (v.at[:, columns], kv.at[rows : 2 * rows])]
+    if not other:
+        away = pl.ds(pl.multiple_of((1 - side) * half, LANES), half)
+        moves += [(k.at[:, away], kv.at[0:rows]), (v.at[:, away], kv.at[rows : 2 * rows])]
     copies = [pltpu.make_async_copy(a, b, sems.at[n]) for n, (a, b) in enumerate(moves)]
     for copy in copies:
         copy.start()
-    if other:
+    if not other:
         kv[2 * rows :] = jnp.zeros((PAD, half), kv.dtype)
     row = lax.broadcasted_iota(jnp.int32, (8, LANES), 0)
     lane = lax.broadcasted_iota(jnp.int32, (8, LANES), 1)
@@ -79,7 +80,7 @@
         shapes.append(jax.ShapeDtypeStruct((2 * rows + PAD, width // 2), jnp.bfloat16))
     operands = [pltpu.with_memory_space_constraint(a, pltpu.HBM) for a in (q, o, g, norms, *kv)]
     return pl.pallas_call(
-        functools.partial(pack_kernel, other=bool(kv)),
+        functools.partial(pack_kernel, other=not kv),
         in_specs=[pl.BlockSpec(memory_space=pltpu.SMEM)] + [IN_HBM] * len(operands),
         out_specs=[WHOLE] * len(shapes),
         out_shape=shapes,
@@ -411,10 +412,10 @@
     def send(a, perm):
         return lax.ppermute(a, AXES, perm)
 
-    to_other, kv_to_other = pack(
-        x, query_rows, layer_output, output_grad, log_norms, key_rows, value_rows, name="pack_other"
-    )
-    (own,) = pack(x, query_rows, layer_output, output_grad, log_norms, name="pack_own")
+    (to_other,) = pack(x, query_rows, layer_output, output_grad, log_norms, name="pack_other")
+    own, kv_to_other = pack(
+        x, query_rows, layer_output, output_grad, log_norms, key_rows, value_rows, name="pack_own"
+    )
     other = send(to_other, swap)
     near_1, near_2 = send(own, step_1), send(own, step_2_own)
     relayed = send(send(own, across), onward)

time: 76.1 us -> 75.3 us (0.989)
  waiting for transfers between devices: 28.4 us -> 27.6 us
    ppermute x14, waiting for transfers between devices: 28.4 us -> 27.6 us  [send(): return lax.ppermute(a, AXES, perm)]
  transfers between devices with their start and end apart: 14 -> 14, of which waited for: 8 -> 8; matrix products, arithmetic and copies ran while one was open for 0% -> 0% of each run, Pallas kernels for 17% -> 18%
where the time goes in v5:
time: 75.3 us; the launch traced here: 75 us
  waiting for transfers between devices  27.6 us (37%)
  starting transfers between devices  24.9 us (33%)
  Pallas kernels  21.5 us (29%)
  between operations  0.95 us (1%)
    ppermute x14, waiting for transfers between devices, send(): return lax.ppermute(a, AXES, perm)  27.6 us
    ppermute x14, starting transfers between devices, send(): return lax.ppermute(a, AXES, perm)  24.9 us
    pallas_call x1, Pallas kernels, near_tiles(): pl.pallas_call(functools.partial(near_kernel, scale=scale), in_specs=[pl....  6.31 us
    pallas_call x1, Pallas kernels, far_tiles(): pl.pallas_call(functools.partial(far_kernel, scale=scale), in_specs=[pl.B...  5.6 us
    pallas_call x1, Pallas kernels, mid_tiles(): pl.pallas_call(functools.partial(mid_kernel, scale=scale), in_specs=[pl.B...  4.18 us
    pallas_call x2, Pallas kernels, pack(): pl.pallas_call(functools.partial(pack_kernel, other=not kv), in_specs=[pl...  3.53 us
  transfers between devices with their start and end apart: 14, of which 8 were waited for; matrix products, arithmetic and copies ran while one was open for 0% of the time, Pallas kernels for 18%

profile of v5, /device:TPU:24, one launch (start us, length us, event | category | flops | bytes accessed | tf_op | source)
XLA Modules:
  0.0 75.0 jit_solution(11927411004372137637)
XLA Ops:
  0.6 1.4 %pack_other.1 = bf16[528,512]{1,0:T(8,128)(2,1)S(1)} custom-call(s32[1]{0:T(128)} %bitcast.x_ref, bf16[256,1024]{1,0:T(8,128)(2,1)} %q.3, bf16[256,1024]{1,0:T(8,128)(2,1)} %o.3, bf16[256,1024]{1,0:T(8,128)(2,1)} %g.3, f32[16,256]{1,0:T(8,128)} %norms.3), custom_call_target="tpu_custom_call" | custom-call | tf_op jit(solution)/shard_map/pack_other/pallas_call | solution.py:82
  2.0 3.1 %collective-permute-start = (bf16[528,512]{1,0:T(8,128)(2,1)S(1)}, bf16[528,512]{1,0:T(8,128)(2,1)S(1)}, u32[]{:S(2)}, u32[]{:S(2)}) collective-permute-start(bf16[528,512]{1,0:T(8,128)(2,1)S(1)} %pack_other.1), channel_id=1, source_target_pairs={{0,1},{1,0},{2,3},{3,2},{4,5},{5,4},{6,7},{7,6},{8,9},{9,8},{10,11... | collective-permute-start | bytes 1622024 | tf_op jit(solution)/shard_map/ppermute | solution.py:413
  5.1 2.2 %pack_own.1 = (bf16[528,512]{1,0:T(8,128)(2,1)S(1)}, bf16[528,512]{1,0:T(8,128)(2,1)}) custom-call(s32[1]{0:T(128)} %bitcast.x_ref, bf16[256,1024]{1,0:T(8,128)(2,1)} %q.3, bf16[256,1024]{1,0:T(8,128)(2,1)} %o.3, bf16[256,1024]{1,0:T(8,128)(2,1)} %g.3, f32[16,256]{1,0:T(8,128)} %norms.3, bf16[256,1024]{1,0:T(8,128)(2,1)} %k.1, bf16[256,1024]{1,0:T(8,128)(2,1)} %v.1), custom_call_target="tpu_custom_call" | custom-call | tf_op jit(solution)/shard_map/pack_own/pallas_call | solution.py:82
  7.3 0.8 %collective-permute-start.2 = (bf16[528,512]{1,0:T(8,128)(2,1)S(1)}, bf16[528,512]{1,0:T(8,128)(2,1)S(1)}, u32[]{:S(2)}, u32[]{:S(2)}) collective-permute-start(bf16[528,512]{1,0:T(8,128)(2,1)S(1)} %get-tuple-element.29.own), channel_id=1, source_target_pairs={{0,2},{1,3},{2,0},{3,1},{4,6},{5,7},{6,4},{7,5},{8,10},{9,11},{10,... | collective-permute-start | bytes 1622024 | tf_op jit(solution)/shard_map/ppermute | solution.py:413
  8.1 1.5 %collective-permute-start.6 = (bf16[528,512]{1,0:T(8,128)(2,1)S(1)}, bf16[528,512]{1,0:T(8,128)(2,1)}, u32[]{:S(2)}, u32[]{:S(2)}) collective-permute-start(bf16[528,512]{1,0:T(8,128)(2,1)S(1)} %get-tuple-element.29.own), channel_id=1, source_target_pairs={{126,254},{127,255},{128,0},{129,1}} | collective-permute-start | bytes 1622024 | tf_op jit(solution)/shard_map/ppermute | solution.py:413
  9.6 1.9 %collective-permute-start.3 = (bf16[528,512]{1,0:T(8,128)(2,1)S(1)}, bf16[528,512]{1,0:T(8,128)(2,1)S(1)}, u32[]{:S(2)}, u32[]{:S(2)}) collective-permute-start(bf16[528,512]{1,0:T(8,128)(2,1)S(1)} %get-tuple-element.29.own), channel_id=1, source_target_pairs={{2,4},{3,5},{4,2},{5,3},{6,8},{7,9},{8,6},{9,7},{10,12},{11,13},{1... | collective-permute-start | bytes 1622024 | tf_op jit(solution)/shard_map/ppermute | solution.py:413
  11.5 6.1 %collective-permute-done.other = bf16[528,512]{1,0:T(8,128)(2,1)S(1)} collective-permute-done((bf16[528,512]{1,0:T(8,128)(2,1)S(1)}, bf16[528,512]{1,0:T(8,128)(2,1)S(1)}, u32[]{:S(2)}, u32[]{:S(2)}) %collective-permute-start) | collective-permute-done | bytes 540704 | tf_op jit(solution)/shard_map/ppermute | solution.py:413
  17.6 3.0 %collective-permute-start.1 = (bf16[528,512]{1,0:T(8,128)(2,1)}, bf16[528,512]{1,0:T(8,128)(2,1)S(1)}, u32[]{:S(2)}, u32[]{:S(2)}) collective-permute-start(bf16[528,512]{1,0:T(8,128)(2,1)} %get-tuple-element.28), channel_id=1, source_target_pairs={{0,1},{1,0},{2,3},{3,2},{4,5},{5,4},{6,7},{7,6},{8,9},{9,8},{10,11... | collective-permute-start | bytes 1622024 | tf_op jit(solution)/shard_map/ppermute | solution.py:413
  20.6 0.7 collective-permute-start.4
  21.4 0.0 collective-permute-done.2.near_1
  21.4 1.9 %collective-permute-start.5 = (bf16[528,512]{1,0:T(8,128)(2,1)S(1)}, bf16[528,512]{1,0:T(8,128)(2,1)}, u32[]{:S(2)}, u32[]{:S(2)}) collective-permute-start(bf16[528,512]{1,0:T(8,128)(2,1)S(1)} %collective-permute-done.other), channel_id=1, source_target_pairs={{2,4},{3,5},{4,2},{5,3},{6,8},{7,9},{8,6},{9,7},{10,12},{11,13},{1... | collective-permute-start | bytes 1622024 | tf_op jit(solution)/shard_map/ppermute | solution.py:413
  23.3 0.0 collective-permute-done.6
  23.3 1.5 %collective-permute-start.7 = (bf16[528,512]{1,0:T(8,128)(2,1)}, bf16[528,512]{1,0:T(8,128)(2,1)}, u32[]{:S(2)}, u32[]{:S(2)}) collective-permute-start(bf16[528,512]{1,0:T(8,128)(2,1)} %collective-permute-done.6), channel_id=1, source_target_pairs={{254,128},{255,129},{0,126},{1,127}} | collective-permute-start | bytes 1622024 | tf_op jit(solution)/shard_map/ppermute | solution.py:413
  24.8 2.5 %collective-permute-done.3.near_2 = bf16[528,512]{1,0:T(8,128)(2,1)S(1)} collective-permute-done((bf16[528,512]{1,0:T(8,128)(2,1)S(1)}, bf16[528,512]{1,0:T(8,128)(2,1)S(1)}, u32[]{:S(2)}, u32[]{:S(2)}) %collective-permute-start.3) | collective-permute-done | bytes 540704 | tf_op jit(solution)/shard_map/ppermute | solution.py:413
  27.3 6.3 %near_tiles.1 = (f32[256,512]{1,0:T(8,128)S(1)}, f32[256,512]{1,0:T(8,128)S(1)}, f32[256,512]{1,0:T(8,128)S(1)}, f32[256,512]{1,0:T(8,128)S(1)}, f32[512,512]{1,0:T(8,128)S(1)}, /*index=5*/bf16[512,512]{1,0:T(8,128)(2,1)S(1)}) custom-call(s32[1]{0:T(128)} %bitcast.x_ref, bf16[256,1024]{1,0:T(8,128)(2,1)} %k.1, bf16[256,1024]{1,0:T(8,128)(2,1)} %v.1, ...), custom_call_target="tpu_custom_call" | custom-call | tf_op jit(solution)/shard_map/near_tiles/pallas_call | solution.py:219
  33.6 4.7 %collective-permute-done.1.kv_other = bf16[528,512]{1,0:T(8,128)(2,1)S(1)} collective-permute-done((bf16[528,512]{1,0:T(8,128)(2,1)}, bf16[528,512]{1,0:T(8,128)(2,1)S(1)}, u32[]{:S(2)}, u32[]{:S(2)}) %collective-permute-start.1) | collective-permute-done | bytes 540704 | tf_op jit(solution)/shard_map/ppermute | solution.py:413
  38.3 4.2 %mid_tiles.1 = (f32[256,512]{1,0:T(8,128)S(1)}, f32[256,512]{1,0:T(8,128)S(1)}, bf16[256,512]{1,0:T(8,128)(2,1)S(1)}, bf16[256,512]{1,0:T(8,128)(2,1)S(1)}, f32[512,512]{1,0:T(8,128)S(1)}) custom-call(s32[1]{0:T(128)} %bitcast.1.sides_ref, bf16[528,512]{1,0:T(8,128)(2,1)S(1)} %collective-permute-done.1.kv_other, bf16[528,512]{1,0:T(8,128)(2,1)S(1)} %get-tuple-element.29.own, ...), custom_call_target="tpu_custom_call" | custom-call | tf_op jit(solution)/shard_map/mid_tiles/pallas_call | solution.py:253
  42.5 0.0 collective-permute-done.4.far_1
  42.5 0.0 collective-permute-done.5.far_2
  42.5 0.0 collective-permute-done.7.relayed
  42.5 5.6 %far_tiles.1 = (bf16[256,512]{1,0:T(8,128)(2,1)S(1)}, bf16[256,512]{1,0:T(8,128)(2,1)S(1)}, bf16[256,512]{1,0:T(8,128)(2,1)S(1)}, bf16[256,512]{1,0:T(8,128)(2,1...) custom-call(s32[1]{0:T(128)} %bitcast.1.sides_ref, ...), custom_call_target="tpu_custom_call", output_to_operand_aliasing={{6}: (9, {}), {7}: (10, {})} | custom-call | tf_op jit(solution)/shard_map/far_tiles/pallas_call | solution.py:307
  48.1 3.1 %collective-permute-start.13 = (bf16[528,512]{1,0:T(8,128)(2,1)S(1)}, bf16[528,512]{1,0:T(8,128)(2,1)S(1)}, u32[]{:S(2)}, u32[]{:S(2)}) collective-permute-start(bf16[528,512]{1,0:T(8,128)(2,1)S(1)} %get-tuple-element.47), channel_id=1, source_target_pairs={{0,1},{1,0},{2,3},{3,2},{4,5},{5,4},{6,7},{7,6},{8,9},{9,8},{10,11... | collective-permute-start | bytes 1622024 | tf_op jit(solution)/shard_map/ppermute | solution.py:413
  51.2 0.0 collective-permute-start.8
  51.2 1.9 %collective-permute-start.9 = (bf16[256,512]{1,0:T(8,128)(2,1)S(1)}, bf16[256,512]{1,0:T(8,128)(2,1)S(1)}, u32[]{:S(2)}, u32[]{:S(2)}) collective-permute-start(bf16[256,512]{1,0:T(8,128)(2,1)S(1)} %get-tuple-element.42), channel_id=1, source_target_pairs={{2,4},{3,5},{4,2},{5,3},{6,8},{7,9},{8,6},{9,7},{10,12},{11,13},{1... | collective-permute-start | bytes 786440 | tf_op jit(solution)/shard_map/ppermute | solution.py:413
  53.1 2.1 %collective-permute-start.11 = (bf16[256,512]{1,0:T(8,128)(2,1)S(1)}, bf16[256,512]{1,0:T(8,128)(2,1)S(1)}, u32[]{:S(2)}, u32[]{:S(2)}) collective-permute-start(bf16[256,512]{1,0:T(8,128)(2,1)S(1)} %get-tuple-element.44), channel_id=1, source_target_pairs={{0,2},{1,3},{2,0},{3,1},{4,6},{5,7},{6,4},{7,5},{8,10},{9,11},{10,... | collective-permute-start | bytes 786440 | tf_op jit(solution)/shard_map/ppermute | solution.py:413
  55.2 2.8 %collective-permute-start.12 = (bf16[256,512]{1,0:T(8,128)(2,1)S(1)}, bf16[256,512]{1,0:T(8,128)(2,1)S(1)}, u32[]{:S(2)}, u32[]{:S(2)}) collective-permute-start(bf16[256,512]{1,0:T(8,128)(2,1)S(1)} %get-tuple-element.45), channel_id=1, source_target_pairs={{2,4},{3,5},{4,2},{5,3},{6,8},{7,9},{8,6},{9,7},{10,12},{11,13},{1... | collective-permute-start | bytes 786440 | tf_op jit(solution)/shard_map/ppermute | solution.py:413
  58.1 2.0 %collective-permute-done.8.back_a = bf16[256,512]{1,0:T(8,128)(2,1)S(1)} collective-permute-done((bf16[256,512]{1,0:T(8,128)(2,1)S(1)}, bf16[256,512]{1,0:T(8,128)(2,1)S(1)}, u32[]{:S(2)}, u32[]{:S(2)}) %collective-permute-start.8) | collective-permute-done | bytes 262176 | tf_op jit(solution)/shard_map/ppermute | solution.py:413
  60.1 4.6 %collective-permute-done.9.back_b = bf16[256,512]{1,0:T(8,128)(2,1)S(1)} collective-permute-done((bf16[256,512]{1,0:T(8,128)(2,1)S(1)}, bf16[256,512]{1,0:T(8,128)(2,1)S(1)}, u32[]{:S(2)}, u32[]{:S(2)}) %collective-permute-start.9) | collective-permute-done | bytes 262176 | tf_op jit(solution)/shard_map/ppermute | solution.py:413
  64.7 0.1 sum_other.1
  64.8 0.5 collective-permute-start.10
  65.3 0.0 collective-permute-done.11.back_a
  65.3 2.2 %collective-permute-done.12.back_b = bf16[256,512]{1,0:T(8,128)(2,1)S(1)} collective-permute-done((bf16[256,512]{1,0:T(8,128)(2,1)S(1)}, bf16[256,512]{1,0:T(8,128)(2,1)S(1)}, u32[]{:S(2)}, u32[]{:S(2)}) %collective-permute-start.12) | collective-permute-done | bytes 262176 | tf_op jit(solution)/shard_map/ppermute | solution.py:413
  67.5 2.0 %collective-permute-done.13.dkv_other = bf16[528,512]{1,0:T(8,128)(2,1)S(1)} collective-permute-done((bf16[528,512]{1,0:T(8,128)(2,1)S(1)}, bf16[528,512]{1,0:T(8,128)(2,1)S(1)}, u32[]{:S(2)}, u32[]{:S(2)}) %collective-permute-start.13) | collective-permute-done | bytes 540704 | tf_op jit(solution)/shard_map/ppermute | solution.py:413
  69.5 1.1 %finish.1 = (bf16[256,1024]{1,0:T(8,128)(2,1)}, bf16[256,1024]{1,0:T(8,128)(2,1)}, bf16[256,1024]{1,0:T(8,128)(2,1)}) custom-call(s32[1]{0:T(128)} %bitcast.x_ref, f32[256,512]{1,0:T(8,128)S(1)} %get-tuple-element.43.dq_own, bf16[256,512]{1,0:T(8,128)(2,1)S(1)} %collective-permute-done.11.back_a, bf16[256,512]{1,0:T(8,128)(2,1)S(1)} %collective-permute-done.12.back_b, ...), custom_call_target="tpu_custom_call" | custom-call | tf_op jit(solution)/shard_map/finish/pallas_call | solution.py:361
  70.6 3.6 %collective-permute-done.10.part = bf16[256,512]{1,0:T(8,128)(2,1)S(1)} collective-permute-done((bf16[256,512]{1,0:T(8,128)(2,1)S(1)}, bf16[256,512]{1,0:T(8,128)(2,1)S(1)}, u32[]{:S(2)}, u32[]{:S(2)}) %collective-permute-start.10) | collective-permute-done | bytes 262176 | tf_op jit(solution)/shard_map/ppermute | solution.py:413
  74.1 0.7 place.1
Async XLA Ops:
  2.0 15.6 %collective-permute-start = (bf16[528,512]{1,0:T(8,128)(2,1)S(1)}, bf16[528,512]{1,0:T(8,128)(2,1)S(1)}, u32[]{:S(2)}, u32[]{:S(2)}) collective-permute-start(bf16[528,512]{1,0:T(8,128)(2,1)S(1)} %pack_other.1), channel_id=1, source_target_pairs={{0,1},{1,0},{2,3},{3,2},{4,5},{5,4},{6,7},{7,6},{8,9},{9,8},{10,11... | collective-permute-start | bytes 1622024 | tf_op jit(solution)/shard_map/ppermute | solution.py:413
  7.3 14.1 %collective-permute-start.2 = (bf16[528,512]{1,0:T(8,128)(2,1)S(1)}, bf16[528,512]{1,0:T(8,128)(2,1)S(1)}, u32[]{:S(2)}, u32[]{:S(2)}) collective-permute-start(bf16[528,512]{1,0:T(8,128)(2,1)S(1)} %get-tuple-element.29.own), channel_id=1, source_target_pairs={{0,2},{1,3},{2,0},{3,1},{4,6},{5,7},{6,4},{7,5},{8,10},{9,11},{10,... | collective-permute-start | bytes 1622024 | tf_op jit(solution)/shard_map/ppermute | solution.py:413
  8.1 15.2 %collective-permute-start.6 = (bf16[528,512]{1,0:T(8,128)(2,1)S(1)}, bf16[528,512]{1,0:T(8,128)(2,1)}, u32[]{:S(2)}, u32[]{:S(2)}) collective-permute-start(bf16[528,512]{1,0:T(8,128)(2,1)S(1)} %get-tuple-element.29.own), channel_id=1, source_target_pairs={{126,254},{127,255},{128,0},{129,1}} | collective-permute-start | bytes 1622024 | tf_op jit(solution)/shard_map/ppermute | solution.py:413
  9.6 17.7 %collective-permute-start.3 = (bf16[528,512]{1,0:T(8,128)(2,1)S(1)}, bf16[528,512]{1,0:T(8,128)(2,1)S(1)}, u32[]{:S(2)}, u32[]{:S(2)}) collective-permute-start(bf16[528,512]{1,0:T(8,128)(2,1)S(1)} %get-tuple-element.29.own), channel_id=1, source_target_pairs={{2,4},{3,5},{4,2},{5,3},{6,8},{7,9},{8,6},{9,7},{10,12},{11,13},{1... | collective-permute-start | bytes 1622024 | tf_op jit(solution)/shard_map/ppermute | solution.py:413
  17.6 20.7 %collective-permute-start.1 = (bf16[528,512]{1,0:T(8,128)(2,1)}, bf16[528,512]{1,0:T(8,128)(2,1)S(1)}, u32[]{:S(2)}, u32[]{:S(2)}) collective-permute-start(bf16[528,512]{1,0:T(8,128)(2,1)} %get-tuple-element.28), channel_id=1, source_target_pairs={{0,1},{1,0},{2,3},{3,2},{4,5},{5,4},{6,7},{7,6},{8,9},{9,8},{10,11... | collective-permute-start | bytes 1622024 | tf_op jit(solution)/shard_map/ppermute | solution.py:413
  20.6 21.8 %collective-permute-start.4 = (bf16[528,512]{1,0:T(8,128)(2,1)S(1)}, bf16[528,512]{1,0:T(8,128)(2,1)S(1)}, u32[]{:S(2)}, u32[]{:S(2)}) collective-permute-start(bf16[528,512]{1,0:T(8,128)(2,1)S(1)} %collective-permute-done.other), channel_id=1, source_target_pairs={{0,2},{1,3},{2,0},{3,1},{4,6},{5,7},{6,4},{7,5},{8,10},{9,11},{10,... | collective-permute-start | bytes 1622024 | tf_op jit(solution)/shard_map/ppermute | solution.py:413
  21.4 21.1 %collective-permute-start.5 = (bf16[528,512]{1,0:T(8,128)(2,1)S(1)}, bf16[528,512]{1,0:T(8,128)(2,1)}, u32[]{:S(2)}, u32[]{:S(2)}) collective-permute-start(bf16[528,512]{1,0:T(8,128)(2,1)S(1)} %collective-permute-done.other), channel_id=1, source_target_pairs={{2,4},{3,5},{4,2},{5,3},{6,8},{7,9},{8,6},{9,7},{10,12},{11,13},{1... | collective-permute-start | bytes 1622024 | tf_op jit(solution)/shard_map/ppermute | solution.py:413
  23.3 19.2 %collective-permute-start.7 = (bf16[528,512]{1,0:T(8,128)(2,1)}, bf16[528,512]{1,0:T(8,128)(2,1)}, u32[]{:S(2)}, u32[]{:S(2)}) collective-permute-start(bf16[528,512]{1,0:T(8,128)(2,1)} %collective-permute-done.6), channel_id=1, source_target_pairs={{254,128},{255,129},{0,126},{1,127}} | collective-permute-start | bytes 1622024 | tf_op jit(solution)/shard_map/ppermute | solution.py:413
  48.1 21.4 %collective-permute-start.13 = (bf16[528,512]{1,0:T(8,128)(2,1)S(1)}, bf16[528,512]{1,0:T(8,128)(2,1)S(1)}, u32[]{:S(2)}, u32[]{:S(2)}) collective-permute-start(bf16[528,512]{1,0:T(8,128)(2,1)S(1)} %get-tuple-element.47), channel_id=1, source_target_pairs={{0,1},{1,0},{2,3},{3,2},{4,5},{5,4},{6,7},{7,6},{8,9},{9,8},{10,11... | collective-permute-start | bytes 1622024 | tf_op jit(solution)/shard_map/ppermute | solution.py:413
  51.2 8.9 %collective-permute-start.8 = (bf16[256,512]{1,0:T(8,128)(2,1)S(1)}, bf16[256,512]{1,0:T(8,128)(2,1)S(1)}, u32[]{:S(2)}, u32[]{:S(2)}) collective-permute-start(bf16[256,512]{1,0:T(8,128)(2,1)S(1)} %get-tuple-element.41), channel_id=1, source_target_pairs={{0,2},{1,3},{2,0},{3,1},{4,6},{5,7},{6,4},{7,5},{8,10},{9,11},{10,... | collective-permute-start | bytes 786440 | tf_op jit(solution)/shard_map/ppermute | solution.py:413
  51.2 13.5 %collective-permute-start.9 = (bf16[256,512]{1,0:T(8,128)(2,1)S(1)}, bf16[256,512]{1,0:T(8,128)(2,1)S(1)}, u32[]{:S(2)}, u32[]{:S(2)}) collective-permute-start(bf16[256,512]{1,0:T(8,128)(2,1)S(1)} %get-tuple-element.42), channel_id=1, source_target_pairs={{2,4},{3,5},{4,2},{5,3},{6,8},{7,9},{8,6},{9,7},{10,12},{11,13},{1... | collective-permute-start | bytes 786440 | tf_op jit(solution)/shard_map/ppermute | solution.py:413
  53.1 12.1 %collective-permute-start.11 = (bf16[256,512]{1,0:T(8,128)(2,1)S(1)}, bf16[256,512]{1,0:T(8,128)(2,1)S(1)}, u32[]{:S(2)}, u32[]{:S(2)}) collective-permute-start(bf16[256,512]{1,0:T(8,128)(2,1)S(1)} %get-tuple-element.44), channel_id=1, source_target_pairs={{0,2},{1,3},{2,0},{3,1},{4,6},{5,7},{6,4},{7,5},{8,10},{9,11},{10,... | collective-permute-start | bytes 786440 | tf_op jit(solution)/shard_map/ppermute | solution.py:413
  55.2 12.2 %collective-permute-start.12 = (bf16[256,512]{1,0:T(8,128)(2,1)S(1)}, bf16[256,512]{1,0:T(8,128)(2,1)S(1)}, u32[]{:S(2)}, u32[]{:S(2)}) collective-permute-start(bf16[256,512]{1,0:T(8,128)(2,1)S(1)} %get-tuple-element.45), channel_id=1, source_target_pairs={{2,4},{3,5},{4,2},{5,3},{6,8},{7,9},{8,6},{9,7},{10,12},{11,13},{1... | collective-permute-start | bytes 786440 | tf_op jit(solution)/shard_map/ppermute | solution.py:413
  64.8 9.4 %collective-permute-start.10 = (bf16[256,512]{1,0:T(8,128)(2,1)S(1)}, bf16[256,512]{1,0:T(8,128)(2,1)S(1)}, u32[]{:S(2)}, u32[]{:S(2)}) collective-permute-start(bf16[256,512]{1,0:T(8,128)(2,1)S(1)} %sum_other.1), channel_id=1, source_target_pairs={{0,1},{1,0},{2,3},{3,2},{4,5},{5,4},{6,7},{7,6},{8,9},{9,8},{10,11... | collective-permute-start | bytes 786440 | tf_op jit(solution)/shard_map/ppermute | solution.py:413

commit v6 on v5

--- a/solution.py
+++ b/solution.py
@@ -101,7 +101,7 @@
     return jnp.where(flag, first[rows, columns], second[rows, columns])
 
 
-def run_tiles(kv_refs, msg_refs, pairs, dq_in, dkv_in, dq_out, dkv_out, scale):
+def run_tiles(kv_refs, msg_refs, pairs, dq_in, dkv_in, dq_out, dkv_out, scale, arrive=None):
     rows, width = next(iter(dq_out.values())).shape
     half = LANES // 2
     masks = head_masks(jnp.bfloat16)
@@ -112,6 +112,8 @@
 
     def keys_of(u, group):
         if (u, group) not in key_side:
+            if arrive is not None:
+                arrive(group)
             k, v = kv_refs[u][0:rows, span(group)], kv_refs[u][rows : 2 * rows, span(group)]
             kt = k.T
             sums = [None, None]
@@ -192,13 +194,19 @@
     dq_own, dq_other, dq_1, dq_2, dkv, kv, sems, *, scale
 ):
     rows, half = dq_own.shape
-    columns = pl.ds(pl.multiple_of(x_ref[0] * half, LANES), half)
-    moves = ((k, kv.at[0:rows]), (v, kv.at[rows : 2 * rows]))
-    copies = [pltpu.make_async_copy(a.at[:, columns], b, sems.at[n]) for n, (a, b) in enumerate(moves)]
-    for copy in copies:
+    copies = []
+    for group in range(half // LANES):
+        columns = pl.ds(pl.multiple_of(x_ref[0] * half + group * LANES, LANES), LANES)
+        span = slice(group * LANES, (group + 1) * LANES)
+        moves = ((k, kv.at[0:rows, span]), (v, kv.at[rows : 2 * rows, span]))
+        copies.append([pltpu.make_async_copy(a.at[:, columns], b, sems.at[group, n]) for n, (a, b) in enumerate(moves)])
+    for copy in sum(copies, []):
         copy.start()
-    for copy in copies:
-        copy.wait()
+
+    def arrive(group):
+        for copy in copies[group]:
+            copy.wait()
+
     run_tiles(
         {"own": kv},
         {"own": own, "other": other, "1": near_1, "2": near_2},
@@ -208,6 +216,7 @@
         {"own": dq_own, "other": dq_other, "1": dq_1, "2": dq_2},
         {"own": dkv},
         scale,
+        arrive,
     )
 
 
@@ -221,7 +230,7 @@
         in_specs=[pl.BlockSpec(memory_space=pltpu.SMEM)] + [IN_HBM] * 2 + [WHOLE] * len(msgs),
         out_specs=[WHOLE] * 6,
         out_shape=[part] * 4 + [sums, kv],
-        scratch_shapes=[pltpu.SemaphoreType.DMA((2,))],
+        scratch_shapes=[pltpu.SemaphoreType.DMA((width // LANES, 2))],
         compiler_params=PARAMS,
         name="near_tiles",
     )(x, *(pltpu.with_memory_space_constraint(a, pltpu.HBM) for a in (k, v)), *msgs)

time: 75.3 us -> 75.3 us (level)
  transfers between devices with their start and end apart: 14 -> 14, of which waited for: 8 -> 8; matrix products, arithmetic and copies ran while one was open for 0% -> 0% of each run, Pallas kernels for 18% -> 19%
where the time goes in v6:
time: 75.3 us; the launch traced here: 75 us
  waiting for transfers between devices  27 us (36%)
  starting transfers between devices  24.9 us (33%)
  Pallas kernels  22.1 us (29%)
  between operations  0.95 us (1%)
    ppermute x14, waiting for transfers between devices, send(): return lax.ppermute(a, AXES, perm)  27 us
    ppermute x14, starting transfers between devices, send(): return lax.ppermute(a, AXES, perm)  24.9 us
    pallas_call x1, Pallas kernels, near_tiles(): pl.pallas_call(functools.partial(near_kernel, scale=scale), in_specs=[pl....  6.89 us
    pallas_call x1, Pallas kernels, far_tiles(): pl.pallas_call(functools.partial(far_kernel, scale=scale), in_specs=[pl.B...  5.6 us
    pallas_call x1, Pallas kernels, mid_tiles(): pl.pallas_call(functools.partial(mid_kernel, scale=scale), in_specs=[pl.B...  4.18 us
    pallas_call x2, Pallas kernels, pack(): pl.pallas_call(functools.partial(pack_kernel, other=not kv), in_specs=[pl...  3.53 us
  transfers between devices with their start and end apart: 14, of which 8 were waited for; matrix products, arithmetic and copies ran while one was open for 0% of the time, Pallas kernels for 19%

profile of v6, /device:TPU:24, one launch (start us, length us, event | category | flops | bytes accessed | tf_op | source)
XLA Modules:
  0.0 75.0 jit_solution(15772355943307046115)
XLA Ops:
  0.6 1.4 %pack_other.1 = bf16[528,512]{1,0:T(8,128)(2,1)S(1)} custom-call(s32[1]{0:T(128)} %bitcast.x_ref, bf16[256,1024]{1,0:T(8,128)(2,1)} %q.3, bf16[256,1024]{1,0:T(8,128)(2,1)} %o.3, bf16[256,1024]{1,0:T(8,128)(2,1)} %g.3, f32[16,256]{1,0:T(8,128)} %norms.3), custom_call_target="tpu_custom_call" | custom-call | tf_op jit(solution)/shard_map/pack_other/pallas_call | solution.py:82
  2.0 3.1 %collective-permute-start = (bf16[528,512]{1,0:T(8,128)(2,1)S(1)}, bf16[528,512]{1,0:T(8,128)(2,1)S(1)}, u32[]{:S(2)}, u32[]{:S(2)}) collective-permute-start(bf16[528,512]{1,0:T(8,128)(2,1)S(1)} %pack_other.1), channel_id=1, source_target_pairs={{0,1},{1,0},{2,3},{3,2},{4,5},{5,4},{6,7},{7,6},{8,9},{9,8},{10,11... | collective-permute-start | bytes 1622024 | tf_op jit(solution)/shard_map/ppermute | solution.py:422
  5.1 2.2 %pack_own.1 = (bf16[528,512]{1,0:T(8,128)(2,1)S(1)}, bf16[528,512]{1,0:T(8,128)(2,1)}) custom-call(s32[1]{0:T(128)} %bitcast.x_ref, bf16[256,1024]{1,0:T(8,128)(2,1)} %q.3, bf16[256,1024]{1,0:T(8,128)(2,1)} %o.3, bf16[256,1024]{1,0:T(8,128)(2,1)} %g.3, f32[16,256]{1,0:T(8,128)} %norms.3, bf16[256,1024]{1,0:T(8,128)(2,1)} %k.1, bf16[256,1024]{1,0:T(8,128)(2,1)} %v.1), custom_call_target="tpu_custom_call" | custom-call | tf_op jit(solution)/shard_map/pack_own/pallas_call | solution.py:82
  7.3 0.8 %collective-permute-start.2 = (bf16[528,512]{1,0:T(8,128)(2,1)S(1)}, bf16[528,512]{1,0:T(8,128)(2,1)S(1)}, u32[]{:S(2)}, u32[]{:S(2)}) collective-permute-start(bf16[528,512]{1,0:T(8,128)(2,1)S(1)} %get-tuple-element.29.own), channel_id=1, source_target_pairs={{0,2},{1,3},{2,0},{3,1},{4,6},{5,7},{6,4},{7,5},{8,10},{9,11},{10,... | collective-permute-start | bytes 1622024 | tf_op jit(solution)/shard_map/ppermute | solution.py:422
  8.1 1.5 %collective-permute-start.6 = (bf16[528,512]{1,0:T(8,128)(2,1)S(1)}, bf16[528,512]{1,0:T(8,128)(2,1)}, u32[]{:S(2)}, u32[]{:S(2)}) collective-permute-start(bf16[528,512]{1,0:T(8,128)(2,1)S(1)} %get-tuple-element.29.own), channel_id=1, source_target_pairs={{126,254},{127,255},{128,0},{129,1}} | collective-permute-start | bytes 1622024 | tf_op jit(solution)/shard_map/ppermute | solution.py:422
  9.6 1.9 %collective-permute-start.3 = (bf16[528,512]{1,0:T(8,128)(2,1)S(1)}, bf16[528,512]{1,0:T(8,128)(2,1)S(1)}, u32[]{:S(2)}, u32[]{:S(2)}) collective-permute-start(bf16[528,512]{1,0:T(8,128)(2,1)S(1)} %get-tuple-element.29.own), channel_id=1, source_target_pairs={{2,4},{3,5},{4,2},{5,3},{6,8},{7,9},{8,6},{9,7},{10,12},{11,13},{1... | collective-permute-start | bytes 1622024 | tf_op jit(solution)/shard_map/ppermute | solution.py:422
  11.5 6.1 %collective-permute-done.other = bf16[528,512]{1,0:T(8,128)(2,1)S(1)} collective-permute-done((bf16[528,512]{1,0:T(8,128)(2,1)S(1)}, bf16[528,512]{1,0:T(8,128)(2,1)S(1)}, u32[]{:S(2)}, u32[]{:S(2)}) %collective-permute-start) | collective-permute-done | bytes 540704 | tf_op jit(solution)/shard_map/ppermute | solution.py:422
  17.6 3.0 %collective-permute-start.1 = (bf16[528,512]{1,0:T(8,128)(2,1)}, bf16[528,512]{1,0:T(8,128)(2,1)S(1)}, u32[]{:S(2)}, u32[]{:S(2)}) collective-permute-start(bf16[528,512]{1,0:T(8,128)(2,1)} %get-tuple-element.28), channel_id=1, source_target_pairs={{0,1},{1,0},{2,3},{3,2},{4,5},{5,4},{6,7},{7,6},{8,9},{9,8},{10,11... | collective-permute-start | bytes 1622024 | tf_op jit(solution)/shard_map/ppermute | solution.py:422
  20.6 0.7 collective-permute-start.4
  21.4 0.0 collective-permute-done.2.near_1
  21.4 1.9 %collective-permute-start.5 = (bf16[528,512]{1,0:T(8,128)(2,1)S(1)}, bf16[528,512]{1,0:T(8,128)(2,1)}, u32[]{:S(2)}, u32[]{:S(2)}) collective-permute-start(bf16[528,512]{1,0:T(8,128)(2,1)S(1)} %collective-permute-done.other), channel_id=1, source_target_pairs={{2,4},{3,5},{4,2},{5,3},{6,8},{7,9},{8,6},{9,7},{10,12},{11,13},{1... | collective-permute-start | bytes 1622024 | tf_op jit(solution)/shard_map/ppermute | solution.py:422
  23.3 0.0 collective-permute-done.6
  23.3 1.5 %collective-permute-start.7 = (bf16[528,512]{1,0:T(8,128)(2,1)}, bf16[528,512]{1,0:T(8,128)(2,1)}, u32[]{:S(2)}, u32[]{:S(2)}) collective-permute-start(bf16[528,512]{1,0:T(8,128)(2,1)} %collective-permute-done.6), channel_id=1, source_target_pairs={{254,128},{255,129},{0,126},{1,127}} | collective-permute-start | bytes 1622024 | tf_op jit(solution)/shard_map/ppermute | solution.py:422
  24.8 2.5 %collective-permute-done.3.near_2 = bf16[528,512]{1,0:T(8,128)(2,1)S(1)} collective-permute-done((bf16[528,512]{1,0:T(8,128)(2,1)S(1)}, bf16[528,512]{1,0:T(8,128)(2,1)S(1)}, u32[]{:S(2)}, u32[]{:S(2)}) %collective-permute-start.3) | collective-permute-done | bytes 540704 | tf_op jit(solution)/shard_map/ppermute | solution.py:422
  27.3 6.9 %near_tiles.1 = (f32[256,512]{1,0:T(8,128)S(1)}, f32[256,512]{1,0:T(8,128)S(1)}, f32[256,512]{1,0:T(8,128)S(1)}, f32[256,512]{1,0:T(8,128)S(1)}, f32[512,512]{1,0:T(8,128)S(1)}, /*index=5*/bf16[512,512]{1,0:T(8,128)(2,1)S(1)}) custom-call(s32[1]{0:T(128)} %bitcast.x_ref, bf16[256,1024]{1,0:T(8,128)(2,1)} %k.1, bf16[256,1024]{1,0:T(8,128)(2,1)} %v.1, ...), custom_call_target="tpu_custom_call" | custom-call | tf_op jit(solution)/shard_map/near_tiles/pallas_call | solution.py:228
  34.2 4.1 %collective-permute-done.1.kv_other = bf16[528,512]{1,0:T(8,128)(2,1)S(1)} collective-permute-done((bf16[528,512]{1,0:T(8,128)(2,1)}, bf16[528,512]{1,0:T(8,128)(2,1)S(1)}, u32[]{:S(2)}, u32[]{:S(2)}) %collective-permute-start.1) | collective-permute-done | bytes 540704 | tf_op jit(solution)/shard_map/ppermute | solution.py:422
  38.3 4.2 %mid_tiles.1 = (f32[256,512]{1,0:T(8,128)S(1)}, f32[256,512]{1,0:T(8,128)S(1)}, bf16[256,512]{1,0:T(8,128)(2,1)S(1)}, bf16[256,512]{1,0:T(8,128)(2,1)S(1)}, f32[512,512]{1,0:T(8,128)S(1)}) custom-call(s32[1]{0:T(128)} %bitcast.1.sides_ref, bf16[528,512]{1,0:T(8,128)(2,1)S(1)} %collective-permute-done.1.kv_other, bf16[528,512]{1,0:T(8,128)(2,1)S(1)} %get-tuple-element.29.own, ...), custom_call_target="tpu_custom_call" | custom-call | tf_op jit(solution)/shard_map/mid_tiles/pallas_call | solution.py:262
  42.5 0.0 collective-permute-done.4.far_1
  42.5 0.0 collective-permute-done.5.far_2
  42.5 0.0 collective-permute-done.7.relayed
  42.5 5.6 %far_tiles.1 = (bf16[256,512]{1,0:T(8,128)(2,1)S(1)}, bf16[256,512]{1,0:T(8,128)(2,1)S(1)}, bf16[256,512]{1,0:T(8,128)(2,1)S(1)}, bf16[256,512]{1,0:T(8,128)(2,1...) custom-call(s32[1]{0:T(128)} %bitcast.1.sides_ref, ...), custom_call_target="tpu_custom_call", output_to_operand_aliasing={{6}: (9, {}), {7}: (10, {})} | custom-call | tf_op jit(solution)/shard_map/far_tiles/pallas_call | solution.py:316
  48.1 3.1 %collective-permute-start.13 = (bf16[528,512]{1,0:T(8,128)(2,1)S(1)}, bf16[528,512]{1,0:T(8,128)(2,1)S(1)}, u32[]{:S(2)}, u32[]{:S(2)}) collective-permute-start(bf16[528,512]{1,0:T(8,128)(2,1)S(1)} %get-tuple-element.47), channel_id=1, source_target_pairs={{0,1},{1,0},{2,3},{3,2},{4,5},{5,4},{6,7},{7,6},{8,9},{9,8},{10,11... | collective-permute-start | bytes 1622024 | tf_op jit(solution)/shard_map/ppermute | solution.py:422
  51.2 0.0 collective-permute-start.8
  51.2 1.9 %collective-permute-start.9 = (bf16[256,512]{1,0:T(8,128)(2,1)S(1)}, bf16[256,512]{1,0:T(8,128)(2,1)S(1)}, u32[]{:S(2)}, u32[]{:S(2)}) collective-permute-start(bf16[256,512]{1,0:T(8,128)(2,1)S(1)} %get-tuple-element.42), channel_id=1, source_target_pairs={{2,4},{3,5},{4,2},{5,3},{6,8},{7,9},{8,6},{9,7},{10,12},{11,13},{1... | collective-permute-start | bytes 786440 | tf_op jit(solution)/shard_map/ppermute | solution.py:422
  53.1 2.1 %collective-permute-start.11 = (bf16[256,512]{1,0:T(8,128)(2,1)S(1)}, bf16[256,512]{1,0:T(8,128)(2,1)S(1)}, u32[]{:S(2)}, u32[]{:S(2)}) collective-permute-start(bf16[256,512]{1,0:T(8,128)(2,1)S(1)} %get-tuple-element.44), channel_id=1, source_target_pairs={{0,2},{1,3},{2,0},{3,1},{4,6},{5,7},{6,4},{7,5},{8,10},{9,11},{10,... | collective-permute-start | bytes 786440 | tf_op jit(solution)/shard_map/ppermute | solution.py:422
  55.2 2.8 %collective-permute-start.12 = (bf16[256,512]{1,0:T(8,128)(2,1)S(1)}, bf16[256,512]{1,0:T(8,128)(2,1)S(1)}, u32[]{:S(2)}, u32[]{:S(2)}) collective-permute-start(bf16[256,512]{1,0:T(8,128)(2,1)S(1)} %get-tuple-element.45), channel_id=1, source_target_pairs={{2,4},{3,5},{4,2},{5,3},{6,8},{7,9},{8,6},{9,7},{10,12},{11,13},{1... | collective-permute-start | bytes 786440 | tf_op jit(solution)/shard_map/ppermute | solution.py:422
  58.1 2.0 %collective-permute-done.8.back_a = bf16[256,512]{1,0:T(8,128)(2,1)S(1)} collective-permute-done((bf16[256,512]{1,0:T(8,128)(2,1)S(1)}, bf16[256,512]{1,0:T(8,128)(2,1)S(1)}, u32[]{:S(2)}, u32[]{:S(2)}) %collective-permute-start.8) | collective-permute-done | bytes 262176 | tf_op jit(solution)/shard_map/ppermute | solution.py:422
  60.1 4.6 %collective-permute-done.9.back_b = bf16[256,512]{1,0:T(8,128)(2,1)S(1)} collective-permute-done((bf16[256,512]{1,0:T(8,128)(2,1)S(1)}, bf16[256,512]{1,0:T(8,128)(2,1)S(1)}, u32[]{:S(2)}, u32[]{:S(2)}) %collective-permute-start.9) | collective-permute-done | bytes 262176 | tf_op jit(solution)/shard_map/ppermute | solution.py:422
  64.7 0.1 sum_other.1
  64.8 0.5 collective-permute-start.10
  65.3 0.0 collective-permute-done.11.back_a
  65.3 2.2 %collective-permute-done.12.back_b = bf16[256,512]{1,0:T(8,128)(2,1)S(1)} collective-permute-done((bf16[256,512]{1,0:T(8,128)(2,1)S(1)}, bf16[256,512]{1,0:T(8,128)(2,1)S(1)}, u32[]{:S(2)}, u32[]{:S(2)}) %collective-permute-start.12) | collective-permute-done | bytes 262176 | tf_op jit(solution)/shard_map/ppermute | solution.py:422
  67.5 2.0 %collective-permute-done.13.dkv_other = bf16[528,512]{1,0:T(8,128)(2,1)S(1)} collective-permute-done((bf16[528,512]{1,0:T(8,128)(2,1)S(1)}, bf16[528,512]{1,0:T(8,128)(2,1)S(1)}, u32[]{:S(2)}, u32[]{:S(2)}) %collective-permute-start.13) | collective-permute-done | bytes 540704 | tf_op jit(solution)/shard_map/ppermute | solution.py:422
  69.5 1.1 %finish.1 = (bf16[256,1024]{1,0:T(8,128)(2,1)}, bf16[256,1024]{1,0:T(8,128)(2,1)}, bf16[256,1024]{1,0:T(8,128)(2,1)}) custom-call(s32[1]{0:T(128)} %bitcast.x_ref, f32[256,512]{1,0:T(8,128)S(1)} %get-tuple-element.43.dq_own, bf16[256,512]{1,0:T(8,128)(2,1)S(1)} %collective-permute-done.11.back_a, bf16[256,512]{1,0:T(8,128)(2,1)S(1)} %collective-permute-done.12.back_b, ...), custom_call_target="tpu_custom_call" | custom-call | tf_op jit(solution)/shard_map/finish/pallas_call | solution.py:370
  70.6 3.6 %collective-permute-done.10.part = bf16[256,512]{1,0:T(8,128)(2,1)S(1)} collective-permute-done((bf16[256,512]{1,0:T(8,128)(2,1)S(1)}, bf16[256,512]{1,0:T(8,128)(2,1)S(1)}, u32[]{:S(2)}, u32[]{:S(2)}) %collective-permute-start.10) | collective-permute-done | bytes 262176 | tf_op jit(solution)/shard_map/ppermute | solution.py:422
  74.1 0.7 place.1
Async XLA Ops:
  2.0 15.6 %collective-permute-start = (bf16[528,512]{1,0:T(8,128)(2,1)S(1)}, bf16[528,512]{1,0:T(8,128)(2,1)S(1)}, u32[]{:S(2)}, u32[]{:S(2)}) collective-permute-start(bf16[528,512]{1,0:T(8,128)(2,1)S(1)} %pack_other.1), channel_id=1, source_target_pairs={{0,1},{1,0},{2,3},{3,2},{4,5},{5,4},{6,7},{7,6},{8,9},{9,8},{10,11... | collective-permute-start | bytes 1622024 | tf_op jit(solution)/shard_map/ppermute | solution.py:422
  7.3 14.1 %collective-permute-start.2 = (bf16[528,512]{1,0:T(8,128)(2,1)S(1)}, bf16[528,512]{1,0:T(8,128)(2,1)S(1)}, u32[]{:S(2)}, u32[]{:S(2)}) collective-permute-start(bf16[528,512]{1,0:T(8,128)(2,1)S(1)} %get-tuple-element.29.own), channel_id=1, source_target_pairs={{0,2},{1,3},{2,0},{3,1},{4,6},{5,7},{6,4},{7,5},{8,10},{9,11},{10,... | collective-permute-start | bytes 1622024 | tf_op jit(solution)/shard_map/ppermute | solution.py:422
  8.1 15.2 %collective-permute-start.6 = (bf16[528,512]{1,0:T(8,128)(2,1)S(1)}, bf16[528,512]{1,0:T(8,128)(2,1)}, u32[]{:S(2)}, u32[]{:S(2)}) collective-permute-start(bf16[528,512]{1,0:T(8,128)(2,1)S(1)} %get-tuple-element.29.own), channel_id=1, source_target_pairs={{126,254},{127,255},{128,0},{129,1}} | collective-permute-start | bytes 1622024 | tf_op jit(solution)/shard_map/ppermute | solution.py:422
  9.6 17.7 %collective-permute-start.3 = (bf16[528,512]{1,0:T(8,128)(2,1)S(1)}, bf16[528,512]{1,0:T(8,128)(2,1)S(1)}, u32[]{:S(2)}, u32[]{:S(2)}) collective-permute-start(bf16[528,512]{1,0:T(8,128)(2,1)S(1)} %get-tuple-element.29.own), channel_id=1, source_target_pairs={{2,4},{3,5},{4,2},{5,3},{6,8},{7,9},{8,6},{9,7},{10,12},{11,13},{1... | collective-permute-start | bytes 1622024 | tf_op jit(solution)/shard_map/ppermute | solution.py:422
  17.6 20.7 %collective-permute-start.1 = (bf16[528,512]{1,0:T(8,128)(2,1)}, bf16[528,512]{1,0:T(8,128)(2,1)S(1)}, u32[]{:S(2)}, u32[]{:S(2)}) collective-permute-start(bf16[528,512]{1,0:T(8,128)(2,1)} %get-tuple-element.28), channel_id=1, source_target_pairs={{0,1},{1,0},{2,3},{3,2},{4,5},{5,4},{6,7},{7,6},{8,9},{9,8},{10,11... | collective-permute-start | bytes 1622024 | tf_op jit(solution)/shard_map/ppermute | solution.py:422
  20.6 21.8 %collective-permute-start.4 = (bf16[528,512]{1,0:T(8,128)(2,1)S(1)}, bf16[528,512]{1,0:T(8,128)(2,1)S(1)}, u32[]{:S(2)}, u32[]{:S(2)}) collective-permute-start(bf16[528,512]{1,0:T(8,128)(2,1)S(1)} %collective-permute-done.other), channel_id=1, source_target_pairs={{0,2},{1,3},{2,0},{3,1},{4,6},{5,7},{6,4},{7,5},{8,10},{9,11},{10,... | collective-permute-start | bytes 1622024 | tf_op jit(solution)/shard_map/ppermute | solution.py:422
  21.4 21.1 %collective-permute-start.5 = (bf16[528,512]{1,0:T(8,128)(2,1)S(1)}, bf16[528,512]{1,0:T(8,128)(2,1)}, u32[]{:S(2)}, u32[]{:S(2)}) collective-permute-start(bf16[528,512]{1,0:T(8,128)(2,1)S(1)} %collective-permute-done.other), channel_id=1, source_target_pairs={{2,4},{3,5},{4,2},{5,3},{6,8},{7,9},{8,6},{9,7},{10,12},{11,13},{1... | collective-permute-start | bytes 1622024 | tf_op jit(solution)/shard_map/ppermute | solution.py:422
  23.3 19.2 %collective-permute-start.7 = (bf16[528,512]{1,0:T(8,128)(2,1)}, bf16[528,512]{1,0:T(8,128)(2,1)}, u32[]{:S(2)}, u32[]{:S(2)}) collective-permute-start(bf16[528,512]{1,0:T(8,128)(2,1)} %collective-permute-done.6), channel_id=1, source_target_pairs={{254,128},{255,129},{0,126},{1,127}} | collective-permute-start | bytes 1622024 | tf_op jit(solution)/shard_map/ppermute | solution.py:422
  48.1 21.4 %collective-permute-start.13 = (bf16[528,512]{1,0:T(8,128)(2,1)S(1)}, bf16[528,512]{1,0:T(8,128)(2,1)S(1)}, u32[]{:S(2)}, u32[]{:S(2)}) collective-permute-start(bf16[528,512]{1,0:T(8,128)(2,1)S(1)} %get-tuple-element.47), channel_id=1, source_target_pairs={{0,1},{1,0},{2,3},{3,2},{4,5},{5,4},{6,7},{7,6},{8,9},{9,8},{10,11... | collective-permute-start | bytes 1622024 | tf_op jit(solution)/shard_map/ppermute | solution.py:422
  51.2 8.9 %collective-permute-start.8 = (bf16[256,512]{1,0:T(8,128)(2,1)S(1)}, bf16[256,512]{1,0:T(8,128)(2,1)S(1)}, u32[]{:S(2)}, u32[]{:S(2)}) collective-permute-start(bf16[256,512]{1,0:T(8,128)(2,1)S(1)} %get-tuple-element.41), channel_id=1, source_target_pairs={{0,2},{1,3},{2,0},{3,1},{4,6},{5,7},{6,4},{7,5},{8,10},{9,11},{10,... | collective-permute-start | bytes 786440 | tf_op jit(solution)/shard_map/ppermute | solution.py:422
  51.2 13.5 %collective-permute-start.9 = (bf16[256,512]{1,0:T(8,128)(2,1)S(1)}, bf16[256,512]{1,0:T(8,128)(2,1)S(1)}, u32[]{:S(2)}, u32[]{:S(2)}) collective-permute-start(bf16[256,512]{1,0:T(8,128)(2,1)S(1)} %get-tuple-element.42), channel_id=1, source_target_pairs={{2,4},{3,5},{4,2},{5,3},{6,8},{7,9},{8,6},{9,7},{10,12},{11,13},{1... | collective-permute-start | bytes 786440 | tf_op jit(solution)/shard_map/ppermute | solution.py:422
  53.1 12.1 %collective-permute-start.11 = (bf16[256,512]{1,0:T(8,128)(2,1)S(1)}, bf16[256,512]{1,0:T(8,128)(2,1)S(1)}, u32[]{:S(2)}, u32[]{:S(2)}) collective-permute-start(bf16[256,512]{1,0:T(8,128)(2,1)S(1)} %get-tuple-element.44), channel_id=1, source_target_pairs={{0,2},{1,3},{2,0},{3,1},{4,6},{5,7},{6,4},{7,5},{8,10},{9,11},{10,... | collective-permute-start | bytes 786440 | tf_op jit(solution)/shard_map/ppermute | solution.py:422
  55.2 12.2 %collective-permute-start.12 = (bf16[256,512]{1,0:T(8,128)(2,1)S(1)}, bf16[256,512]{1,0:T(8,128)(2,1)S(1)}, u32[]{:S(2)}, u32[]{:S(2)}) collective-permute-start(bf16[256,512]{1,0:T(8,128)(2,1)S(1)} %get-tuple-element.45), channel_id=1, source_target_pairs={{2,4},{3,5},{4,2},{5,3},{6,8},{7,9},{8,6},{9,7},{10,12},{11,13},{1... | collective-permute-start | bytes 786440 | tf_op jit(solution)/shard_map/ppermute | solution.py:422
  64.8 9.4 %collective-permute-start.10 = (bf16[256,512]{1,0:T(8,128)(2,1)S(1)}, bf16[256,512]{1,0:T(8,128)(2,1)S(1)}, u32[]{:S(2)}, u32[]{:S(2)}) collective-permute-start(bf16[256,512]{1,0:T(8,128)(2,1)S(1)} %sum_other.1), channel_id=1, source_target_pairs={{0,1},{1,0},{2,3},{3,2},{4,5},{5,4},{6,7},{7,6},{8,9},{9,8},{10,11... | collective-permute-start | bytes 786440 | tf_op jit(solution)/shard_map/ppermute | solution.py:422
